TPU v7x, 32 devices: a whole 2x2x4 slice. The times are simulated.
32 devices in a mesh: dp: 2 (over core), fsdp: 16 (over z, y, x).
Axes of the slice: x: 2, y: 2, z: 4, core: 2. Of those that a mesh axis runs over, the one named last changes fastest.
Arguments:
- patches: bfloat16 [128, 576, 768], P(('dp', 'fsdp')), may hold values from -6 to 6
- resolution: int32 [128], P(('dp', 'fsdp')), may hold values 0 or 1
- labels: int32 [128], P(('dp', 'fsdp')), may hold values from 0 to 999
- dense_weights: float32 [384, 3840], P(None, ('dp', 'fsdp')), may hold values from -0.20412415 to 0.20412415
- attention: float32 [3, 384, 1536], P(None, None, ('dp', 'fsdp')), may hold values from -1.1547005 to 1.1547005
- router: float32 [2, 384, 128], P(None, 'dp', 'fsdp'), may hold values from -0.21875 to 0.21875
- expert_in: float32 [2, 128, 384, 1536], P(None, 'fsdp', None, 'dp'), may hold values from -4 to 4
- expert_out: float32 [2, 128, 1536, 384], P(None, 'fsdp', 'dp'), may hold values from -0.21875 to 0.21875
- classifier: float32 [385, 1000], replicated, may hold values from -0.3125 to 0.3125
- norm_table: float32 [210, 384], replicated, may hold values from -2 to 2
- dense_weights_first: float32 [384, 3840], P(None, ('dp', 'fsdp')), may hold values from -3.7252903e-08 to 3.7252903e-08
- dense_weights_second: float32 [384, 3840], P(None, ('dp', 'fsdp')), may hold values from 1.7200905e-16 to 6.8672815e-16
- attention_first: float32 [3, 384, 1536], P(None, None, ('dp', 'fsdp')), may hold values from -2.3841858e-07 to 2.3841858e-07
- attention_second: float32 [3, 384, 1536], P(None, None, ('dp', 'fsdp')), may hold values from 8.600452e-15 to 3.433641e-14
- router_first: float32 [2, 384, 128], P(None, 'dp', 'fsdp'), may hold values from -3.7252903e-08 to 3.7252903e-08
- router_second: float32 [2, 384, 128], P(None, 'dp', 'fsdp'), may hold values from 1.7200905e-16 to 6.8672815e-16
- expert_in_first: float32 [2, 128, 384, 1536], P(None, 'fsdp', None, 'dp'), may hold values from -1.6298145e-09 to 1.6298145e-09
- expert_in_second: float32 [2, 128, 384, 1536], P(None, 'fsdp', None, 'dp'), may hold values from 1.1870587e-18 to 4.741694e-18
- expert_out_first: float32 [2, 128, 1536, 384], P(None, 'fsdp', 'dp'), may hold values from -3.7252903e-08 to 3.7252903e-08
- expert_out_second: float32 [2, 128, 1536, 384], P(None, 'fsdp', 'dp'), may hold values from 1.7200905e-16 to 6.8672815e-16
- classifier_first: float32 [385, 1000], replicated, may hold values from -3.7252903e-08 to 3.7252903e-08
- classifier_second: float32 [385, 1000], replicated, may hold values from 1.7200905e-16 to 6.8672815e-16
- norm_table_first: float32 [210, 384], replicated, may hold values from -3.7252903e-08 to 3.7252903e-08
- norm_table_second: float32 [210, 384], replicated, may hold values from 1.7200905e-16 to 6.8672815e-16
Outputs:
- loss: float32 [], replicated
- grad_norm: float32 [], replicated
- new_dense_weights: float32 [384, 3840], P(None, ('dp', 'fsdp'))
- new_dense_weights_first: float32 [384, 3840], P(None, ('dp', 'fsdp'))
- new_dense_weights_second: float32 [384, 3840], P(None, ('dp', 'fsdp'))
- new_attention: float32 [3, 384, 1536], P(None, None, ('dp', 'fsdp'))
- new_attention_first: float32 [3, 384, 1536], P(None, None, ('dp', 'fsdp'))
- new_attention_second: float32 [3, 384, 1536], P(None, None, ('dp', 'fsdp'))
- new_router: float32 [2, 384, 128], P(None, 'dp', 'fsdp')
- new_router_first: float32 [2, 384, 128], P(None, 'dp', 'fsdp')
- new_router_second: float32 [2, 384, 128], P(None, 'dp', 'fsdp')
- new_expert_in: float32 [2, 128, 384, 1536], P(None, 'fsdp', None, 'dp')
- new_expert_in_first: float32 [2, 128, 384, 1536], P(None, 'fsdp', None, 'dp')
- new_expert_in_second: float32 [2, 128, 384, 1536], P(None, 'fsdp', None, 'dp')
- new_expert_out: float32 [2, 128, 1536, 384], P(None, 'fsdp', 'dp')
- new_expert_out_first: float32 [2, 128, 1536, 384], P(None, 'fsdp', 'dp')
- new_expert_out_second: float32 [2, 128, 1536, 384], P(None, 'fsdp', 'dp')
- new_classifier: float32 [385, 1000], replicated
- new_classifier_first: float32 [385, 1000], replicated
- new_classifier_second: float32 [385, 1000], replicated
- new_norm_table: float32 [210, 384], replicated
- new_norm_table_first: float32 [210, 384], replicated
- new_norm_table_second: float32 [210, 384], replicated
All inputs are finite; a program needn't handle non-finite values. No bound on the sum of `resolution` on one device may be relied on, other than what follows from the above.
Results may differ from a plain program's by a relative error of at most 0.022.
Values may be sent and summed in bfloat16 or wider, within the bound.
A program may use at most 512 MiB of HBM per device.

v0:
```python
import jax
import jax.numpy as jnp
from jax import lax
from jax.sharding import PartitionSpec as P

HEADS = 6
FF = 1536
G_LO = 14
G_HI = 24
LEN = 576
LEN_LO = 196
STEP = 10


LN_EPS = 1e-06
CLIP_NORM = 0.001
LEARN_RATE = 0.05
ATTENTION_RATE = 0.15
EXPERT_RATE = 1.0
TABLE_RATE = 0.5
BETA_ONE = 0.9
BETA_TWO = 0.95
ADAM_EPS = 1e-10
WEIGHT_DECAY = 0.1
SMOOTH = 0.1
NEG_FILL = -1e30
PRECISE = lax.Precision.HIGHEST


def layer_norm(values, gain, bias):
    center = values - jnp.mean(values, -1, keepdims=True)
    spread = jnp.mean(center * center, -1, keepdims=True)
    return center * lax.rsqrt(spread + LN_EPS) * gain + bias


def norm_back(values, gain, bias, grad):
    _, pull = jax.vjp(layer_norm, values, gain, bias)
    return pull(grad)


def interp_matrix():
    rows = jnp.arange(G_HI, dtype=jnp.float32)[:, None]
    cols = jnp.arange(G_LO, dtype=jnp.float32)[None, :]
    weight = jnp.maximum(0.0, 1.0 - jnp.abs(rows * (G_LO - 1) - cols * (G_HI - 1)) / (G_HI - 1))
    return (weight[:, None, :, None] * weight[None, :, None, :]).reshape(G_HI * G_HI, G_LO * G_LO)


def matmul(left, right, form):
    return jnp.einsum(form, left, right, preferred_element_type=jnp.float32)


def fetch_dense(attention_layer, router_layer, width):
    rows_dp = lax.axis_size("dp")
    cols_fsdp = lax.axis_size("fsdp")
    dense, router_flat = (
        lax.all_gather(attention_layer.astype(jnp.bfloat16), ("dp", "fsdp"), axis=1, tiled=True),
        lax.all_gather(
            router_layer.astype(jnp.bfloat16).reshape(-1), ("dp", "fsdp"), axis=0, tiled=True
        ),
    )
    part_rows, part_cols = router_layer.shape
    router_b = (
        router_flat.reshape(rows_dp, cols_fsdp, part_rows, part_cols)
        .transpose(0, 2, 1, 3)
        .reshape(rows_dp * part_rows, cols_fsdp * part_cols)
    )
    return (dense[:, : 3 * width], dense[:, 3 * width :], router_b)


def router_to_flat(grad_router):
    rows_dp = lax.axis_size("dp")
    cols_fsdp = lax.axis_size("fsdp")
    full_rows, full_cols = grad_router.shape
    return (
        grad_router.reshape(rows_dp, full_rows // rows_dp, cols_fsdp, full_cols // cols_fsdp)
        .transpose(0, 2, 1, 3)
        .reshape(-1)
    )


def to_experts(values):
    return lax.all_to_all(values, "fsdp", split_axis=1, concat_axis=0, tiled=True)


def from_experts(values):
    return lax.all_to_all(values, "fsdp", split_axis=0, concat_axis=1, tiled=True)


def sum_rows(partial_value):
    return lax.psum_scatter(partial_value, "dp", scatter_dimension=0, tiled=True)


def attend(x_img, valid_img, wqkv, gains):
    width = x_img.shape[-1]
    head_size = width // HEADS
    factor = head_size ** (-0.5)
    normed_b = layer_norm(x_img, gains[0], gains[1]).astype(jnp.bfloat16)
    mixed = matmul(normed_b, wqkv, "rd,dc->rc").astype(jnp.bfloat16)
    query, keys, values = [
        part.reshape(-1, HEADS, head_size) for part in jnp.split(mixed, 3, axis=1)
    ]
    scores = matmul(query, keys, "qhd,khd->hqk") * factor
    scores = jnp.where(valid_img[None, None, :] > 0, scores, NEG_FILL)
    probs = jax.nn.softmax(scores, axis=-1)
    probs_b = probs.astype(jnp.bfloat16)
    context = matmul(probs_b, values, "hqk,khd->qhd").reshape(-1, width).astype(jnp.bfloat16)
    return (normed_b, query, keys, values, probs, probs_b, context)


def attend_back(x_img, valid_img, grad_img, wqkv, wout, gains):
    width = x_img.shape[-1]
    head_size = width // HEADS
    factor = head_size ** (-0.5)
    normed_b, query, keys, values, probs, probs_b, context = attend(x_img, valid_img, wqkv, gains)
    grad_b = grad_img.astype(jnp.bfloat16)
    grad_wout = matmul(grad_b, context, "qe,qd->ed")
    grad_context = (
        matmul(grad_b, wout, "qe,ed->qd").astype(jnp.bfloat16).reshape(-1, HEADS, head_size)
    )
    grad_probs = matmul(grad_context, values, "qhd,khd->hqk")
    grad_values = matmul(probs_b, grad_context, "hqk,qhd->khd")
    grad_scores = (probs * (grad_probs - jnp.sum(grad_probs * probs, -1, keepdims=True))).astype(
        jnp.bfloat16
    )
    grad_query = matmul(grad_scores, keys, "hqk,khd->qhd") * factor
    grad_keys = matmul(grad_scores, query, "hqk,qhd->khd") * factor
    grad_mixed = jnp.concatenate(
        [
            grad_query.reshape(-1, width),
            grad_keys.reshape(-1, width),
            grad_values.reshape(-1, width),
        ],
        1,
    ).astype(jnp.bfloat16)
    grad_wqkv = matmul(normed_b, grad_mixed, "rd,rc->dc")
    grad_normed = matmul(grad_mixed, wqkv, "rc,dc->rd")
    grad_x, grad_gain, grad_bias = norm_back(x_img, gains[0], gains[1], grad_normed)
    return (grad_img + grad_x, grad_wqkv, grad_wout, grad_gain, grad_bias)


def attention_forward(hidden, valid, wqkv, wout, gains):

    def forward_image(item):
        context = attend(item[0], item[1], wqkv, gains)[-1]
        return matmul(context, wout, "qd,ed->qe")

    return hidden + lax.map(forward_image, (hidden, valid))


def attention_backward(before, valid, grad_middle, wqkv, wout, gains):
    width = before.shape[-1]

    def back_image(carry, item):
        grad_x, grad_wqkv, grad_wout_one, grad_gain, grad_bias = attend_back(
            item[0], item[1], item[2], wqkv, wout, gains
        )
        return (
            (
                carry[0] + grad_wqkv,
                carry[1] + grad_wout_one,
                carry[2] + grad_gain,
                carry[3] + grad_bias,
            ),
            grad_x,
        )

    start = (
        jnp.zeros((width, 3 * width), jnp.float32),
        jnp.zeros((width, width), jnp.float32),
        jnp.zeros((width,), jnp.float32),
        jnp.zeros((width,), jnp.float32),
    )
    sums, grad_hidden = lax.scan(back_image, start, (before, valid, grad_middle))
    return (grad_hidden, jnp.concatenate([sums[0], sums[1]], 1), sums[2], sums[3])


def mlp_forward(middle, w_in, w_out, gains):
    normed_b = layer_norm(middle, gains[2], gains[3]).astype(jnp.bfloat16)
    hid = jax.nn.gelu(matmul(normed_b, w_in, "ird,df->irf")).astype(jnp.bfloat16)
    return middle + matmul(hid, w_out, "irf,ef->ire")


def mlp_backward(middle, grad_hidden, w_in, w_out, gains):
    normed_b = layer_norm(middle, gains[2], gains[3]).astype(jnp.bfloat16)
    pre = matmul(normed_b, w_in, "ird,df->irf")
    hid = jax.nn.gelu(pre).astype(jnp.bfloat16)
    grad_b = grad_hidden.astype(jnp.bfloat16)
    grad_w_out = matmul(grad_b, hid, "ire,irf->ef")
    grad_hid = matmul(grad_b, w_out, "ire,ef->irf")
    _, pull = jax.vjp(jax.nn.gelu, pre)
    grad_pre = pull(grad_hid)[0].astype(jnp.bfloat16)
    grad_w_in = matmul(normed_b, grad_pre, "ird,irf->df")
    grad_normed = matmul(grad_pre, w_in, "irf,df->ird")
    grad_x, grad_gain, grad_bias = norm_back(middle, gains[2], gains[3], grad_normed)
    return (grad_hidden + grad_x, grad_w_in, grad_w_out, grad_gain, grad_bias)


def route(middle, valid, router_b, gains):
    normed_b = layer_norm(middle, gains[2], gains[3]).astype(jnp.bfloat16)
    logits = matmul(normed_b, router_b, "ird,de->ire")
    dispatch = jax.nn.softmax(jnp.where(valid[..., None] > 0, logits, NEG_FILL), axis=1)
    combine = jax.nn.softmax(logits, axis=2)
    return (normed_b, dispatch, combine)


def expert_forward(received, win, wout):
    pre = matmul(received, win, "ned,edf->nef")
    hidden = jax.nn.gelu(pre).astype(jnp.bfloat16)
    return matmul(hidden, wout, "nef,efd->ned")


def expert_backward(received, grad_out, win, wout):
    pre = matmul(received, win, "ned,edf->nef")
    hidden = jax.nn.gelu(pre).astype(jnp.bfloat16)
    grad_hidden = matmul(grad_out, wout, "ned,efd->nef")
    _, pull = jax.vjp(jax.nn.gelu, pre)
    grad_pre = pull(grad_hidden)[0].astype(jnp.bfloat16)
    grad_wout = matmul(hidden, grad_out, "nef,ned->efd")
    grad_win = matmul(received, grad_pre, "ned,nef->edf")
    grad_slots = matmul(grad_pre, win, "nef,edf->ned")
    return (grad_slots, grad_win, grad_wout)


def adam(weight, first, second, grad, rate):
    first = BETA_ONE * first + (1.0 - BETA_ONE) * grad
    second = BETA_TWO * second + (1.0 - BETA_TWO) * grad * grad
    ratio = first / (1.0 - BETA_ONE**STEP) / (jnp.sqrt(second / (1.0 - BETA_TWO**STEP)) + ADAM_EPS)
    return (weight - rate * (ratio + WEIGHT_DECAY * weight), first, second)


def on_device(
    patches,
    resolution,
    labels,
    dense_weights,
    attention,
    router,
    expert_in,
    expert_out,
    classifier,
    norm_table,
    dense_weights_first,
    dense_weights_second,
    attention_first,
    attention_second,
    router_first,
    router_second,
    expert_in_first,
    expert_in_second,
    expert_out_first,
    expert_out_second,
    classifier_first,
    classifier_second,
    norm_table_first,
    norm_table_second,
):
    layers = attention.shape[0]
    width = norm_table.shape[1]
    classes = classifier.shape[1]
    pixels = patches.shape[2]
    images = patches.shape[0] * lax.axis_size("dp") * lax.axis_size("fsdp")
    lengths = jnp.where(resolution == 1, LEN, LEN_LO)
    valid = (jnp.arange(LEN)[None, :] < lengths[:, None]).astype(jnp.float32)
    interp = interp_matrix()
    position = norm_table[:LEN_LO]
    pos_high = jnp.dot(interp, position, precision=PRECISE)
    pos_low = jnp.pad(position, ((0, LEN - LEN_LO), (0, 0)))
    high_mask = (resolution == 1)[:, None, None]
    pos_image = jnp.where(high_mask, pos_high[None], pos_low[None])
    first_all, attn_first = (
        lax.all_gather(dense_weights.astype(jnp.bfloat16), ("dp", "fsdp"), axis=1, tiled=True),
        lax.all_gather(attention[0].astype(jnp.bfloat16), ("dp", "fsdp"), axis=1, tiled=True),
    )
    embed_t = first_all[:, :pixels]
    mlp_in = first_all[:, pixels : pixels + FF]
    mlp_out = first_all[:, pixels + FF :]
    wqkv_first = attn_first[:, : 3 * width]
    wout_first = attn_first[:, 3 * width :]
    first_input = (matmul(patches, embed_t, "irp,dp->ird") + pos_image) * valid[..., None]
    gains = norm_table[LEN_LO : LEN_LO + 4]
    first_middle = attention_forward(first_input, valid, wqkv_first, wout_first, gains)
    hidden = mlp_forward(first_middle, mlp_in, mlp_out, gains)
    kept = [None] * layers
    for layer in range(1, layers):
        gains = norm_table[LEN_LO + 4 * layer : LEN_LO + 4 * layer + 4]
        wqkv, wout, router_b = fetch_dense(attention[layer], router[layer - 1], width)
        middle = attention_forward(hidden, valid, wqkv, wout, gains)
        normed_b, dispatch, combine = route(middle, valid, router_b, gains)
        slots = matmul(dispatch.astype(jnp.bfloat16), normed_b, "ire,ird->ied").astype(jnp.bfloat16)
        received = to_experts(slots)
        rows_all = lax.all_gather(received, "dp", axis=0, tiled=True)
        produced = sum_rows(
            expert_forward(
                rows_all,
                expert_in[layer - 1].astype(jnp.bfloat16),
                expert_out[layer - 1].astype(jnp.bfloat16),
            )
        ).astype(jnp.bfloat16)
        returned = from_experts(produced)
        kept[layer] = (hidden, middle, received, returned)
        hidden = middle + matmul(combine.astype(jnp.bfloat16), returned, "ire,ied->ird")
    final_gain = norm_table[LEN_LO + 4 * layers]
    final_bias = norm_table[LEN_LO + 4 * layers + 1]

    def pool(last, gain, bias):
        normed = layer_norm(last, gain, bias)
        return jnp.sum(normed * valid[..., None], 1) / jnp.sum(valid, 1)[:, None]

    pooled, pull_pool = jax.vjp(pool, hidden, final_gain, final_bias)
    pooled_b = pooled.astype(jnp.bfloat16)
    head_b = classifier[:width].astype(jnp.bfloat16)
    logits = matmul(pooled_b, head_b, "id,dc->ic") + classifier[width]
    log_probs = jax.nn.log_softmax(logits, axis=-1)
    onehot = (labels[:, None] == jnp.arange(classes)[None, :]).astype(jnp.float32)
    target = (1.0 - SMOOTH) * onehot + SMOOTH / classes
    loss_part = -jnp.sum(target * log_probs) / images
    grad_logits = (jnp.exp(log_probs) - target) / images
    grad_logits_b = grad_logits.astype(jnp.bfloat16)
    grad_head = jnp.concatenate(
        [matmul(pooled_b, grad_logits_b, "id,ic->dc"), jnp.sum(grad_logits, 0)[None]], 0
    )
    grad_pooled = matmul(grad_logits_b, head_b, "ic,dc->id")
    grad_hidden, grad_final_gain, grad_final_bias = pull_pool(grad_pooled)
    dense_grads = [None] * layers
    router_grads = [None] * (layers - 1)
    win_grads = [None] * (layers - 1)
    wout_grads = [None] * (layers - 1)
    gain_grads = [None] * layers
    for layer in reversed(range(1, layers)):
        before, middle, received, returned = kept[layer]
        gains = norm_table[LEN_LO + 4 * layer : LEN_LO + 4 * layer + 4]
        wqkv, wout, router_b = fetch_dense(attention[layer], router[layer - 1], width)
        normed_b, dispatch, combine = route(middle, valid, router_b, gains)
        grad_b = grad_hidden.astype(jnp.bfloat16)
        grad_combine = matmul(grad_b, returned, "ird,ied->ire")
        grad_returned = matmul(combine.astype(jnp.bfloat16), grad_b, "ire,ird->ied").astype(
            jnp.bfloat16
        )
        grad_received = to_experts(grad_returned)
        rows_all, grads_all = (
            lax.all_gather(received, "dp", axis=0, tiled=True),
            lax.all_gather(grad_received, "dp", axis=0, tiled=True),
        )
        grad_part, grad_win, grad_wout = expert_backward(
            rows_all,
            grads_all,
            expert_in[layer - 1].astype(jnp.bfloat16),
            expert_out[layer - 1].astype(jnp.bfloat16),
        )
        grad_slots = sum_rows(grad_part).astype(jnp.bfloat16)
        grad_home = from_experts(grad_slots)
        grad_dispatch = matmul(normed_b, grad_home, "ird,ied->ire")
        grad_normed = matmul(dispatch.astype(jnp.bfloat16), grad_home, "ire,ied->ird")
        grad_route = dispatch * (
            grad_dispatch - jnp.sum(grad_dispatch * dispatch, 1, keepdims=True)
        ) + combine * (grad_combine - jnp.sum(grad_combine * combine, 2, keepdims=True))
        grad_route_b = grad_route.astype(jnp.bfloat16)
        grad_router = matmul(normed_b, grad_route_b, "ird,ire->de")
        grad_normed = grad_normed + matmul(grad_route_b, router_b, "ire,de->ird")
        grad_norm_x, grad_gain_two, grad_bias_two = norm_back(
            middle, gains[2], gains[3], grad_normed
        )
        grad_middle = grad_hidden + grad_norm_x
        grad_hidden, grad_dense, grad_gain_one, grad_bias_one = attention_backward(
            before, valid, grad_middle, wqkv, wout, gains
        )
        local_dense, local_router = (
            lax.psum_scatter(grad_dense, ("dp", "fsdp"), scatter_dimension=1, tiled=True),
            lax.psum_scatter(
                router_to_flat(grad_router), ("dp", "fsdp"), scatter_dimension=0, tiled=True
            ),
        )
        dense_grads[layer] = local_dense
        router_grads[layer - 1] = local_router.reshape(router.shape[1:])
        win_grads[layer - 1] = grad_win
        wout_grads[layer - 1] = grad_wout
        gain_grads[layer] = jnp.stack([grad_gain_one, grad_bias_one, grad_gain_two, grad_bias_two])
    gains = norm_table[LEN_LO : LEN_LO + 4]
    grad_middle, grad_mlp_in, grad_mlp_out, grad_gain_two, grad_bias_two = mlp_backward(
        first_middle, grad_hidden, mlp_in, mlp_out, gains
    )
    grad_hidden, grad_dense_first, grad_gain_one, grad_bias_one = attention_backward(
        first_input, valid, grad_middle, wqkv_first, wout_first, gains
    )
    gain_grads[0] = jnp.stack([grad_gain_one, grad_bias_one, grad_gain_two, grad_bias_two])
    grad_embedded = grad_hidden * valid[..., None]
    grad_embed_t = matmul(grad_embedded.astype(jnp.bfloat16), patches, "ird,irp->dp")
    grad_first_all = jnp.concatenate([grad_embed_t, grad_mlp_in, grad_mlp_out], 1)
    grad_first, dense_grads[0] = (
        lax.psum_scatter(grad_first_all, ("dp", "fsdp"), scatter_dimension=1, tiled=True),
        lax.psum_scatter(grad_dense_first, ("dp", "fsdp"), scatter_dimension=1, tiled=True),
    )
    grad_pos = jnp.sum(jnp.where(high_mask, 0.0, grad_embedded), 0)[:LEN_LO] + jnp.dot(
        interp.T, jnp.sum(jnp.where(high_mask, grad_embedded, 0.0), 0), precision=PRECISE
    )
    grad_table = jnp.concatenate(
        [grad_pos] + gain_grads + [jnp.stack([grad_final_gain, grad_final_bias])], 0
    )
    grad_attention = jnp.stack(dense_grads)
    grad_router_all = jnp.stack(router_grads)
    grad_expert_in = jnp.stack(win_grads)
    grad_expert_out = jnp.stack(wout_grads)
    local_squares = (
        jnp.sum(grad_first * grad_first)
        + jnp.sum(grad_attention * grad_attention)
        + jnp.sum(grad_router_all * grad_router_all)
        + jnp.sum(grad_expert_in * grad_expert_in)
        + jnp.sum(grad_expert_out * grad_expert_out)
    )
    shared_head, shared_table, loss_total, squares = lax.psum(
        (grad_head, grad_table, loss_part, local_squares), ("dp", "fsdp")
    )
    norm = jnp.sqrt(
        squares + jnp.sum(shared_head * shared_head) + jnp.sum(shared_table * shared_table)
    )
    scale = jnp.minimum(1.0, CLIP_NORM / norm)
    new_first = adam(
        dense_weights, dense_weights_first, dense_weights_second, grad_first * scale, LEARN_RATE
    )
    new_attention = adam(
        attention, attention_first, attention_second, grad_attention * scale, ATTENTION_RATE
    )
    new_router = adam(router, router_first, router_second, grad_router_all * scale, LEARN_RATE)
    new_expert_in = adam(
        expert_in, expert_in_first, expert_in_second, grad_expert_in * scale, EXPERT_RATE
    )
    new_expert_out = adam(
        expert_out, expert_out_first, expert_out_second, grad_expert_out * scale, LEARN_RATE
    )
    new_classifier = adam(
        classifier, classifier_first, classifier_second, shared_head * scale, LEARN_RATE
    )
    new_table = adam(
        norm_table, norm_table_first, norm_table_second, shared_table * scale, TABLE_RATE
    )
    return (
        loss_total,
        norm,
        new_first[0],
        new_first[1],
        new_first[2],
        new_attention[0],
        new_attention[1],
        new_attention[2],
        new_router[0],
        new_router[1],
        new_router[2],
        new_expert_in[0],
        new_expert_in[1],
        new_expert_in[2],
        new_expert_out[0],
        new_expert_out[1],
        new_expert_out[2],
        new_classifier[0],
        new_classifier[1],
        new_classifier[2],
        new_table[0],
        new_table[1],
        new_table[2],
    )


def solution(mesh):
    return jax.shard_map(
        on_device,
        mesh=mesh,
        in_specs=(
            P(("dp", "fsdp"), None, None),
            P(("dp", "fsdp")),
            P(("dp", "fsdp")),
            P(None, ("dp", "fsdp")),
            P(None, None, ("dp", "fsdp")),
            P(None, "dp", "fsdp"),
            P(None, "fsdp", None, "dp"),
            P(None, "fsdp", "dp", None),
            P(),
            P(),
            P(None, ("dp", "fsdp")),
            P(None, ("dp", "fsdp")),
            P(None, None, ("dp", "fsdp")),
            P(None, None, ("dp", "fsdp")),
            P(None, "dp", "fsdp"),
            P(None, "dp", "fsdp"),
            P(None, "fsdp", None, "dp"),
            P(None, "fsdp", None, "dp"),
            P(None, "fsdp", "dp", None),
            P(None, "fsdp", "dp", None),
            P(),
            P(),
            P(),
            P(),
        ),
        out_specs=(
            P(),
            P(),
            P(None, ("dp", "fsdp")),
            P(None, ("dp", "fsdp")),
            P(None, ("dp", "fsdp")),
            P(None, None, ("dp", "fsdp")),
            P(None, None, ("dp", "fsdp")),
            P(None, None, ("dp", "fsdp")),
            P(None, "dp", "fsdp"),
            P(None, "dp", "fsdp"),
            P(None, "dp", "fsdp"),
            P(None, "fsdp", None, "dp"),
            P(None, "fsdp", None, "dp"),
            P(None, "fsdp", None, "dp"),
            P(None, "fsdp", "dp", None),
            P(None, "fsdp", "dp", None),
            P(None, "fsdp", "dp", None),
            P(),
            P(),
            P(),
            P(),
            P(),
            P(),
        ),
        check_vma=False,
    )
```

profile of v0, /device:TPU:0, one launch (start us, length us, event | category | flops | bytes accessed | tf_op | source)
XLA Modules:
  0.0 2438.7 jit_solution(13202341309966527321)
XLA Ops:
  20.1 76.1 %all-gather.3 = bf16[32,1,1536]{2,1,0:T(2,128)(2,1)} all-gather(bf16[1,1,1536]{2,1,0:T(2,128)(2,1)S(1)} %reshape.688), channel_id=1, replica_groups=mesh['dp'=2,'fsdp'=16] {'dp','fsdp'}, dimensions={0}, use_global_device_ids=true | all-gather | bytes 101376 | tf_op jit(solution)/shard_map/all_gather | solution.py:57
  137.1 49.2 %all-gather.10.cloned.1.call-done = bf16[384,3840]{0,1:T(8,128)(2,1)} async-done(((bf16[384,120]{0,1:T(8,128)(2,1)}), bf16[384,3840]{0,1:T(8,128)(2,1)}) %all-gather.10.cloned.1.call-update) | async-done | bytes 2949136 | tf_op jit(solution)/shard_map/all_gather | solution.py:271
  193.7 112.1 %while.87 = (s32[]{:T(128)}, f32[4,576,384]{2,1,0:T(8,128)}, f32[4,576,384]{2,1,0:T(8,128)}, f32[4,384]{1,0:T(4,128)}, bf16[384,1152]{1,0:T(8,128)(2,1)}, /*inde...) while((s32[]{:T(128)}, f32[4,576,384]{2,1,0:T(8,128)}, f32[4,576,384]{2,1,0:T(8,128)}, ...), condition=%wide.region_5.6_spmd, body=%wide.region_0.5_spmd.sunk | while | flops 1203906304 | bytes 30732044 | solution.py:147
  325.5 109.7 %while.88 = (s32[]{:T(128)}, f32[4,576,384]{2,1,0:T(8,128)}, f32[4,576,384]{2,1,0:T(8,128)}, f32[4,384]{1,0:T(4,128)}, bf16[384,1152]{1,0:T(8,128)(2,1)}, /*inde...) while((s32[]{:T(128)}, f32[4,576,384]{2,1,0:T(8,128)}, f32[4,576,384]{2,1,0:T(8,128)}, ...), condition=%wide.region_13.14_spmd, body=%wide.region_8.13_spmd.sunk | while | flops 1203906304 | bytes 30732044 | solution.py:147
  455.3 9.8 convert.68
  465.1 9.8 convert.67
  490.4 9.9 reduce-scatter.9.cloned.1.call-done
  511.6 74.8 %all-gather.4 = bf16[32,1,1536]{2,1,0:T(2,128)(2,1)} all-gather(bf16[1,1,1536]{2,1,0:T(2,128)(2,1)} %reshape.690), channel_id=1, replica_groups=mesh['dp'=2,'fsdp'=16] {'dp','fsdp'}, dimensions={0}, use_global_device_ids=true | all-gather | bytes 101376 | tf_op jit(solution)/shard_map/all_gather | solution.py:57
  618.2 110.6 %while.89 = (s32[]{:T(128)}, f32[4,576,384]{2,1,0:T(8,128)}, f32[4,576,384]{2,1,0:T(8,128)}, f32[4,384]{1,0:T(4,128)}, bf16[384,1152]{1,0:T(8,128)(2,1)}, /*inde...) while((s32[]{:T(128)}, f32[4,576,384]{2,1,0:T(8,128)}, f32[4,576,384]{2,1,0:T(8,128)}, ...), condition=%wide.region_26.27_spmd, body=%wide.region_21.26_spmd.sunk | while | flops 1203906304 | bytes 30732044 | solution.py:147
  742.5 15.8 all_to_all.144
  835.4 15.5 all_to_all.145
  888.5 13.3 fusion.209
  933.9 287.4 %while.90 = (s32[]{:T(128)}, f32[384,1152]{1,0:T(8,128)}, f32[384,384]{1,0:T(8,128)}, f32[384]{0:T(512)}, f32[384]{0:T(512)}, /*index=5*/f32[4,576,384]{2,1,0:T(...) while((s32[]{:T(128)}, f32[384,1152]{1,0:T(8,128)}, ...), condition=%wide.region_59.60_spmd.clone, body=%wide.region_49.0_spmd.clone.sunk | while | flops 3445459456 | bytes 160614656 | solution.py:173
  1230.6 19.2 all_to_all.146
  1307.3 13.3 fusion.214
  1350.1 285.1 %while.91 = (s32[]{:T(128)}, f32[384,1152]{1,0:T(8,128)}, f32[384,384]{1,0:T(8,128)}, f32[384]{0:T(512)}, f32[384]{0:T(512)}, /*index=5*/f32[4,576,384]{2,1,0:T(...) while((s32[]{:T(128)}, f32[384,1152]{1,0:T(8,128)}, ...), condition=%wide.region_75.76_spmd.clone, body=%wide.region_65.0_spmd.clone.sunk | while | flops 3445459456 | bytes 160614656 | solution.py:173
  1635.2 17.0 fusion.154
  1679.5 285.9 %while.92 = (s32[]{:T(128)}, f32[384,1152]{1,0:T(8,128)}, f32[384,384]{1,0:T(8,128)}, f32[384]{0:T(512)}, f32[384]{0:T(512)}, /*index=5*/f32[4,576,384]{2,1,0:T(...) while((s32[]{:T(128)}, f32[384,1152]{1,0:T(8,128)}, ...), condition=%wide.region_88.89_spmd.clone, body=%wide.region_78.88_spmd.clone.sunk | while | flops 3445459456 | bytes 160614656 | solution.py:173
  2057.7 11.9 multiply_reduce_fusion.16
  2069.6 11.9 multiply_reduce_fusion.15
  2087.3 185.4 %all-reduce.8.cloned.1.call-done = (f32[384,3840]{1,0:T(8,128)}, f32[49152]{0:T(1024)}, f32[49152]{0:T(1024)}, f32[385,1000]{1,0:T(8,128)}, f32[210,384]{1,0:T(8,128)}) async-done(((f32[384,3840]{1,0:T(8,128)}, f32[49152]{0:T(1024)}, f32[49152]{0:T(1024)}, f32[385,1000]{1,0:T(8,128)}, f32[210,384]{1,0:T(8,128)}), (f32[384,3840]{1,0:T(8,128)}, f32[49152]{0:T(1024)}, f32[49152]{0:T(1024)}, ...) | async-done | bytes 8154032
  2287.6 40.0 %all-reduce.4 = (f32[]{:T(128)}, f32[]{:T(128)}) all-reduce(f32[]{:T(128)S(6)} %div.417, f32[]{:T(128)S(6)} %add.569), channel_id=1, replica_groups=mesh['dp'=2,'fsdp'=16] {'dp','fsdp'}, use_global_device_ids=true, to_apply=%region_41.42 | all-reduce | flops 2 | bytes 16 | tf_op jit(solution)/shard_map/psum | solution.py:410
  2340.7 41.7 %add_subtract_fusion = (f32[2,8,384,768]{3,2,1,0:T(8,128)}, f32[2,8,384,768]{3,2,1,0:T(8,128)}, f32[2,8,384,768]{3,2,1,0:T(8,128)}) fusion(f32[2,8,384,768]{3,2,1,0:T(8,128)} %param.42, f32[]{:T(128)S(6)} %min.3, f32[1,8,384,768]{3,2,1,0:T(8,128)} %convolution_bitcast_fusion.5, f32[1,8,384,768]{3,2,1,0:T(8,128)} %convolution_bitcast_fusion.6, ...), kind=kLoop, calls=%fused_computation.273 | loop fusion | flops 75497472 | bytes 132120576 | tf_op jit(solution)/shard_map/sub | solution.py:228
  2382.4 43.4 %multiply_subtract_fusion = (f32[2,8,768,384]{3,2,1,0:T(8,128)}, f32[2,8,768,384]{3,2,1,0:T(8,128)}, f32[2,8,768,384]{3,2,1,0:T(8,128)}) fusion(f32[2,8,768,384]{3,2,1,0:T(8,128)} %param.43, f32[]{:T(128)S(6)} %min.3, f32[1,8,768,384]{3,2,1,0:T(8,128)} %convolution_bitcast_fusion.3, f32[1,8,768,384]{3,2,1,0:T(8,128)} %convolution_bitcast_fusion.4, ...), kind=kLoop, calls=%fused_computation.271 | loop fusion | flops 80216064 | bytes 132120576 | tf_op jit(solution)/shard_map/sub | solution.py:228
  (1570 shorter events, 1751.0 us)
Async XLA Ops:
  7.2 179.1 %copy-start = (bf16[4,576,768]{2,1,0:T(8,128)(2,1)S(1)}, bf16[4,576,768]{2,1,0:T(8,128)(2,1)}, u32[]{:S(2)}) copy-start(bf16[4,576,768]{2,1,0:T(8,128)(2,1)} %param.36) | copy-start | bytes 10616836
  7.2 107.8 %all-gather.12.cloned.1.call-start = ((), (), s32[]{:S(2)}) async-start(), calls=%async_computation.23 | async-start | bytes 1216512 | tf_op jit(solution)/shard_map/all_gather | solution.py:272
  9.0 116.0 %all-gather.14.cloned.1.call-start = ((), (), s32[]{:S(2)}) async-start(), calls=%async_computation.24 | async-start | bytes 1216512 | tf_op jit(solution)/shard_map/all_gather | solution.py:56
  9.8 176.5 %all-gather.10.cloned.1.call-start = ((), (), s32[]{:S(2)}) async-start(), calls=%async_computation.15 | async-start | bytes 3041280 | tf_op jit(solution)/shard_map/all_gather | solution.py:271
  17.8 91.2 %copy-start.176 = (s32[4]{0:T(128)S(1)}, s32[4]{0:T(128)}, u32[]{:S(2)}) copy-start(s32[4]{0:T(128)} %param.37) | copy-start | bytes 52
  109.0 201.8 %copy-start.120 = (f32[384]{0:T(512)}, f32[384]{0:T(512)S(1)}, u32[]{:S(2)}) copy-start(f32[384]{0:T(512)S(1)} %get-tuple-element.716) | copy-start | bytes 4612
  450.9 24.1 all-to-all-start
  455.3 45.0 %reduce-scatter.9.cloned.1.call-start = ((), (), s32[]{:S(2)}) async-start(), calls=%async_computation.16 | async-start | bytes 2359296 | tf_op jit(solution)/shard_map/reduce_scatter | solution.py:90
  489.8 106.0 %all-gather.16.cloned.1.call-start = ((), (), s32[]{:S(2)}) async-start(), calls=%async_computation.25 | async-start | bytes 1216512 | tf_op jit(solution)/shard_map/all_gather | solution.py:56
  502.5 105.0 %all-to-all-start.1 = ((bf16[64,8,384]{2,1,0:T(8,128)(2,1)}), bf16[64,8,384]{2,1,0:T(8,128)(2,1)}, u32[]{:S(2)}, u32[]{:S(2)}) async-start(bf16[64,8,384]{2,1,0:T(8,128)(2,1)} %copy.378), calls=%async_computation.2 | async-start | bytes 786432 | tf_op jit(solution)/shard_map/all_to_all | solution.py:86
  509.3 272.5 %reduce-scatter.11.cloned.1.call-start = ((), (), s32[]{:S(2)}) async-start(), calls=%async_computation.17 | async-start | bytes 2359296 | tf_op jit(solution)/shard_map/reduce_scatter | solution.py:90
  783.9 20.0 all-to-all-start.3
  790.8 84.9 %reduce-scatter.13.cloned.1.call-start = ((), (), s32[]{:S(2)}) async-start(), calls=%async_computation.18 | async-start | bytes 2359296 | tf_op jit(solution)/shard_map/reduce_scatter | solution.py:90
  877.9 24.0 all-to-all-start.5
  884.8 413.2 %reduce-scatter.15.cloned.1.call-start = ((), (), s32[]{:S(2)}) async-start(), calls=%async_computation.19 | async-start | bytes 2359296 | tf_op jit(solution)/shard_map/reduce_scatter | solution.py:90
  1265.2 816.3 %reduce-scatter.21.cloned.1.call-start = ((), (), s32[]{:S(2)}) async-start(), calls=%async_computation.22 | async-start | bytes 2433024 | tf_op jit(solution)/shard_map/reduce_scatter | solution.py:368
  1300.1 20.5 all-to-all-start.7
  1304.4 777.2 %reduce-scatter.19.cloned.1.call-start = ((), (), s32[]{:S(2)}) async-start(), calls=%async_computation.21 | async-start | bytes 2433024 | tf_op jit(solution)/shard_map/reduce_scatter | solution.py:368
  1677.4 408.3 %reduce-scatter.17.cloned.1.call-start = ((), (), s32[]{:S(2)}) async-start(), calls=%async_computation.20 | async-start | bytes 2433024 | tf_op jit(solution)/shard_map/reduce_scatter | solution.py:391
  1985.4 287.3 %all-reduce.8.cloned.1.call-start = ((), (), s32[]{:S(2)}) async-start(), calls=%async_computation.26 | async-start | bytes 16457728
  2382.4 43.4 %copy-start.34 = (f32[385,1000]{1,0:T(8,128)S(1)}, f32[385,1000]{1,0:T(8,128)}, u32[]{:S(2)}) copy-start(f32[385,1000]{1,0:T(8,128)} %param.44) | copy-start | bytes 4620004
  2382.4 43.4 %copy-start.51 = (f32[385,1000]{1,0:T(8,128)S(1)}, f32[385,1000]{1,0:T(8,128)}, u32[]{:S(2)}) copy-start(f32[385,1000]{1,0:T(8,128)} %get-tuple-element.840) | copy-start | bytes 4620004
  2382.4 43.4 %copy-start.66 = (f32[385,1000]{1,0:T(8,128)S(1)}, f32[385,1000]{1,0:T(8,128)}, u32[]{:S(2)}) copy-start(f32[385,1000]{1,0:T(8,128)} %param.56) | copy-start | bytes 4620004
  2382.4 43.4 %copy-start.67 = (f32[385,1000]{1,0:T(8,128)S(1)}, f32[385,1000]{1,0:T(8,128)}, u32[]{:S(2)}) copy-start(f32[385,1000]{1,0:T(8,128)} %param.57) | copy-start | bytes 4620004
  (393 other events, 1408.1 us)
Sparse Core Ops, SparseCore 0:
  11.5 56.7 all-gather.11
  71.8 53.1 all-gather.13
  128.4 57.7 all-gather.9
  490.0 10.3 reduce-scatter.8
  504.0 55.8 all-gather.15
  774.5 7.2 reduce-scatter.10
  868.6 7.0 reduce-scatter.12
  1265.4 6.9 reduce-scatter.14
  1298.1 97.0 reduce-scatter.20
  1677.5 100.1 reduce-scatter.18
  1985.5 100.1 reduce-scatter.16
  2094.8 177.8 all-reduce.7
where the time goes:
time: 2460 us; the launch traced here: 2440 us
  matrix products  942 us (38%)
  other arithmetic  492 us (20%)
  local copies, waits for them, and re-layouts  413 us (17%)
  waiting for transfers between devices  279 us (11%)
  blocking collectives  252 us (10%)
  starting transfers between devices  29.7 us (1%)
    dot_general x197, matrix products, matmul(): return jnp.einsum(form, left, right, preferred_element_type=jnp.float32)  736 us
    sub x24, matrix products, attend(): probs = jax.nn.softmax(scores, axis=-1)  201 us
    unnamed x13, waiting for transfers between devices  187 us
    split x96, local copies, waits for them, and re-layouts, attend(): jnp.split(mixed, 3, axis=1)  170 us
    all_gather x2, blocking collectives, fetch_dense(): lax.all_gather(router_layer.astype(jnp.bfloat16).reshape(-1), ('dp', 'fsd...  151 us
    convert_element_type x12, other arithmetic, attend_back(): (probs * (grad_probs - jnp.sum(grad_probs * probs, -1, keepdims=True))).a...  113 us
    sub x7, other arithmetic, adam(): return (weight - rate * (ratio + WEIGHT_DECAY * weight), first, second)  95.2 us
    all_to_all x3, blocking collectives, to_experts(): lax.all_to_all(values, 'fsdp', split_axis=1, concat_axis=0, tiled=True)  50.4 us
  transfers between devices with their start and end apart: 17, of which 8 were waited for; matrix products, arithmetic and copies ran while one was open for 37% of the time, Pallas kernels for 0%

commit v1 on v0

v1 whole, which is shorter than its diff:
```python
import functools

import jax
import jax.numpy as jnp
from jax import lax
from jax.experimental import pallas as pl
from jax.experimental.pallas import tpu as pltpu
from jax.sharding import PartitionSpec as P

HEADS = 6
FF = 1536
G_LO = 14
G_HI = 24
LEN = 576
LEN_LO = 196
ROWS_LO = 208
STEP = 10


LN_EPS = 1e-06
CLIP_NORM = 0.001
LEARN_RATE = 0.05
ATTENTION_RATE = 0.15
EXPERT_RATE = 1.0
TABLE_RATE = 0.5
BETA_ONE = 0.9
BETA_TWO = 0.95
ADAM_EPS = 1e-10
WEIGHT_DECAY = 0.1
SMOOTH = 0.1
NEG_FILL = -1e30
PRECISE = lax.Precision.HIGHEST
F32 = jnp.float32
BF16 = jnp.bfloat16
VMEM_BYTES = 60 * 1024 * 1024


def interp_matrix():
    rows = jnp.arange(G_HI, dtype=jnp.float32)[:, None]
    cols = jnp.arange(G_LO, dtype=jnp.float32)[None, :]
    weight = jnp.maximum(0.0, 1.0 - jnp.abs(rows * (G_LO - 1) - cols * (G_HI - 1)) / (G_HI - 1))
    return (weight[:, None, :, None] * weight[None, :, None, :]).reshape(G_HI * G_HI, G_LO * G_LO)


def matmul(left, right, form):
    return jnp.einsum(form, left, right, preferred_element_type=jnp.float32)


def contract(left, right, left_dim, right_dim):
    return lax.dot_general(
        left, right, (((left_dim,), (right_dim,)), ((), ())), preferred_element_type=F32
    )


def nn(left, right):
    return contract(left, right, 1, 0)


def nt(left, right):
    return contract(left, right, 1, 1)


def tn(left, right):
    return contract(left, right, 0, 0)


def normalise(values):
    center = values - jnp.mean(values, -1, keepdims=True)
    rate = lax.rsqrt(jnp.mean(center * center, -1, keepdims=True) + LN_EPS)
    return center * rate, rate


def normalise_back(unit, rate, gain, grad):
    scaled = grad * gain
    inner = scaled - jnp.mean(scaled, -1, keepdims=True)
    grad_in = rate * (inner - unit * jnp.mean(scaled * unit, -1, keepdims=True))
    return (
        grad_in,
        jnp.sum(grad * unit, 0, keepdims=True),
        jnp.sum(grad, 0, keepdims=True),
    )


def row_number(shape):
    return lax.broadcasted_iota(jnp.int32, shape, 0)


def side_masks():
    lane = lax.broadcasted_iota(jnp.int32, (1, 128), 1)
    first = (lane < 64).astype(F32)
    return (first.astype(BF16), (1.0 - first).astype(BF16))


def lanes(offset):
    return pl.ds(pl.multiple_of(offset, 128), 128)


GELU_RATE = 0.7978845608028654


def gelu(v):
    return 0.5 * v * (1.0 + jnp.tanh(GELU_RATE * (v + 0.044715 * (v * v * v))))


def gelu_both(v):
    square = v * v
    bend = jnp.tanh(GELU_RATE * (v + 0.044715 * (square * v)))
    half = 0.5 * (1.0 + bend)
    slope = half + 0.5 * v * (1.0 - bend * bend) * (GELU_RATE * (1.0 + 3 * 0.044715 * square))
    return v * half, slope


def attention_rows(rows, limit, qkv, context):
    width = context.shape[1]
    first = lax.broadcasted_iota(jnp.int32, (rows, 128), 1) < 64
    masks = side_masks()

    def pair(index, carry):
        offset = index * 128
        query = qkv[:rows, lanes(offset)] * BF16(0.125)
        keys = qkv[:rows, lanes(width + offset)]
        values = qkv[:rows, lanes(2 * width + offset)]
        found = []
        for side in (0, 1):
            scores = nt(query * masks[side], keys)
            if limit is not None:
                lane = lax.broadcasted_iota(jnp.int32, (rows, rows), 1)
                scores = jnp.where(lane < limit, scores, NEG_FILL)
            raised = jnp.exp(scores - jnp.max(scores, 1, keepdims=True))
            total = jnp.sum(raised, 1, keepdims=True)
            found.append(nn(raised.astype(BF16), values) * (1.0 / total))
        context[:rows, lanes(offset)] = jnp.where(first, found[0], found[1]).astype(BF16)
        return carry

    lax.fori_loop(0, width // 128, pair, 0)


def attention_rows_back(rows, limit, qkv, grad_context, grad_qkv):
    width = grad_context.shape[1]
    masks = side_masks()

    def pair(index, carry):
        offset = index * 128
        query = qkv[:rows, lanes(offset)] * BF16(0.125)
        keys = qkv[:rows, lanes(width + offset)]
        values = qkv[:rows, lanes(2 * width + offset)]
        grad = grad_context[:rows, lanes(offset)]
        grad_query = grad_keys = grad_values = None
        for side in (0, 1):
            query_side = query * masks[side]
            grad_side = grad * masks[side]
            scores = nt(keys, query_side)
            if limit is not None:
                scores = jnp.where(row_number((rows, rows)) < limit, scores, NEG_FILL)
            raised = jnp.exp(scores - jnp.max(scores, 0, keepdims=True))
            probs = raised * (1.0 / jnp.sum(raised, 0, keepdims=True))
            part_values = nn(probs.astype(BF16), grad_side)
            grad_probs = nt(values, grad_side)
            mixed = jnp.sum(probs * grad_probs, 0, keepdims=True)
            grad_scores = (probs * (grad_probs - mixed)).astype(BF16)
            part_keys = nn(grad_scores, query_side)
            part_query = tn(grad_scores, keys * masks[side])
            if side == 0:
                grad_query, grad_keys, grad_values = part_query, part_keys, part_values
            else:
                grad_query = grad_query + part_query
                grad_keys = grad_keys + part_keys
                grad_values = grad_values + part_values
        grad_qkv[:rows, lanes(offset)] = (grad_query * 0.125).astype(BF16)
        grad_qkv[:rows, lanes(width + offset)] = grad_keys.astype(BF16)
        grad_qkv[:rows, lanes(2 * width + offset)] = grad_values.astype(BF16)
        return carry

    lax.fori_loop(0, width // 128, pair, 0)


def attention_forward(rows, limit, hidden, gains, weights, qkv, context):
    width = hidden.shape[1]
    unit, _ = normalise(hidden)
    normed = (unit * gains[0:1] + gains[1:2]).astype(BF16)
    qkv[:rows] = nt(normed, weights[: 3 * width]).astype(BF16)
    attention_rows(rows, limit, qkv, context)
    return hidden + nn(context[:rows], weights[3 * width :])


def attention_backward(
    rows, limit, hidden, grad_middle, gains, weights, qkv, context, hold_context, hold_qkv,
    grad_weights, grad_gains,
):
    width = hidden.shape[1]
    grad_b = grad_middle.astype(BF16)
    hold_context[:rows] = nt(grad_b, weights[3 * width :]).astype(BF16)
    grad_weights[3 * width :] += tn(context[:rows], grad_b)
    attention_rows_back(rows, limit, qkv, hold_context, hold_qkv)
    unit, rate = normalise(hidden)
    normed = (unit * gains[0:1] + gains[1:2]).astype(BF16)
    grad_weights[: 3 * width] += tn(hold_qkv[:rows], normed)
    grad_normed = nn(hold_qkv[:rows], weights[: 3 * width])
    grad_in, grad_gain, grad_bias = normalise_back(unit, rate, gains[0:1], grad_normed)
    grad_gains[0:1] += grad_gain
    grad_gains[1:2] += grad_bias
    return grad_middle + grad_in


def mlp_forward(rows, middle, gains, weights, pixels):
    unit, _ = normalise(middle)
    normed = (unit * gains[2:3] + gains[3:4]).astype(BF16)
    chunk = middle.shape[1]
    total = middle
    for start in range(0, FF, chunk):
        pre = nt(normed, weights[pixels + start : pixels + start + chunk])
        out = weights[pixels + FF + start : pixels + FF + start + chunk]
        total = total + nn(gelu(pre).astype(BF16), out)
    return total


def mlp_backward(rows, middle, grad, gains, weights, pixels, grad_weights, grad_gains):
    unit, rate = normalise(middle)
    normed = (unit * gains[2:3] + gains[3:4]).astype(BF16)
    grad_b = grad.astype(BF16)
    chunk = middle.shape[1]
    grad_normed = None
    for start in range(0, FF, chunk):
        first = slice(pixels + start, pixels + start + chunk)
        second = slice(pixels + FF + start, pixels + FF + start + chunk)
        hid, slope = gelu_both(nt(normed, weights[first]))
        grad_weights[second] += tn(hid.astype(BF16), grad_b)
        grad_pre = (nt(grad_b, weights[second]) * slope).astype(BF16)
        grad_weights[first] += tn(grad_pre, normed)
        part = nn(grad_pre, weights[first])
        grad_normed = part if grad_normed is None else grad_normed + part
    grad_in, grad_gain, grad_bias = normalise_back(unit, rate, gains[2:3], grad_normed)
    grad_gains[2:3] += grad_gain
    grad_gains[3:4] += grad_bias
    return grad + grad_in


def route(limit, middle, gains, router):
    unit, rate = normalise(middle)
    normed = (unit * gains[2:3] + gains[3:4]).astype(BF16)
    logits = nt(normed, router[...])
    masked = logits
    if limit is not None:
        masked = jnp.where(row_number(logits.shape) < limit, logits, NEG_FILL)
    raised = jnp.exp(masked - jnp.max(masked, 0, keepdims=True))
    dispatch = raised * (1.0 / jnp.sum(raised, 0, keepdims=True))
    raised = jnp.exp(logits - jnp.max(logits, 1, keepdims=True))
    combine = raised * (1.0 / jnp.sum(raised, 1, keepdims=True))
    return unit, rate, normed, dispatch, combine


def masked_rows(limit, values):
    if limit is None:
        return values
    return jnp.where(row_number(values.shape) < limit, values, 0.0)


def by_image(name, body, scalars, per_image, whole, out_image, out_sum, scratch=()):
    images = scalars[0].shape[0]
    counts = (len(scalars), len(per_image), len(whole), len(out_image), len(out_sum), len(scratch))

    def kernel(*refs):
        groups, at = [], 0
        for count in counts:
            groups.append(refs[at : at + count])
            at += count
        index = pl.program_id(0)

        @pl.when(index == 0)
        def _():
            for ref in groups[4]:
                ref[...] = jnp.zeros_like(ref)

        numbers = [ref[index] for ref in groups[0]]

        @pl.when(numbers[0] == 1)
        def _():
            body(LEN, None, numbers, *groups[1:])

        @pl.when(numbers[0] != 1)
        def _():
            body(ROWS_LO, LEN_LO + numbers[0], numbers, *groups[1:])

    def image_spec(shape):
        return pl.BlockSpec((None,) + tuple(shape[1:]), lambda i, *_: (i, 0, 0))

    return pl.pallas_call(
        kernel,
        grid_spec=pltpu.PrefetchScalarGridSpec(
            num_scalar_prefetch=len(scalars),
            grid=(images,),
            in_specs=[image_spec(a.shape) for a in per_image]
            + [pl.BlockSpec(memory_space=pltpu.VMEM) for _ in whole],
            out_specs=[image_spec((images,) + shape) for shape, _ in out_image]
            + [pl.BlockSpec(shape, lambda i, *_: (0, 0)) for shape in out_sum],
            scratch_shapes=list(scratch),
        ),
        out_shape=[jax.ShapeDtypeStruct((images,) + shape, dtype) for shape, dtype in out_image]
        + [jax.ShapeDtypeStruct(shape, F32) for shape in out_sum],
        compiler_params=pltpu.CompilerParams(vmem_limit_bytes=VMEM_BYTES),
        name=name,
    )(*scalars, *per_image, *whole)


def first_forward(resolution, patches, dense, attention, positions, gains, width):
    pixels = patches.shape[2]

    def body(rows, limit, numbers, images, whole, outs, sums, scratch):
        dense_ref, attention_ref, position_ref, gain_ref = whole
        start, qkv, context, middle, last = outs
        place = position_ref[0 if limit is not None else 1, :rows]
        embedded = masked_rows(limit, nn(images[0][:rows], dense_ref[:pixels]) + place)
        start[:rows] = embedded
        middle_rows = attention_forward(
            rows, limit, embedded, gain_ref, attention_ref, qkv, context
        )
        middle[:rows] = middle_rows
        last[:rows] = mlp_forward(rows, middle_rows, gain_ref, dense_ref, pixels)

    return by_image(
        "first_forward",
        body,
        [resolution],
        [patches],
        [dense, attention, positions, gains],
        [
            ((LEN, width), F32),
            ((LEN, 3 * width), BF16),
            ((LEN, width), BF16),
            ((LEN, width), F32),
            ((LEN, width), F32),
        ],
        [],
    )


def sparse_forward(resolution, hidden, mixing, attention, router, gains):
    width = hidden.shape[2]
    experts = router.shape[0]

    def body(rows, limit, numbers, images, whole, outs, sums, scratch):
        attention_ref, router_ref, gain_ref = whole
        before, qkv, context, middle, combine, slots = ([None] + list(outs))[-6:]
        hidden_rows = images[0][:rows]
        if mixing is not None:
            hidden_rows = hidden_rows + nn(images[1][:rows], images[2][...])
            before[:rows] = hidden_rows
        middle_rows = attention_forward(
            rows, limit, hidden_rows, gain_ref, attention_ref, qkv, context
        )
        middle[:rows] = middle_rows
        _, _, normed, dispatch, share = route(limit, middle_rows, gain_ref, router_ref)
        combine[:rows] = share.astype(BF16)
        slots[...] = tn(dispatch.astype(BF16), normed).astype(BF16)

    outs = [
        ((LEN, 3 * width), BF16),
        ((LEN, width), BF16),
        ((LEN, width), F32),
        ((LEN, experts), BF16),
        ((experts, width), BF16),
    ]
    if mixing is not None:
        outs = [((LEN, width), F32)] + outs
    return by_image(
        "sparse_forward",
        body,
        [resolution],
        [hidden] + list(mixing or ()),
        [attention, router, gains],
        outs,
        [],
    )


def top(resolution, labels, middle, combine, returned, head, head_bias, last_gains, classes, images):
    width = middle.shape[2]
    experts = returned.shape[1]
    padded = head.shape[1]

    def body(rows, limit, numbers, per_image, whole, outs, sums, scratch):
        middle_ref, combine_ref, returned_ref = per_image
        head_ref, bias_ref, gain_ref = whole
        grad_hidden, grad_returned = outs
        grad_head, grad_bias_row, grad_gains, loss = sums
        length = float(LEN if limit is None else LEN_LO)
        share = combine_ref[:rows]
        hidden = middle_ref[:rows] + nn(share, returned_ref[...])
        unit, rate = normalise(hidden)
        normed = masked_rows(limit, unit * gain_ref[0:1] + gain_ref[1:2])
        pooled = jnp.sum(normed, 0, keepdims=True) * (1.0 / length)
        one_row = (row_number((8, width)) == 0).astype(F32)
        pooled_b = (one_row * pooled).astype(BF16)
        logits = nn(pooled_b, head_ref[...])[0:1] + bias_ref[...]
        shifted = logits - jnp.max(logits, 1, keepdims=True)
        raised = jnp.exp(shifted)
        total = jnp.sum(raised, 1, keepdims=True)
        log_probs = shifted - jnp.log(total)
        lane = lax.broadcasted_iota(jnp.int32, (1, padded), 1)
        target = jnp.where(lane == numbers[1], 1.0 - SMOOTH, 0.0) + jnp.where(
            lane < classes, SMOOTH / classes, 0.0
        )
        picked = jnp.sum(target * log_probs, 1, keepdims=True)
        loss[...] += jnp.broadcast_to(picked * (-1.0 / images), loss.shape)
        grad_logits = (raised * (1.0 / total) - target) * (1.0 / images)
        grad_bias_row[0:1] += grad_logits
        row_mask = (row_number((8, padded)) == 0).astype(F32)
        grad_logits_b = (row_mask * grad_logits).astype(BF16)
        grad_head[...] += tn(pooled_b, grad_logits_b)
        grad_pooled = nt(grad_logits_b, head_ref[...])[0:1] * (1.0 / length)
        grad_normed = masked_rows(limit, jnp.broadcast_to(grad_pooled, (rows, width)))
        grad_rows, grad_gain, grad_bias = normalise_back(
            unit, rate, gain_ref[0:1], grad_normed
        )
        grad_gains[0:1] += grad_gain
        grad_gains[1:2] += grad_bias
        grad_hidden[:rows] = grad_rows
        grad_returned[...] = tn(share, grad_rows.astype(BF16)).astype(BF16)

    return by_image(
        "top",
        body,
        [resolution, labels],
        [middle, combine, returned],
        [head, head_bias, last_gains],
        [((LEN, width), F32), ((experts, width), BF16)],
        [(width, padded), (8, padded), (8, width), (8, 128)],
    )


def sparse_backward(
    resolution, hidden, qkv, context, middle, grad_hidden, returned, grad_home, below, attention,
    router, gains,
):
    width = middle.shape[2]
    experts = router.shape[0]

    def body(rows, limit, numbers, images, whole, outs, sums, scratch):
        hidden_ref, qkv_ref, context_ref, middle_ref, grad_ref, returned_ref, home_ref = images[:7]
        attention_ref, router_ref, gain_ref = whole
        grad_attention, grad_router, grad_gains = sums
        grad = grad_ref[:rows]
        grad_combine = nt(grad.astype(BF16), returned_ref[...])
        unit, rate, normed, dispatch, share = route(
            limit, middle_ref[:rows], gain_ref, router_ref
        )
        home = home_ref[...]
        grad_dispatch = nt(normed, home)
        grad_normed = nn(dispatch.astype(BF16), home)
        grad_route = dispatch * (
            grad_dispatch - jnp.sum(grad_dispatch * dispatch, 0, keepdims=True)
        ) + share * (grad_combine - jnp.sum(grad_combine * share, 1, keepdims=True))
        grad_route_b = grad_route.astype(BF16)
        grad_router[...] += tn(grad_route_b, normed)
        grad_normed = grad_normed + nn(grad_route_b, router_ref[...])
        grad_in, grad_gain, grad_bias = normalise_back(unit, rate, gain_ref[2:3], grad_normed)
        grad_gains[2:3] += grad_gain
        grad_gains[3:4] += grad_bias
        grad_rows = attention_backward(
            rows, limit, hidden_ref[:rows], grad + grad_in, gain_ref, attention_ref, qkv_ref,
            context_ref, scratch[0], scratch[1], grad_attention, grad_gains,
        )
        outs[0][:rows] = grad_rows
        if below is not None:
            outs[1][...] = tn(images[7][:rows], grad_rows.astype(BF16)).astype(BF16)

    outs = [((LEN, width), F32)]
    if below is not None:
        outs.append(((experts, width), BF16))
    return by_image(
        "sparse_backward",
        body,
        [resolution],
        [hidden, qkv, context, middle, grad_hidden, returned, grad_home]
        + ([] if below is None else [below]),
        [attention, router, gains],
        outs,
        [(4 * width, width), (experts, width), (8, width)],
        [pltpu.VMEM((LEN, width), BF16), pltpu.VMEM((LEN, 3 * width), BF16)],
    )


def first_backward(resolution, patches, start, qkv, context, middle, grad_hidden, dense, attention, gains):
    width = middle.shape[2]
    pixels = patches.shape[2]

    def body(rows, limit, numbers, images, whole, outs, sums, scratch):
        patches_ref, start_ref, qkv_ref, context_ref, middle_ref, grad_ref = images
        dense_ref, attention_ref, gain_ref = whole
        grad_dense, grad_attention, grad_gains, grad_low, grad_high = sums
        grad_middle = mlp_backward(
            rows, middle_ref[:rows], grad_ref[:rows], gain_ref, dense_ref, pixels, grad_dense,
            grad_gains,
        )
        grad_rows = attention_backward(
            rows, limit, start_ref[:rows], grad_middle, gain_ref, attention_ref, qkv_ref,
            context_ref, scratch[0], scratch[1], grad_attention, grad_gains,
        )
        grad_rows = masked_rows(limit, grad_rows)
        grad_dense[:pixels] += tn(patches_ref[:rows], grad_rows.astype(BF16))
        if limit is None:
            grad_high[...] += grad_rows
        else:
            grad_low[...] += grad_rows

    return by_image(
        "first_backward",
        body,
        [resolution],
        [patches, start, qkv, context, middle, grad_hidden],
        [dense, attention, gains],
        [],
        [(dense.shape[0], width), (4 * width, width), (8, width), (ROWS_LO, width), (LEN, width)],
        [pltpu.VMEM((LEN, width), BF16), pltpu.VMEM((LEN, 3 * width), BF16)],
    )


def to_experts(values):
    return lax.all_to_all(values, "fsdp", split_axis=1, concat_axis=0, tiled=True)


def from_experts(values):
    return lax.all_to_all(values, "fsdp", split_axis=0, concat_axis=1, tiled=True)


def sum_rows(partial_value):
    return lax.psum_scatter(partial_value, "dp", scatter_dimension=0, tiled=True)


def expert_forward(received, win, wout):
    pre = matmul(received, win, "ned,edf->nef")
    hidden = jax.nn.gelu(pre).astype(jnp.bfloat16)
    return matmul(hidden, wout, "nef,efd->ned")


def expert_backward(received, grad_out, win, wout):
    pre = matmul(received, win, "ned,edf->nef")
    hidden = jax.nn.gelu(pre).astype(jnp.bfloat16)
    grad_hidden = matmul(grad_out, wout, "ned,efd->nef")
    _, pull = jax.vjp(jax.nn.gelu, pre)
    grad_pre = pull(grad_hidden)[0].astype(jnp.bfloat16)
    grad_wout = matmul(hidden, grad_out, "nef,ned->efd")
    grad_win = matmul(received, grad_pre, "ned,nef->edf")
    grad_slots = matmul(grad_pre, win, "nef,edf->ned")
    return (grad_slots, grad_win, grad_wout)


def fetch_layer(attention_t, router_t):
    part, width = attention_t.shape
    part_cols, part_rows = router_t.shape
    flat = router_t.reshape(-1)
    pack = jnp.concatenate(
        [attention_t, jnp.pad(flat, (0, -flat.size % width)).reshape(-1, width)], 0
    )
    both = lax.all_gather(pack, ("dp", "fsdp"), axis=0)
    rows_dp = lax.axis_size("dp")
    cols_fsdp = lax.axis_size("fsdp")
    router = (
        both[:, part:]
        .reshape(rows_dp * cols_fsdp, -1)[:, : flat.size]
        .reshape(rows_dp, cols_fsdp, part_cols, part_rows)
        .transpose(1, 2, 0, 3)
        .reshape(cols_fsdp * part_cols, rows_dp * part_rows)
    )
    return both[:, :part].reshape(-1, width), router


def share_layer(grad_attention, grad_router, part_cols, part_rows):
    rows_dp = lax.axis_size("dp")
    cols_fsdp = lax.axis_size("fsdp")
    devices = rows_dp * cols_fsdp
    width = grad_attention.shape[1]
    router = (
        grad_router.reshape(cols_fsdp, part_cols, rows_dp, part_rows)
        .transpose(2, 0, 1, 3)
        .reshape(devices, -1)
    )
    router = jnp.pad(router, ((0, 0), (0, -part_cols * part_rows % width)))
    router = router.reshape(devices, -1, width)
    pack = jnp.concatenate([grad_attention.reshape(devices, -1, width), router], 1)
    mine = lax.psum_scatter(pack, ("dp", "fsdp"), scatter_dimension=0, tiled=False)
    part = grad_attention.shape[0] // devices
    return mine[:part], mine[part:].reshape(-1)[: part_cols * part_rows].reshape(part_cols, part_rows)


def adam(weight, first, second, grad, rate):
    first = BETA_ONE * first + (1.0 - BETA_ONE) * grad
    second = BETA_TWO * second + (1.0 - BETA_TWO) * grad * grad
    ratio = first / (1.0 - BETA_ONE**STEP) / (jnp.sqrt(second / (1.0 - BETA_TWO**STEP)) + ADAM_EPS)
    return (weight - rate * (ratio + WEIGHT_DECAY * weight), first, second)


def on_device(
    patches,
    resolution,
    labels,
    dense_weights,
    attention,
    router,
    expert_in,
    expert_out,
    classifier,
    norm_table,
    dense_weights_first,
    dense_weights_second,
    attention_first,
    attention_second,
    router_first,
    router_second,
    expert_in_first,
    expert_in_second,
    expert_out_first,
    expert_out_second,
    classifier_first,
    classifier_second,
    norm_table_first,
    norm_table_second,
):
    layers = attention.shape[0]
    width = norm_table.shape[1]
    classes = classifier.shape[1]
    devices = lax.axis_size("dp") * lax.axis_size("fsdp")
    images = patches.shape[0] * devices
    interp = interp_matrix()
    position = norm_table[:LEN_LO]
    pos_high = jnp.dot(interp, position, precision=PRECISE)
    pos_low = jnp.pad(position, ((0, LEN - LEN_LO), (0, 0)))
    positions = jnp.stack([pos_low, pos_high])
    gains = [
        jnp.pad(norm_table[LEN_LO + 4 * layer : LEN_LO + 4 * layer + 4], ((0, 4), (0, 0)))
        for layer in range(layers)
    ]
    last_gains = jnp.pad(norm_table[LEN_LO + 4 * layers :], ((0, 6), (0, 0)))
    attention_t = attention.transpose(0, 2, 1).astype(BF16)
    router_t = router.transpose(0, 2, 1).astype(BF16)
    dense = lax.all_gather(dense_weights.T.astype(BF16), ("dp", "fsdp"), axis=0, tiled=True)
    attention_all = [
        lax.all_gather(attention_t[0], ("dp", "fsdp"), axis=0, tiled=True)
    ]
    router_all = [None]
    for layer in range(1, layers):
        one, two = fetch_layer(attention_t[layer], router_t[layer - 1])
        attention_all.append(one)
        router_all.append(two)

    start, qkv, context, middle, hidden = first_forward(
        resolution, patches, dense, attention_all[0], positions, gains[0], width
    )
    kept = [(start, qkv, context, middle)]
    mixing = None
    for layer in range(1, layers):
        outs = sparse_forward(
            resolution, hidden, mixing, attention_all[layer], router_all[layer], gains[layer]
        )
        if mixing is not None:
            hidden = outs[0]
        qkv, context, middle, combine, slots = outs[-5:]
        received = to_experts(slots)
        rows_all = lax.all_gather(received, "dp", axis=0, tiled=True)
        produced = sum_rows(
            expert_forward(
                rows_all, expert_in[layer - 1].astype(BF16), expert_out[layer - 1].astype(BF16)
            )
        ).astype(BF16)
        returned = from_experts(produced)
        kept.append((hidden, qkv, context, middle, combine, returned, received))
        hidden = middle
        mixing = (combine, returned)

    padding = -classes % 128
    head = jnp.pad(classifier[:width].astype(BF16), ((0, 0), (0, padding)))
    head_bias = jnp.pad(classifier[width:], ((0, 0), (0, padding)), constant_values=NEG_FILL)
    grad_hidden, grad_returned, grad_head, grad_bias, grad_last, loss_part = top(
        resolution, labels, middle, combine, returned, head, head_bias, last_gains, classes, images
    )
    grad_head = jnp.concatenate([grad_head[:, :classes], grad_bias[0:1, :classes]], 0)
    attention_grads = [None] * layers
    router_grads = [None] * (layers - 1)
    win_grads = [None] * (layers - 1)
    wout_grads = [None] * (layers - 1)
    gain_grads = [None] * layers
    for layer in reversed(range(1, layers)):
        before, qkv, context, middle, combine, returned, received = kept[layer]
        grad_received = to_experts(grad_returned)
        rows_all = lax.all_gather(received, "dp", axis=0, tiled=True)
        grads_all = lax.all_gather(grad_received, "dp", axis=0, tiled=True)
        grad_part, grad_win, grad_wout = expert_backward(
            rows_all, grads_all, expert_in[layer - 1].astype(BF16), expert_out[layer - 1].astype(BF16)
        )
        grad_home = from_experts(sum_rows(grad_part).astype(BF16))
        below = kept[layer - 1][4] if layer > 1 else None
        outs = sparse_backward(
            resolution, before, qkv, context, middle, grad_hidden, returned, grad_home, below,
            attention_all[layer], router_all[layer], gains[layer],
        )
        grad_hidden = outs[0]
        if below is not None:
            grad_returned = outs[1]
        grad_attention, grad_router, grad_gain = outs[-3:]
        attention_grads[layer], router_grads[layer - 1] = share_layer(
            grad_attention, grad_router, router.shape[2], router.shape[1]
        )
        win_grads[layer - 1] = grad_win
        wout_grads[layer - 1] = grad_wout
        gain_grads[layer] = grad_gain[:4]
    start, qkv, context, middle = kept[0]
    grad_dense, grad_attention, grad_gain, grad_low, grad_high = first_backward(
        resolution, patches, start, qkv, context, middle, grad_hidden, dense, attention_all[0],
        gains[0],
    )
    gain_grads[0] = grad_gain[:4]
    grad_first = lax.psum_scatter(grad_dense, ("dp", "fsdp"), scatter_dimension=0, tiled=True).T
    attention_grads[0] = lax.psum_scatter(
        grad_attention, ("dp", "fsdp"), scatter_dimension=0, tiled=True
    )
    grad_pos = grad_low[:LEN_LO] + jnp.dot(interp.T, grad_high, precision=PRECISE)
    grad_table = jnp.concatenate([grad_pos] + gain_grads + [grad_last[:2]], 0)
    grad_attention = jnp.stack(attention_grads).transpose(0, 2, 1)
    grad_router_all = jnp.stack(router_grads).transpose(0, 2, 1)
    grad_expert_in = jnp.stack(win_grads)
    grad_expert_out = jnp.stack(wout_grads)
    local_squares = (
        jnp.sum(grad_first * grad_first)
        + jnp.sum(grad_attention * grad_attention)
        + jnp.sum(grad_router_all * grad_router_all)
        + jnp.sum(grad_expert_in * grad_expert_in)
        + jnp.sum(grad_expert_out * grad_expert_out)
    )
    shared_head, shared_table, loss_total, squares = lax.psum(
        (grad_head, grad_table, loss_part[0, 0], local_squares), ("dp", "fsdp")
    )
    norm = jnp.sqrt(
        squares + jnp.sum(shared_head * shared_head) + jnp.sum(shared_table * shared_table)
    )
    scale = jnp.minimum(1.0, CLIP_NORM / norm)
    updates = (
        adam(dense_weights, dense_weights_first, dense_weights_second, grad_first * scale, LEARN_RATE),
        adam(attention, attention_first, attention_second, grad_attention * scale, ATTENTION_RATE),
        adam(router, router_first, router_second, grad_router_all * scale, LEARN_RATE),
        adam(expert_in, expert_in_first, expert_in_second, grad_expert_in * scale, EXPERT_RATE),
        adam(expert_out, expert_out_first, expert_out_second, grad_expert_out * scale, LEARN_RATE),
        adam(classifier, classifier_first, classifier_second, shared_head * scale, LEARN_RATE),
        adam(norm_table, norm_table_first, norm_table_second, shared_table * scale, TABLE_RATE),
    )
    return (loss_total, norm) + tuple(part for update in updates for part in update)


def solution(mesh):
    spread = P(("dp", "fsdp"))
    weights = (
        P(None, ("dp", "fsdp")),
        P(None, None, ("dp", "fsdp")),
        P(None, "dp", "fsdp"),
        P(None, "fsdp", None, "dp"),
        P(None, "fsdp", "dp", None),
        P(),
        P(),
    )
    moments = tuple(spec for spec in weights for _ in range(2))
    triples = tuple(spec for spec in weights for _ in range(3))
    return jax.shard_map(
        on_device,
        mesh=mesh,
        in_specs=(spread, spread, spread) + weights + moments,
        out_specs=(P(), P()) + triples,
        check_vma=False,
    )
```

time: 2460 us -> 1290 us (0.52)
  matrix products: 942 us -> 54.6 us
  local copies, waits for them, and re-layouts: 413 us -> 47.2 us
  waiting for transfers between devices: 279 us -> 641 us
  other arithmetic: 492 us -> 164 us
  Pallas kernels: 0 us -> 170 us
  blocking collectives: 252 us -> 141 us
    dot_general x197 -> x12, matrix products: 736 us -> 52.2 us  [matmul(): return jnp.einsum(form, left, right, preferred_element_type=jnp.float32)]
    sub x24 -> x0, matrix products: 201 us -> none  [attend(): probs = jax.nn.softmax(scores, axis=-1)]
    split x96 -> x0, local copies, waits for them, and re-layouts: 170 us -> none  [attend(): jnp.split(mixed, 3, axis=1)]
    pallas_call x0 -> x7, Pallas kernels: none -> 170 us  [by_image(): pl.pallas_call(kernel, grid_spec=pltpu.PrefetchScalarGridSpec(num_scalar_...]
    all_gather x4, waiting for transfers between devices: 55.3 us -> 215 us  [the longest x2 101 us: fetch_layer(): both = lax.all_gather(pack, ('dp', 'fsdp'), axis=0)]
    all_gather x4 -> x2, blocking collectives: 156 us -> 5.6 us  [on_device(): grads_all = lax.all_gather(grad_received, 'dp', axis=0, tiled=True)]
    convert_element_type x17 -> x5, other arithmetic: 119 us -> 5.6 us  [the longest x2 2.35 us: on_device(): grad_home = from_experts(sum_rows(grad_part).astype(BF16))]
    reduce_sum x77 -> x0, other arithmetic: 111 us -> none  [the longest x39 48.1 us: layer_norm(): center = values - jnp.mean(values, -1, keepdims=True)]
  transfers between devices with their start and end apart: 17 -> 15, of which waited for: 8 -> 13; matrix products, arithmetic and copies ran while one was open for 37% -> 8% of each run, Pallas kernels for 0% -> 0%
where the time goes in v1:
time: 1290 us; the launch traced here: 1280 us
  waiting for transfers between devices  641 us (50%)
  Pallas kernels  170 us (13%)
  other arithmetic  164 us (13%)
  blocking collectives  141 us (11%)
  matrix products  54.6 us (4%)
  local copies, waits for them, and re-layouts  47.2 us (4%)
  starting transfers between devices  40.5 us (3%)
  between operations  21.2 us (2%)
    unnamed x13, waiting for transfers between devices  277 us
    pallas_call x7, Pallas kernels, by_image(): pl.pallas_call(kernel, grid_spec=pltpu.PrefetchScalarGridSpec(num_scalar_...  170 us
    reduce_scatter x1, waiting for transfers between devices, on_device(): lax.psum_scatter(grad_attention, ('dp', 'fsdp'), scatter_dimension=0, til...  102 us
    all_gather x2, waiting for transfers between devices, fetch_layer(): both = lax.all_gather(pack, ('dp', 'fsdp'), axis=0)  101 us
    sub x7, other arithmetic, adam(): return (weight - rate * (ratio + WEIGHT_DECAY * weight), first, second)  93.9 us
    all_to_all x3, blocking collectives, to_experts(): lax.all_to_all(values, 'fsdp', split_axis=1, concat_axis=0, tiled=True)  70.8 us
    all_gather x1, waiting for transfers between devices, on_device(): lax.all_gather(dense_weights.T.astype(BF16), ('dp', 'fsdp'), axis=0, tile...  61.2 us
    dot_general x12, matrix products, matmul(): return jnp.einsum(form, left, right, preferred_element_type=jnp.float32)  52.2 us
  transfers between devices with their start and end apart: 15, of which 13 were waited for; matrix products, arithmetic and copies ran while one was open for 8% of the time, Pallas kernels for 0%

profile of v1, /device:TPU:0, one launch (start us, length us, event | category | flops | bytes accessed | tf_op | source)
XLA Modules:
  0.0 1280.1 jit_solution(12548123960359560310)
XLA Ops:
  17.8 51.0 %all-gather.14.cloned.1.call-done = bf16[32,52,384]{2,1,0:T(8,128)(2,1)} async-done(((bf16[1,52,384]{2,1,0:T(8,128)(2,1)}), bf16[32,52,384]{2,1,0:T(8,128)(2,1)}) %all-gather.14.cloned.1.call-update) | async-done | bytes 1277968 | tf_op jit(solution)/shard_map/all_gather | solution.py:555
  73.1 52.2 %all-gather.12.cloned.1.call-done = bf16[1,1536,384]{2,1,0:T(8,128)(2,1)} async-done(((bf16[1,48,384]{2,1,0:T(8,128)(2,1)}), bf16[1,1536,384]{2,1,0:T(8,128)(2,1)}) %all-gather.12.cloned.1.call-update) | async-done | bytes 1179664 | tf_op jit(solution)/shard_map/all_gather | solution.py:638
  125.3 61.2 %all-gather.10.cloned.1.call-done.refs_2_.refs_7_ = bf16[3840,384]{1,0:T(8,128)(2,1)} async-done(((bf16[120,384]{1,0:T(8,128)(2,1)}), bf16[3840,384]{1,0:T(8,128)(2,1)}) %all-gather.10.cloned.1.call-update) | async-done | bytes 2949136 | tf_op jit(solution)/shard_map/all_gather | solution.py:636
  186.5 25.8 %first_forward.1 = (f32[4,576,384]{2,1,0:T(8,128)}, bf16[4,576,1152]{2,1,0:T(8,128)(2,1)}, bf16[4,576,384]{2,1,0:T(8,128)(2,1)}, f32[4,576,384]{2,1,0:T(8,128)}, f32[4,576,384]{2,1,0:T(8,128)}) custom-call(s32[4]{0:T(128)} %refs_0_.13, bf16[4,576,768]{2,1,0:T(8,128)(2,1)} %refs_1_.5, bf16[3840,384]{1,0:T(8,128)(2,1)} %all-gather.10.cloned.1.call-done.refs_2_.refs_7_, ...), custom_call_target="tpu_custom_call" | custom-call | tf_op jit(solution)/shard_map/first_forward/pallas_call | solution.py:287
  212.3 18.9 %sparse_forward.2 = (bf16[4,576,1152]{2,1,0:T(8,128)(2,1)}, bf16[4,576,384]{2,1,0:T(8,128)(2,1)}, f32[4,576,384]{2,1,0:T(8,128)}, bf16[4,576,128]{2,1,0:T(8,128)(2,1)}, bf16[4,128,384]{2,1,0:T(8,128)(2,1)}) custom-call(s32[4]{0:T(128)} %refs_0_.13, f32[4,576,384]{2,1,0:T(8,128)} %get-tuple-element.59.refs_1_, bf16[1536,384]{1,0:T(8,128)(2,1)} %bitcast.232, ...), custom_call_target="tpu_custom_call" | custom-call | tf_op jit(solution)/shard_map/sparse_forward/pallas_call | solution.py:287
  233.3 19.6 %all-to-all-start = ((bf16[4,128,384]{2,0,1:T(4,128)(2,1)}), bf16[4,128,384]{2,0,1:T(4,128)(2,1)S(1)}, u32[]{:S(2)}, u32[]{:S(2)}) async-start(bf16[4,128,384]{2,0,1:T(4,128)(2,1)} %copy.76), calls=%async_computation | async-start | bytes 786432 | tf_op jit(solution)/shard_map/all_to_all | solution.py:519
  303.7 50.3 %all-gather.16.cloned.1.call-done = bf16[32,52,384]{2,1,0:T(8,128)(2,1)} async-done(((bf16[1,52,384]{2,1,0:T(8,128)(2,1)}), bf16[32,52,384]{2,1,0:T(8,128)(2,1)}) %all-gather.16.cloned.1.call-update) | async-done | bytes 1277968 | tf_op jit(solution)/shard_map/all_gather | solution.py:555
  359.2 20.1 %sparse_forward.3 = (f32[4,576,384]{2,1,0:T(8,128)}, bf16[4,576,1152]{2,1,0:T(8,128)(2,1)}, bf16[4,576,384]{2,1,0:T(8,128)(2,1)}, f32[4,576,384]{2,1,0:T(8,128)}...) custom-call(s32[4]{0:T(128)} %refs_0_.13, f32[4,576,384]{2,1,0:T(8,128)} %get-tuple-element.60.refs_1_.refs_4_, ...), custom_call_target="tpu_custom_call" | custom-call | tf_op jit(solution)/shard_map/sparse_forward/pallas_call | solution.py:287
  380.7 23.0 %all_to_all.144 = bf16[4,128,384]{2,0,1:T(4,128)(2,1)S(1)} all-to-all(bf16[4,128,384]{2,0,1:T(4,128)(2,1)S(1)} %copy.81), channel_id=1, replica_groups=mesh['dp'=2,'fsdp'=16] {'fsdp'}, dimensions={1} | all-to-all | bytes 786432 | tf_op jit(solution)/shard_map/all_to_all | solution.py:519
  447.6 10.8 top.1
  459.7 15.7 %all_to_all.145 = bf16[4,128,384]{2,0,1:T(4,128)(2,1)S(1)} all-to-all(bf16[4,128,384]{2,0,1:T(4,128)(2,1)S(1)} %copy.85), channel_id=1, replica_groups=mesh['dp'=2,'fsdp'=16] {'fsdp'}, dimensions={1} | all-to-all | bytes 786432 | tf_op jit(solution)/shard_map/all_to_all | solution.py:519
  496.8 19.6 %all_to_all.146 = bf16[64,8,384]{2,1,0:T(8,128)(2,1)S(1)} all-to-all(bf16[64,8,384]{2,1,0:T(8,128)(2,1)S(1)} %copy.87), channel_id=1, replica_groups=mesh['dp'=2,'fsdp'=16] {'fsdp'}, dimensions={0} | all-to-all | bytes 786432 | tf_op jit(solution)/shard_map/all_to_all | solution.py:523
  517.2 26.1 %sparse_backward.2 = (f32[4,576,384]{2,1,0:T(8,128)}, bf16[4,128,384]{2,1,0:T(8,128)(2,1)}, f32[1536,384]{1,0:T(8,128)}, f32[128,384]{1,0:T(8,128)}, f32[8,384]{1,0:T(8,128)}) custom-call(s32[4]{0:T(128)} %refs_0_.13, f32[4,576,384]{2,1,0:T(8,128)} %get-tuple-element.73.refs_1_, bf16[4,576,1152]{2,1,0:T(8,128)(2,1)} %get-tuple-element.74.refs_2_, ...), custom_call_target="tpu_custom_call" | custom-call | tf_op jit(solution)/shard_map/sparse_backward/pallas_call | solution.py:287
  544.6 32.2 %all_to_all.147 = bf16[4,128,384]{2,0,1:T(4,128)(2,1)S(1)} all-to-all(bf16[4,128,384]{2,0,1:T(4,128)(2,1)S(1)} %copy.89), channel_id=1, replica_groups=mesh['dp'=2,'fsdp'=16] {'fsdp'}, dimensions={1} | all-to-all | bytes 786432 | tf_op jit(solution)/shard_map/all_to_all | solution.py:519
  619.8 25.3 %sparse_backward.3 = (f32[4,576,384]{2,1,0:T(8,128)}, f32[1536,384]{1,0:T(8,128)}, f32[128,384]{1,0:T(8,128)}, f32[8,384]{1,0:T(8,128)}) custom-call(s32[4]{0:T(128)} %refs_0_.13, f32[4,576,384]{2,1,0:T(8,128)} %get-tuple-element.59.refs_1_, bf16[4,576,1152]{2,1,0:T(8,128)(2,1)} %get-tuple-element.71.refs_2_, ...), custom_call_target="tpu_custom_call" | custom-call | tf_op jit(solution)/shard_map/sparse_backward/pallas_call | solution.py:287
  646.5 43.0 %first_backward.1 = (f32[3840,384]{1,0:T(8,128)}, f32[1536,384]{1,0:T(8,128)}, f32[8,384]{1,0:T(8,128)}, f32[208,384]{1,0:T(8,128)}, f32[576,384]{1,0:T(8,128)}) custom-call(s32[4]{0:T(128)} %refs_0_.13, bf16[4,576,768]{2,1,0:T(8,128)(2,1)} %refs_1_.5, f32[4,576,384]{2,1,0:T(8,128)} %get-tuple-element.67.refs_2_, ...), custom_call_target="tpu_custom_call" | custom-call | tf_op jit(solution)/shard_map/first_backward/pallas_call | solution.py:287
  721.7 11.8 multiply_reduce_fusion.1
  733.5 11.9 multiply_reduce_fusion
  745.4 162.3 %all-reduce.14.cloned.1.call-done = (f32[32,52,384]{2,1,0:T(8,128)}, f32[32,52,384]{2,1,0:T(8,128)}, f32[385,1000]{1,0:T(8,128)}, f32[210,384]{1,0:T(8,128)}) async-done(((f32[32,52,384]{2,1,0:T(8,128)}, f32[32,52,384]{2,1,0:T(8,128)}, f32[385,1000]{1,0:T(8,128)}, f32[210,384]{1,0:T(8,128)}), (f32[32,52,384]{2,1,0:T(8,128)}, f32[32,52,384]{2,1,0:T(8,128)}, f32[385,1000]{1,0:T(8,128)}, ...) | async-done | bytes 6974384
  909.5 102.3 %reduce-scatter.17.cloned.1.call-done = f32[48,384]{1,0:T(8,128)} async-done(((f32[1536,384]{1,0:T(8,128)}), f32[48,384]{1,0:T(8,128)}) %reduce-scatter.17.cloned.1.call-update) | async-done | bytes 73744 | tf_op jit(solution)/shard_map/reduce_scatter | solution.py:713
  1018.2 112.6 %reduce-scatter.19.cloned.1.call-done = f32[120,384]{1,0:T(8,128)} async-done(((f32[3840,384]{1,0:T(8,128)}), f32[120,384]{1,0:T(8,128)}) %reduce-scatter.19.cloned.1.call-update) | async-done | bytes 184336
  1135.6 40.5 %all-reduce.10 = (f32[]{:T(128)}, f32[]{:T(128)}) all-reduce(f32[]{:T(128)} %bitcast.32, f32[]{:T(128)S(6)} %add.193), channel_id=1, replica_groups=mesh['dp'=2,'fsdp'=16] {'dp','fsdp'}, use_global_device_ids=true, to_apply=%region_2.3 | all-reduce | flops 2 | bytes 16 | tf_op jit(solution)/shard_map/psum | solution.py:729
  1180.6 43.9 %add_subtract_fusion = (f32[2,8,384,768]{3,2,1,0:T(8,128)}, f32[2,8,384,768]{3,2,1,0:T(8,128)}, f32[2,8,384,768]{3,2,1,0:T(8,128)}) fusion(f32[2,8,384,768]{3,2,1,0:T(8,128)} %param.30, f32[]{:T(128)S(6)} %min.3, f32[1,8,384,768]{3,2,1,0:T(8,128)} %convolution_bitcast_fusion.2, f32[1,8,384,768]{3,2,1,0:T(8,128)} %convolution_bitcast_fusion.3, ...), kind=kLoop, calls=%fused_computation.8 | loop fusion | flops 75497472 | bytes 132120576 | tf_op jit(solution)/shard_map/sub | solution.py:590
  1224.6 39.9 %multiply_subtract_fusion = (f32[2,8,768,384]{3,2,1,0:T(8,128)}, f32[2,8,768,384]{3,2,1,0:T(8,128)}, f32[2,8,768,384]{3,2,1,0:T(8,128)}) fusion(f32[2,8,768,384]{3,2,1,0:T(8,128)} %param.31, f32[]{:T(128)S(6)} %min.3, f32[1,8,768,384]{3,2,1,0:T(8,128)S(1)} %bitcast.227, f32[1,8,768,384]{3,2,1,0:T(8,128)} %convolution_bitcast_fusion.1, ...), kind=kLoop, calls=%fused_computation.6 | loop fusion | flops 80216064 | bytes 132120576 | tf_op jit(solution)/shard_map/sub | solution.py:590
  (247 shorter events, 238.8 us)
Async XLA Ops:
  7.2 61.6 %all-gather.14.cloned.1.call-start = ((), (), s32[]{:S(2)}) async-start(), calls=%async_computation.21 | async-start | bytes 1419264 | tf_op jit(solution)/shard_map/all_gather | solution.py:555
  10.3 115.0 %all-gather.12.cloned.1.call-start = ((), (), s32[]{:S(2)}) async-start(), calls=%async_computation.20 | async-start | bytes 1216512 | tf_op jit(solution)/shard_map/all_gather | solution.py:638
  11.1 175.5 %all-gather.10.cloned.1.call-start = ((), (), s32[]{:S(2)}) async-start(), calls=%async_computation.14 | async-start | bytes 3041280 | tf_op jit(solution)/shard_map/all_gather | solution.py:636
  233.3 39.2 %all-to-all-start = ((bf16[4,128,384]{2,0,1:T(4,128)(2,1)}), bf16[4,128,384]{2,0,1:T(4,128)(2,1)S(1)}, u32[]{:S(2)}, u32[]{:S(2)}) async-start(bf16[4,128,384]{2,0,1:T(4,128)(2,1)} %copy.76), calls=%async_computation | async-start | bytes 786432 | tf_op jit(solution)/shard_map/all_to_all | solution.py:519
  252.8 41.2 %reduce-scatter.9.cloned.1.call-start = ((), (), s32[]{:S(2)}) async-start(), calls=%async_computation.15 | async-start | bytes 2359296 | tf_op jit(solution)/shard_map/reduce_scatter | solution.py:527
  283.6 70.5 %all-gather.16.cloned.1.call-start = ((), (), s32[]{:S(2)}) async-start(), calls=%async_computation.22 | async-start | bytes 1419264 | tf_op jit(solution)/shard_map/all_gather | solution.py:555
  296.2 62.2 %all-to-all-start.1 = ((bf16[64,8,384]{2,1,0:T(8,128)(2,1)}), bf16[64,8,384]{2,1,0:T(8,128)(2,1)S(1)}, u32[]{:S(2)}, u32[]{:S(2)}) async-start(bf16[64,8,384]{2,1,0:T(8,128)(2,1)} %copy.78), calls=%async_computation.2 | async-start | bytes 786432 | tf_op jit(solution)/shard_map/all_to_all | solution.py:523
  303.1 120.6 %reduce-scatter.11.cloned.1.call-start = ((), (), s32[]{:S(2)}) async-start(), calls=%async_computation.16 | async-start | bytes 2359296 | tf_op jit(solution)/shard_map/reduce_scatter | solution.py:527
  410.5 68.6 %copy-start.2 = (f32[8,128,768]{2,1,0:T(8,128)}, f32[8,128,768]{2,1,0:T(8,128)S(1)}, u32[]{:S(2)}) copy-start(f32[8,128,768]{2,1,0:T(8,128)S(1)} %fusion.7) | copy-start | bytes 9437188
  425.8 19.9 %all-to-all-start.3 = ((bf16[64,8,384]{2,1,0:T(8,128)(2,1)}), bf16[64,8,384]{2,1,0:T(8,128)(2,1)}, u32[]{:S(2)}, u32[]{:S(2)}) async-start(bf16[64,8,384]{2,1,0:T(8,128)(2,1)} %copy.83), calls=%async_computation.5 | async-start | bytes 786432 | tf_op jit(solution)/shard_map/all_to_all | solution.py:523
  432.7 62.7 %reduce-scatter.13.cloned.1.call-start = ((), (), s32[]{:S(2)}) async-start(), calls=%async_computation.17 | async-start | bytes 2359296 | tf_op jit(solution)/shard_map/reduce_scatter | solution.py:527
  488.1 108.9 %reduce-scatter.15.cloned.1.call-start = ((), (), s32[]{:S(2)}) async-start(), calls=%async_computation.18 | async-start | bytes 2359296 | tf_op jit(solution)/shard_map/reduce_scatter | solution.py:527
  599.2 19.9 %all-to-all-start.7 = ((bf16[64,8,384]{2,1,0:T(8,128)(2,1)}), bf16[64,8,384]{2,1,0:T(8,128)(2,1)S(1)}, u32[]{:S(2)}, u32[]{:S(2)}) async-start(bf16[64,8,384]{2,1,0:T(8,128)(2,1)} %copy.91), calls=%async_computation.11 | async-start | bytes 786432 | tf_op jit(solution)/shard_map/all_to_all | solution.py:523
  606.0 301.7 %all-reduce.14.cloned.1.call-start = ((), (), s32[]{:S(2)}) async-start(), calls=%async_computation.24 | async-start | bytes 14884864
  646.4 43.9 %copy-start.38 = (f32[8,384]{1,0:T(8,128)S(1)}, f32[8,384]{1,0:T(8,128)}, u32[]{:S(2)}) copy-start(f32[8,384]{1,0:T(8,128)} %get-tuple-element.92) | copy-start | bytes 36868
  698.4 313.5 %reduce-scatter.17.cloned.1.call-start = ((), (), s32[]{:S(2)}) async-start(), calls=%async_computation.19 | async-start | bytes 2433024 | tf_op jit(solution)/shard_map/reduce_scatter | solution.py:713
  699.0 431.8 %reduce-scatter.19.cloned.1.call-start = ((), (), s32[]{:S(2)}) async-start(), calls=%async_computation.23 | async-start | bytes 6082560
  733.5 444.7 %copy-start.23 = (f32[3,384,48]{1,2,0:T(8,128)S(1)}, f32[3,384,48]{1,2,0:T(8,128)}, u32[]{:S(2)}) copy-start(f32[3,384,48]{1,2,0:T(8,128)} %param.28) | copy-start | bytes 663556
  733.5 444.7 %copy-start.29 = (f32[3,384,48]{1,2,0:T(8,128)S(1)}, f32[3,384,48]{1,2,0:T(8,128)}, u32[]{:S(2)}) copy-start(f32[3,384,48]{1,2,0:T(8,128)} %param.36) | copy-start | bytes 663556
  733.5 444.7 %copy-start.30 = (f32[3,384,48]{1,2,0:T(8,128)S(1)}, f32[3,384,48]{1,2,0:T(8,128)}, u32[]{:S(2)}) copy-start(f32[3,384,48]{1,2,0:T(8,128)} %param.37) | copy-start | bytes 663556
  745.4 434.6 %copy-start.34 = (f32[2,192,8]{1,2,0:T(8,128)S(1)}, f32[2,192,8]{1,2,0:T(8,128)}, u32[]{:S(2)}) copy-start(f32[2,192,8]{1,2,0:T(8,128)} %param.29) | copy-start | bytes 36868
  745.4 434.6 %copy-start.35 = (f32[2,192,8]{1,2,0:T(8,128)S(1)}, f32[2,192,8]{1,2,0:T(8,128)}, u32[]{:S(2)}) copy-start(f32[2,192,8]{1,2,0:T(8,128)} %param.38) | copy-start | bytes 36868
  745.4 434.6 %copy-start.36 = (f32[2,192,8]{1,2,0:T(8,128)S(1)}, f32[2,192,8]{1,2,0:T(8,128)}, u32[]{:S(2)}) copy-start(f32[2,192,8]{1,2,0:T(8,128)} %param.39) | copy-start | bytes 36868
  1015.6 208.9 %slice-start = ((s8[9437184]{0:T(1024)(128)(4,1)}), s8[1048576]{0:T(1024)(128)(4,1)S(1)}, s32[]{:S(2)}) async-start(s8[9437184]{0:T(1024)(128)(4,1)} %bitcast.226), calls=%async_computation.25 | async-start | bytes 2097152
  (41 other events, 381.2 us)
Sparse Core Ops, SparseCore 0:
  11.4 57.2 all-gather.13
  72.2 53.0 all-gather.11
  128.7 57.7 all-gather.9
  283.7 10.3 reduce-scatter.8
  297.7 56.2 all-gather.15
  416.6 7.0 reduce-scatter.10
  488.2 7.0 reduce-scatter.12
  589.9 7.0 reduce-scatter.14
  698.5 209.1 all-reduce.13
  912.8 98.9 reduce-scatter.16
  1019.0 111.7 reduce-scatter.18

commit v2 on v1

--- a/solution.py
+++ b/solution.py
@@ -406,7 +406,7 @@
         grad_bias_row[0:1] += grad_logits
         row_mask = (row_number((8, padded)) == 0).astype(F32)
         grad_logits_b = (row_mask * grad_logits).astype(BF16)
-        grad_head[...] += tn(pooled_b, grad_logits_b)
+        grad_head[...] += tn(grad_logits_b, pooled_b)
         grad_pooled = nt(grad_logits_b, head_ref[...])[0:1] * (1.0 / length)
         grad_normed = masked_rows(limit, jnp.broadcast_to(grad_pooled, (rows, width)))
         grad_rows, grad_gain, grad_bias = normalise_back(
@@ -424,7 +424,7 @@
         [middle, combine, returned],
         [head, head_bias, last_gains],
         [((LEN, width), F32), ((experts, width), BF16)],
-        [(width, padded), (8, padded), (8, width), (8, 128)],
+        [(padded, width), (8, padded), (8, width), (8, 128)],
     )
 
 
@@ -523,26 +523,31 @@
     return lax.all_to_all(values, "fsdp", split_axis=0, concat_axis=1, tiled=True)
 
 
-def sum_rows(partial_value):
-    return lax.psum_scatter(partial_value, "dp", scatter_dimension=0, tiled=True)
-
-
-def expert_forward(received, win, wout):
-    pre = matmul(received, win, "ned,edf->nef")
-    hidden = jax.nn.gelu(pre).astype(jnp.bfloat16)
-    return matmul(hidden, wout, "nef,efd->ned")
-
-
-def expert_backward(received, grad_out, win, wout):
-    pre = matmul(received, win, "ned,edf->nef")
-    hidden = jax.nn.gelu(pre).astype(jnp.bfloat16)
-    grad_hidden = matmul(grad_out, wout, "ned,efd->nef")
-    _, pull = jax.vjp(jax.nn.gelu, pre)
-    grad_pre = pull(grad_hidden)[0].astype(jnp.bfloat16)
-    grad_wout = matmul(hidden, grad_out, "nef,ned->efd")
-    grad_win = matmul(received, grad_pre, "ned,nef->edf")
-    grad_slots = matmul(grad_pre, win, "nef,edf->ned")
-    return (grad_slots, grad_win, grad_wout)
+def all_rows(values):
+    return lax.all_gather(to_experts(values), "dp", axis=0, tiled=True).transpose(1, 0, 2)
+
+
+def rows_home(part):
+    shared = lax.psum_scatter(part.transpose(1, 0, 2), "dp", scatter_dimension=0, tiled=True)
+    return from_experts(shared.astype(BF16))
+
+
+def plain_exchange(layer, values, received, expert_in, expert_out):
+    win, wout = expert_in[layer].astype(BF16), expert_out[layer].astype(BF16)
+    rows = all_rows(values)
+    if received is None:
+        hid = gelu(matmul(rows, win, "end,edf->enf")).astype(BF16)
+        return rows_home(matmul(hid, wout, "enf,efd->end")), rows
+    hid, slope = gelu_both(matmul(received, win, "end,edf->enf"))
+    hid = hid.astype(BF16)
+    grad_pre = (matmul(rows, wout, "end,efd->enf") * slope).astype(BF16)
+    home = rows_home(matmul(grad_pre, win, "enf,edf->end"))
+
+    def gram(values):
+        return matmul(values, values, "enk,emk->enm")
+
+    squares = gram(received) * gram(grad_pre) + gram(hid) * gram(rows)
+    return home, hid, grad_pre, rows, jnp.sum(squares, (0, 1)).reshape(1, -1)
 
 
 def fetch_layer(attention_t, router_t):
@@ -581,6 +586,553 @@
     mine = lax.psum_scatter(pack, ("dp", "fsdp"), scatter_dimension=0, tiled=False)
     part = grad_attention.shape[0] // devices
     return mine[:part], mine[part:].reshape(-1)[: part_cols * part_rows].reshape(part_cols, part_rows)
+
+
+BITS = 4
+GATHER_ORDERS = ((3, 2, 0, 1), (0, 1, 2, 3), (0, 1, 3, 2))
+MESH_IDS = pl.DeviceIdType.MESH
+
+
+def my_bits():
+    at = lax.axis_index("fsdp")
+    return [(at // (1 << (BITS - 1 - bit))) % 2 for bit in range(BITS)]
+
+
+def partner_of(bit):
+    at = lax.axis_index("fsdp")
+    step = 1 << (BITS - 1 - bit)
+    return (lax.axis_index("dp"), at + step * (1 - 2 * ((at // step) % 2)))
+
+
+def sibling():
+    return (1 - lax.axis_index("dp"), lax.axis_index("fsdp"))
+
+
+def greet_partners():
+    barrier = pltpu.get_barrier_semaphore()
+    others = [partner_of(bit) for bit in range(BITS)] + [sibling()]
+    for other in others:
+        pl.semaphore_signal(barrier, inc=1, device_id=other, device_id_type=MESH_IDS)
+    pl.semaphore_wait(barrier, len(others))
+
+
+def send(source, target, send_sem, recv_sem, device):
+    copy = pltpu.make_async_remote_copy(
+        src_ref=source,
+        dst_ref=target,
+        send_sem=send_sem,
+        recv_sem=recv_sem,
+        device_id=device,
+        device_id_type=MESH_IDS,
+    )
+    copy.start()
+    return copy
+
+
+def spread(parts, sems):
+    mine = my_bits()
+    core = lax.axis_index("dp")
+    to_send, to_get, pass_send, pass_get = sems
+
+    def view(part, stage, other):
+        ref, lane_part, order = part
+        index = []
+        for bit in range(BITS):
+            if bit in order[:stage]:
+                index.append(slice(None))
+            elif other and bit == order[stage]:
+                index.append(1 - mine[bit])
+            else:
+                index.append(mine[bit])
+        return ref.at[(core, *index, slice(None), lane_part)]
+
+    def go(number, stage):
+        block = view(parts[number], stage, False)
+        return send(
+            block, block, to_send.at[number, stage], to_get.at[number, stage],
+            partner_of(parts[number][2][stage]),
+        )
+
+    def hand_over(number, slot, block):
+        return send(block, block, pass_send.at[number, slot], pass_get.at[number, slot], sibling())
+
+    going = [go(number, 0) for number in range(len(parts))]
+    handed = [
+        hand_over(number, BITS, view(parts[number], 0, False)) for number in range(len(parts))
+    ]
+    for stage in range(BITS):
+        for number in range(len(parts)):
+            going[number].wait()
+            if stage + 1 < BITS:
+                going[number] = go(number, stage + 1)
+            handed.append(hand_over(number, stage, view(parts[number], stage, True)))
+    for copy in handed:
+        copy.wait()
+
+
+def spread_sems(count):
+    return [pltpu.SemaphoreType.DMA((count, BITS + 1)) for _ in range(4)]
+
+
+def lane_parts(width):
+    return [slice(start, start + 128) for start in range(0, width, 128)]
+
+
+def gather_all(shards, collective_id):
+    count = len(shards)
+    width = shards[0].shape[1]
+    cuts = lane_parts(width)
+
+    def kernel(*refs):
+        ins, outs, sems = refs[:count], refs[count : 2 * count], refs[2 * count :]
+        place = (lax.axis_index("dp"), *my_bits())
+        for ref, out in zip(ins, outs):
+            out[place] = ref[...]
+        greet_partners()
+        spread(
+            [
+                (out, cut, GATHER_ORDERS[number % 3])
+                for number, cut in enumerate(cuts)
+                for out in outs
+            ],
+            sems,
+        )
+
+    outs = pl.pallas_call(
+        kernel,
+        in_specs=[pl.BlockSpec(memory_space=pltpu.VMEM)] * count,
+        out_specs=[pl.BlockSpec(memory_space=pltpu.VMEM)] * count,
+        out_shape=[jax.ShapeDtypeStruct((2,) * (BITS + 1) + s.shape, s.dtype) for s in shards],
+        scratch_shapes=spread_sems(count * len(cuts)),
+        compiler_params=pltpu.CompilerParams(
+            collective_id=collective_id, has_side_effects=True, vmem_limit_bytes=VMEM_BYTES
+        ),
+        name="gather_all",
+    )(*shards)
+    return [out.reshape(-1, width) for out in outs]
+
+
+def reduce_all(grads, stats, shared, collective_id):
+    _, rows, width = grads.shape
+    cuts = lane_parts(width)
+    parts = len(cuts)
+    orders = [tuple(reversed(GATHER_ORDERS[number % 3])) for number in range(parts)]
+
+    def kernel(grads_ref, stats_ref, mine_ref, shared_ref, total_ref, *scratch):
+        sums, first_get = scratch[:2]
+        gets = scratch[2 : 2 + BITS]
+        stats_all = scratch[2 + BITS]
+        local_sem, pair_send, pair_get, to_send, to_get = scratch[3 + BITS : 8 + BITS]
+        sems = scratch[8 + BITS :]
+        core = lax.axis_index("dp")
+        bits = my_bits()
+        local = [
+            pltpu.make_async_copy(
+                grads_ref.at[core, :, :, :, :, :, cut],
+                sums.at[:, :, :, :, :, cut],
+                local_sem.at[number],
+            )
+            for number, cut in enumerate(cuts)
+        ]
+        for copy in local:
+            copy.start()
+        greet_partners()
+        pairs = [
+            send(
+                grads_ref.at[1 - core, :, :, :, :, :, cut],
+                first_get.at[:, :, :, :, :, cut],
+                pair_send.at[number],
+                pair_get.at[number],
+                sibling(),
+            )
+            for number, cut in enumerate(cuts)
+        ]
+
+        def index(number, stage, own):
+            order = orders[number]
+            found = []
+            for bit in range(BITS):
+                if bit in order[:stage]:
+                    found.append(bits[bit])
+                elif bit == order[stage]:
+                    found.append(bits[bit] if own else 1 - bits[bit])
+                else:
+                    found.append(slice(None))
+            return (*found, slice(None), cuts[number])
+
+        def go(number, stage):
+            return send(
+                sums.at[index(number, stage, False)],
+                gets[stage].at[number],
+                to_send.at[number, stage],
+                to_get.at[number, stage],
+                partner_of(orders[number][stage]),
+            )
+
+        going = []
+        for number in range(parts):
+            local[number].wait()
+            pairs[number].wait()
+            whole = (slice(None),) * (BITS + 1) + (cuts[number],)
+            sums[whole] = sums[whole] + first_get[whole]
+            going.append(go(number, 0))
+        place = tuple(bits)
+        for stage in range(BITS):
+            for number in range(parts):
+                going[number].wait()
+                if stage + 1 < BITS:
+                    at = index(number, stage, True)
+                    sums[at] = sums[at] + gets[stage][number]
+                    going[number] = go(number, stage + 1)
+                else:
+                    at = index(number, stage, True)
+                    mine_ref[:, cuts[number]] = sums[at].astype(F32) + gets[stage][number].astype(F32)
+        mine = mine_ref[...]
+        squares = jnp.sum(jnp.sum(mine * mine, 0, keepdims=True), 1, keepdims=True)
+        top_row = (row_number((8, 128)) == 0).astype(F32)
+        stats_all[(core, *place)] = stats_ref[...] + top_row * squares
+        shared_ref[(core, *place)] = mine_ref[rows - shared :, :].astype(BF16)
+        spread(
+            [
+                (shared_ref, cut, GATHER_ORDERS[number % 3]) for number, cut in enumerate(cuts)
+            ]
+            + [(stats_all, slice(0, 128), GATHER_ORDERS[1])],
+            sems,
+        )
+        total_ref[...] = jnp.sum(stats_all[...].reshape(32, 8, 128), 0)
+
+    grid = (2,) * BITS
+    return pl.pallas_call(
+        kernel,
+        in_specs=[pl.BlockSpec(memory_space=pl.ANY), pl.BlockSpec(memory_space=pltpu.VMEM)],
+        out_specs=[pl.BlockSpec(memory_space=pltpu.VMEM)] * 3,
+        out_shape=[
+            jax.ShapeDtypeStruct((rows, width), F32),
+            jax.ShapeDtypeStruct((2,) + grid + (shared, width), BF16),
+            jax.ShapeDtypeStruct((8, 128), F32),
+        ],
+        scratch_shapes=[pltpu.VMEM(grid + (rows, width), BF16)] * 2
+        + [pltpu.VMEM((parts,) + (2,) * (BITS - 1 - stage) + (rows, 128), BF16) for stage in range(BITS)]
+        + [pltpu.VMEM((2,) + grid + (8, 128), F32)]
+        + [pltpu.SemaphoreType.DMA((parts,))] * 3
+        + [pltpu.SemaphoreType.DMA((parts, BITS))] * 2
+        + spread_sems(parts + 1),
+        compiler_params=pltpu.CompilerParams(
+            collective_id=collective_id, has_side_effects=True, vmem_limit_bytes=VMEM_BYTES
+        ),
+        name="reduce_all",
+    )(grads.reshape((2,) + grid + (rows, width)), stats)
+
+
+def chip(at):
+    return (lax.axis_index("dp"), at)
+
+
+def greet_all(chips):
+    barrier = pltpu.get_barrier_semaphore()
+    me = lax.axis_index("fsdp")
+
+    def one(step, carry):
+        pl.semaphore_signal(
+            barrier, inc=1, device_id=chip((me + step) % chips), device_id_type=MESH_IDS
+        )
+        return carry
+
+    lax.fori_loop(1, chips, one, 0)
+    pl.semaphore_signal(barrier, inc=1, device_id=sibling(), device_id_type=MESH_IDS)
+    pl.semaphore_wait(barrier, chips)
+
+
+def swap_start(chips, source, target, send_sem, get_sem):
+    me = lax.axis_index("fsdp")
+
+    def one(step, carry):
+        other = (me + step) % chips
+        send(source.at[other], target.at[me], send_sem.at[other], get_sem.at[me], chip(other))
+        return carry
+
+    lax.fori_loop(1, chips, one, 0)
+
+
+def swap_sent(chips, step, source, target, send_sem, get_sem):
+    me = lax.axis_index("fsdp")
+    to = (me + step) % chips
+    pltpu.make_async_remote_copy(
+        src_ref=source.at[to], dst_ref=target.at[me], send_sem=send_sem.at[to],
+        recv_sem=get_sem.at[me], device_id=chip(to), device_id_type=MESH_IDS,
+    ).wait_send()
+
+
+def swap_arrived(chips, step, source, target, send_sem, get_sem):
+    origin = (lax.axis_index("fsdp") + chips - step) % chips
+    pltpu.make_async_remote_copy(
+        src_ref=source.at[origin], dst_ref=target.at[origin], send_sem=send_sem.at[origin],
+        recv_sem=get_sem.at[origin], device_id=chip(origin), device_id_type=MESH_IDS,
+    ).wait_recv()
+    return origin
+
+
+def exchange(layer, values, received, expert_in, expert_out, collective_id):
+    images, experts, width = values.shape
+    chips = lax.axis_size("fsdp")
+    cores = lax.axis_size("dp")
+    local, _, hidden = expert_in.shape[1:]
+    rows = images * local
+    half = chips * images
+    every = cores * half
+    backward = received is not None
+
+    def kernel(*refs):
+        if backward:
+            values_ref, received_ref, in_ref, out_ref = refs[:4]
+            home_ref, hid_ref, pre_ref, gout_ref, squares_ref = refs[4:9]
+            slope_ref = refs[9]
+            scratch = refs[10:]
+        else:
+            values_ref, in_ref, out_ref = refs[:3]
+            home_ref, received_ref = refs[3:5]
+            scratch = refs[5:]
+        win, wout, outbox, inbox, parts, pair_out, pair_in, sorted_ref, backbox, homebox = scratch[:10]
+        win_sem, wout_sem, send_one, get_one, pass_send, pass_get, pair_send, pair_get, send_two, get_two = scratch[10:]
+        core = lax.axis_index("dp")
+        me = lax.axis_index("fsdp")
+
+        def fetch(e):
+            return (
+                pltpu.make_async_copy(in_ref.at[layer, e], win.at[e], win_sem.at[e]),
+                pltpu.make_async_copy(out_ref.at[layer, e], wout.at[e], wout_sem.at[e]),
+            )
+
+        def start_fetch(e, carry):
+            for copy in fetch(e):
+                copy.start()
+            return carry
+
+        lax.fori_loop(0, local, start_fetch, 0)
+        whole = [values_ref[image].astype(F32) for image in range(images)]
+        for at in range(chips):
+            outbox[at] = jnp.concatenate(
+                [one[at * local : (at + 1) * local] for one in whole], 0
+            ).astype(BF16)
+        greet_all(chips)
+        swap_start(chips, outbox, inbox.at[core], send_one, get_one)
+        inbox[core, me] = outbox[me]
+
+        def hand(at):
+            block = inbox.at[core, at]
+            return pltpu.make_async_remote_copy(
+                src_ref=block, dst_ref=block, send_sem=pass_send.at[at],
+                recv_sem=pass_get.at[at], device_id=sibling(), device_id_type=MESH_IDS,
+            )
+
+        def handed(at):
+            block = inbox.at[1 - core, at]
+            return pltpu.make_async_remote_copy(
+                src_ref=block, dst_ref=block, send_sem=pass_send.at[at],
+                recv_sem=pass_get.at[at], device_id=sibling(), device_id_type=MESH_IDS,
+            )
+
+        hand(me).start()
+        if backward:
+
+            def ahead(e, carry):
+                for copy in fetch(e):
+                    copy.wait()
+                rec = received_ref[e]
+                hid, slope = gelu_both(nn(rec, win[e].astype(BF16)))
+                slope_ref[e] = slope
+                hid_ref[e] = hid.astype(BF16)
+                return carry
+
+            lax.fori_loop(0, local, ahead, 0)
+
+        def arrive(step, carry):
+            hand(swap_arrived(chips, step, outbox, inbox.at[core], send_one, get_one)).start()
+            return carry
+
+        lax.fori_loop(1, chips, arrive, 0)
+
+        def all_handed(at, carry):
+            handed(at).wait_recv()
+            return carry
+
+        lax.fori_loop(0, chips, all_handed, 0)
+        arrived = inbox[...].reshape(every * local, width)
+        pick_row = lax.broadcasted_iota(jnp.int32, (every, every * local), 0)
+        pick_col = lax.broadcasted_iota(jnp.int32, (every, every * local), 1)
+        wanted = pick_row * local - pick_col
+
+        def pair_copy(e):
+            return pltpu.make_async_remote_copy(
+                src_ref=pair_out.at[e], dst_ref=pair_in.at[e], send_sem=pair_send.at[e],
+                recv_sem=pair_get.at[e], device_id=sibling(), device_id_type=MESH_IDS,
+            )
+
+        if backward:
+            squares_ref[...] = jnp.zeros_like(squares_ref)
+
+        def work(e, carry):
+            pick = (wanted == -e).astype(F32).astype(BF16)
+            mine = nn(pick, arrived).astype(BF16)
+            if backward:
+                gout_ref[e] = mine
+                grad_pre = (nt(mine, wout[e].astype(BF16)) * slope_ref[e]).astype(BF16)
+                pre_ref[e] = grad_pre
+                part = nt(grad_pre, win[e].astype(BF16))
+                rec, hid = received_ref[e], hid_ref[e]
+                product = nt(rec, rec) * nt(grad_pre, grad_pre) + nt(hid, hid) * nt(mine, mine)
+                squares_ref[...] += jnp.sum(product.reshape(every // 8, 8, every), 0)
+            else:
+                for copy in fetch(e):
+                    copy.wait()
+                received_ref[e] = mine
+                hid = gelu(nn(mine, win[e].astype(BF16))).astype(BF16)
+                part = nn(hid, wout[e].astype(BF16))
+            parts[e] = part.reshape(cores, half, width)
+            pair_out[e] = parts[e, 1 - core].astype(BF16)
+            pair_copy(e).start()
+            return carry
+
+        lax.fori_loop(0, local, work, 0)
+
+        def add(e, carry):
+            pair_copy(e).wait_recv()
+            sorted_ref[pl.ds(pl.multiple_of(e * half, half), half)] = (
+                parts[e, core] + pair_in[e].astype(F32)
+            ).astype(BF16)
+            return carry
+
+        lax.fori_loop(0, local, add, 0)
+        back_row = lax.broadcasted_iota(jnp.int32, (half * local, half * local), 0)
+        back_col = lax.broadcasted_iota(jnp.int32, (half * local, half * local), 1)
+        back = (back_row == (back_col % half) * local + back_col // half).astype(F32).astype(BF16)
+        backbox[...] = nn(back, sorted_ref[...]).astype(BF16).reshape(chips, rows, width)
+        swap_start(chips, backbox, homebox, send_two, get_two)
+        homebox[me] = backbox[me]
+
+        def home(step, carry):
+            swap_arrived(chips, step, backbox, homebox, send_two, get_two)
+            return carry
+
+        lax.fori_loop(1, chips, home, 0)
+        blocks = [homebox[at].astype(F32) for at in range(chips)]
+        for image in range(images):
+            home_ref[image] = jnp.concatenate(
+                [block[image * local : (image + 1) * local] for block in blocks], 0
+            ).astype(BF16)
+
+        def drain(step, carry):
+            swap_sent(chips, step, outbox, inbox.at[core], send_one, get_one)
+            swap_sent(chips, step, backbox, homebox, send_two, get_two)
+            return carry
+
+        lax.fori_loop(1, chips, drain, 0)
+
+        def drain_pass(at, carry):
+            hand(at).wait_send()
+            return carry
+
+        lax.fori_loop(0, chips, drain_pass, 0)
+
+        def drain_pair(e, carry):
+            pair_copy(e).wait_send()
+            return carry
+
+        lax.fori_loop(0, local, drain_pair, 0)
+
+    inside = pl.BlockSpec(memory_space=pltpu.VMEM)
+    outside = pl.BlockSpec(memory_space=pl.ANY)
+    shape = jax.ShapeDtypeStruct
+    home_shape = shape((images, experts, width), BF16)
+    if backward:
+        out_shape = [
+            home_shape,
+            shape((local, every, hidden), BF16),
+            shape((local, every, hidden), BF16),
+            shape((local, every, width), BF16),
+            shape((8, every), F32),
+        ]
+        operands = (values, received, expert_in, expert_out)
+        in_specs = [inside, inside, outside, outside]
+        extra = [pltpu.VMEM((local, every, hidden), F32)]
+    else:
+        out_shape = [home_shape, shape((local, every, width), BF16)]
+        operands = (values, expert_in, expert_out)
+        in_specs = [inside, outside, outside]
+        extra = []
+    dma = pltpu.SemaphoreType.DMA
+    return pl.pallas_call(
+        kernel,
+        in_specs=in_specs,
+        out_specs=[inside] * len(out_shape),
+        out_shape=out_shape,
+        scratch_shapes=extra
+        + [
+            pltpu.VMEM((local, width, hidden), F32),
+            pltpu.VMEM((local, hidden, width), F32),
+            pltpu.VMEM((chips, rows, width), BF16),
+            pltpu.VMEM((cores, chips, rows, width), BF16),
+            pltpu.VMEM((local, cores, half, width), F32),
+            pltpu.VMEM((local, half, width), BF16),
+            pltpu.VMEM((local, half, width), BF16),
+            pltpu.VMEM((local * half, width), BF16),
+            pltpu.VMEM((chips, rows, width), BF16),
+            pltpu.VMEM((chips, rows, width), BF16),
+        ]
+        + [dma((local,))] * 2
+        + [dma((chips,))] * 4
+        + [dma((local,))] * 2
+        + [dma((chips,))] * 2,
+        compiler_params=pltpu.CompilerParams(
+            collective_id=collective_id, has_side_effects=True, vmem_limit_bytes=VMEM_BYTES
+        ),
+        name="exchange_back" if backward else "exchange",
+    )(*operands)
+
+
+def expert_adam(weight, first, second, lefts, rights, scale, rate):
+    layers, local, tall, wide = weight.shape
+    deep = lefts[0].shape[1]
+
+    def kernel(scale_ref, w_ref, m_ref, s_ref, *refs):
+        left_refs, right_refs = refs[:layers], refs[layers : 2 * layers]
+        new_w, new_m, new_s = refs[2 * layers :]
+
+        for layer in range(layers):
+
+            @pl.when(pl.program_id(0) == layer)
+            def _(layer=layer):
+                grad = tn(left_refs[layer][...], right_refs[layer][...]) * scale_ref[0]
+                moment = BETA_ONE * m_ref[...] + (1.0 - BETA_ONE) * grad
+                spread_of = BETA_TWO * s_ref[...] + (1.0 - BETA_TWO) * (grad * grad)
+                ratio = (moment * (1.0 / (1.0 - BETA_ONE**STEP))) / (
+                    jnp.sqrt(spread_of * (1.0 / (1.0 - BETA_TWO**STEP))) + ADAM_EPS
+                )
+                held = w_ref[...]
+                new_m[...] = moment
+                new_s[...] = spread_of
+                new_w[...] = held - rate * (ratio + WEIGHT_DECAY * held)
+
+    def factor_spec(layer, columns):
+        last = local - 1
+        return pl.BlockSpec(
+            (None, deep, columns),
+            lambda l, e: (jnp.where(l == layer, e, jnp.where(l < layer, 0, last)), 0, 0),
+        )
+
+    block = pl.BlockSpec((None, None, tall, wide), lambda l, e: (l, e, 0, 0))
+    return pl.pallas_call(
+        kernel,
+        grid=(layers, local),
+        in_specs=[pl.BlockSpec(memory_space=pltpu.SMEM)]
+        + [block] * 3
+        + [factor_spec(layer, tall) for layer in range(layers)]
+        + [factor_spec(layer, wide) for layer in range(layers)],
+        out_specs=[block] * 3,
+        out_shape=[jax.ShapeDtypeStruct(weight.shape, F32)] * 3,
+        compiler_params=pltpu.CompilerParams(vmem_limit_bytes=VMEM_BYTES),
+        name="expert_adam",
+    )(scale, weight, first, second, *lefts, *rights)
 
 
 def adam(weight, first, second, grad, rate):
@@ -633,10 +1185,22 @@
     last_gains = jnp.pad(norm_table[LEN_LO + 4 * layers :], ((0, 6), (0, 0)))
     attention_t = attention.transpose(0, 2, 1).astype(BF16)
     router_t = router.transpose(0, 2, 1).astype(BF16)
-    dense = lax.all_gather(dense_weights.T.astype(BF16), ("dp", "fsdp"), axis=0, tiled=True)
-    attention_all = [
-        lax.all_gather(attention_t[0], ("dp", "fsdp"), axis=0, tiled=True)
-    ]
+    dense_t = dense_weights.T.astype(BF16)
+    local = expert_in.shape[1]
+    own = (
+        lax.axis_size("dp") == 2
+        and lax.axis_size("fsdp") == 1 << BITS
+        and patches.shape[0] * local % 16 == 0
+        and router.shape[1] * router.shape[2] % width == 0
+    )
+    if own:
+        dense, attention_one = gather_all([dense_t, attention_t[0]], 0)
+    else:
+        dense, attention_one = [
+            lax.all_gather(part, ("dp", "fsdp"), axis=0, tiled=True)
+            for part in (dense_t, attention_t[0])
+        ]
+    attention_all = [attention_one]
     router_all = [None]
     for layer in range(1, layers):
         one, two = fetch_layer(attention_t[layer], router_t[layer - 1])
@@ -655,14 +1219,10 @@
         if mixing is not None:
             hidden = outs[0]
         qkv, context, middle, combine, slots = outs[-5:]
-        received = to_experts(slots)
-        rows_all = lax.all_gather(received, "dp", axis=0, tiled=True)
-        produced = sum_rows(
-            expert_forward(
-                rows_all, expert_in[layer - 1].astype(BF16), expert_out[layer - 1].astype(BF16)
-            )
-        ).astype(BF16)
-        returned = from_experts(produced)
+        if own:
+            returned, received = exchange(layer - 1, slots, None, expert_in, expert_out, layer)
+        else:
+            returned, received = plain_exchange(layer - 1, slots, None, expert_in, expert_out)
         kept.append((hidden, qkv, context, middle, combine, returned, received))
         hidden = middle
         mixing = (combine, returned)
@@ -673,21 +1233,24 @@
     grad_hidden, grad_returned, grad_head, grad_bias, grad_last, loss_part = top(
         resolution, labels, middle, combine, returned, head, head_bias, last_gains, classes, images
     )
-    grad_head = jnp.concatenate([grad_head[:, :classes], grad_bias[0:1, :classes]], 0)
     attention_grads = [None] * layers
     router_grads = [None] * (layers - 1)
-    win_grads = [None] * (layers - 1)
-    wout_grads = [None] * (layers - 1)
     gain_grads = [None] * layers
+    in_factors = [None] * (layers - 1)
+    out_factors = [None] * (layers - 1)
+    local_squares = 0.0
     for layer in reversed(range(1, layers)):
         before, qkv, context, middle, combine, returned, received = kept[layer]
-        grad_received = to_experts(grad_returned)
-        rows_all = lax.all_gather(received, "dp", axis=0, tiled=True)
-        grads_all = lax.all_gather(grad_received, "dp", axis=0, tiled=True)
-        grad_part, grad_win, grad_wout = expert_backward(
-            rows_all, grads_all, expert_in[layer - 1].astype(BF16), expert_out[layer - 1].astype(BF16)
-        )
-        grad_home = from_experts(sum_rows(grad_part).astype(BF16))
+        if own:
+            outs = exchange(
+                layer - 1, grad_returned, received, expert_in, expert_out, layers + layer
+            )
+        else:
+            outs = plain_exchange(layer - 1, grad_returned, received, expert_in, expert_out)
+        grad_home, hid, grad_pre, grad_out, squares = outs
+        local_squares = local_squares + jnp.sum(squares)
+        in_factors[layer - 1] = (received, grad_pre)
+        out_factors[layer - 1] = (hid, grad_out)
         below = kept[layer - 1][4] if layer > 1 else None
         outs = sparse_backward(
             resolution, before, qkv, context, middle, grad_hidden, returned, grad_home, below,
@@ -697,11 +1260,8 @@
         if below is not None:
             grad_returned = outs[1]
         grad_attention, grad_router, grad_gain = outs[-3:]
-        attention_grads[layer], router_grads[layer - 1] = share_layer(
-            grad_attention, grad_router, router.shape[2], router.shape[1]
-        )
-        win_grads[layer - 1] = grad_win
-        wout_grads[layer - 1] = grad_wout
+        attention_grads[layer] = grad_attention
+        router_grads[layer - 1] = grad_router
         gain_grads[layer] = grad_gain[:4]
     start, qkv, context, middle = kept[0]
     grad_dense, grad_attention, grad_gain, grad_low, grad_high = first_backward(
@@ -709,36 +1269,109 @@
         gains[0],
     )
     gain_grads[0] = grad_gain[:4]
-    grad_first = lax.psum_scatter(grad_dense, ("dp", "fsdp"), scatter_dimension=0, tiled=True).T
-    attention_grads[0] = lax.psum_scatter(
-        grad_attention, ("dp", "fsdp"), scatter_dimension=0, tiled=True
-    )
+    attention_grads[0] = grad_attention
     grad_pos = grad_low[:LEN_LO] + jnp.dot(interp.T, grad_high, precision=PRECISE)
     grad_table = jnp.concatenate([grad_pos] + gain_grads + [grad_last[:2]], 0)
-    grad_attention = jnp.stack(attention_grads).transpose(0, 2, 1)
-    grad_router_all = jnp.stack(router_grads).transpose(0, 2, 1)
-    grad_expert_in = jnp.stack(win_grads)
-    grad_expert_out = jnp.stack(wout_grads)
-    local_squares = (
-        jnp.sum(grad_first * grad_first)
-        + jnp.sum(grad_attention * grad_attention)
-        + jnp.sum(grad_router_all * grad_router_all)
-        + jnp.sum(grad_expert_in * grad_expert_in)
-        + jnp.sum(grad_expert_out * grad_expert_out)
-    )
-    shared_head, shared_table, loss_total, squares = lax.psum(
-        (grad_head, grad_table, loss_part[0, 0], local_squares), ("dp", "fsdp")
-    )
-    norm = jnp.sqrt(
-        squares + jnp.sum(shared_head * shared_head) + jnp.sum(shared_table * shared_table)
-    )
+    loss_local = loss_part[0, 0]
+    part_rows, part_cols = router.shape[1:]
+    table_rows = grad_table.shape[0]
+    if own:
+        row_at = [0]
+        blocks = []
+
+        def block(values):
+            shaped = values.astype(BF16).reshape(devices, -1, width)
+            blocks.append(shaped)
+            row_at.append(row_at[-1] + shaped.shape[1])
+
+        block(grad_dense)
+        for grad in attention_grads:
+            block(grad)
+        for grad in router_grads:
+            block(
+                grad.reshape(lax.axis_size("fsdp"), part_cols, lax.axis_size("dp"), part_rows)
+                .transpose(2, 0, 1, 3)
+                .reshape(devices, -1)
+            )
+        alone = row_at[-1]
+        blocks.append(jnp.zeros((devices, -alone % 16, width), BF16))
+        head_rows = grad_head.shape[0]
+        head_pad = -head_rows % devices
+        blocks.append(jnp.pad(grad_head.astype(BF16), ((0, head_pad), (0, 0))).reshape(devices, -1, width))
+        bias_flat = grad_bias[0]
+        bias_flat = jnp.pad(bias_flat, (0, -bias_flat.shape[0] % width)).reshape(-1, width)
+        tail = jnp.concatenate([grad_table, bias_flat], 0).astype(BF16)
+        tail = jnp.pad(tail, ((0, -tail.shape[0] % devices), (0, 0)))
+        blocks.append(tail.reshape(devices, -1, width))
+        shared_rows = blocks[-2].shape[1] + blocks[-1].shape[1]
+        last_pad = -shared_rows % 16
+        blocks.append(jnp.zeros((devices, last_pad, width), BF16))
+        stats = jnp.concatenate(
+            [
+                jnp.broadcast_to(local_squares, (1, 128)),
+                jnp.broadcast_to(loss_local, (1, 128)),
+                jnp.zeros((6, 128), F32),
+            ],
+            0,
+        )
+        mine, shared, totals = reduce_all(
+            jnp.concatenate(blocks, 1), stats, shared_rows + last_pad, 2 * layers
+        )
+        shared = shared.reshape(devices, -1, width).astype(F32)
+        head_each = blocks[-3].shape[1]
+        head_all = shared[:, :head_each].reshape(-1, width)[:classes].T
+        tail_all = shared[:, head_each:shared_rows].reshape(-1, width)
+        shared_table = tail_all[:table_rows]
+        bias_all = tail_all[table_rows:].reshape(-1)[None, :classes]
+        shared_head = jnp.concatenate([head_all, bias_all], 0)
+        norm = jnp.sqrt(totals[0, 0])
+        loss_total = totals[1, 0]
+        pieces = [mine[row_at[i] : row_at[i + 1]] for i in range(len(row_at) - 1)]
+        grad_first = pieces[0].T
+        grad_attention = jnp.stack(pieces[1 : 1 + layers]).transpose(0, 2, 1)
+        grad_router_all = jnp.stack(
+            [piece.reshape(part_cols, part_rows).T for piece in pieces[1 + layers :]]
+        )
+    else:
+        grad_first = lax.psum_scatter(
+            grad_dense, ("dp", "fsdp"), scatter_dimension=0, tiled=True
+        ).T
+        shares = [
+            share_layer(attention_grads[layer], router_grads[layer - 1], part_cols, part_rows)
+            for layer in range(1, layers)
+        ]
+        first_share = lax.psum_scatter(
+            attention_grads[0], ("dp", "fsdp"), scatter_dimension=0, tiled=True
+        )
+        grad_attention = jnp.stack([first_share] + [share[0] for share in shares])
+        grad_attention = grad_attention.transpose(0, 2, 1)
+        grad_router_all = jnp.stack([share[1] for share in shares]).transpose(0, 2, 1)
+        local_squares = (
+            local_squares
+            + jnp.sum(grad_first * grad_first)
+            + jnp.sum(grad_attention * grad_attention)
+            + jnp.sum(grad_router_all * grad_router_all)
+        )
+        grad_head = jnp.concatenate([grad_head[:classes].T, grad_bias[0:1, :classes]], 0)
+        shared_head, shared_table, loss_total, squares = lax.psum(
+            (grad_head, grad_table, loss_local, local_squares), ("dp", "fsdp")
+        )
+        norm = jnp.sqrt(
+            squares + jnp.sum(shared_head * shared_head) + jnp.sum(shared_table * shared_table)
+        )
     scale = jnp.minimum(1.0, CLIP_NORM / norm)
+    scale_row = scale.reshape(1)
+
+    def experts_updated(weight, first, second, factors, rate):
+        lefts, rights = zip(*factors)
+        return tuple(expert_adam(weight, first, second, lefts, rights, scale_row, rate))
+
     updates = (
         adam(dense_weights, dense_weights_first, dense_weights_second, grad_first * scale, LEARN_RATE),
         adam(attention, attention_first, attention_second, grad_attention * scale, ATTENTION_RATE),
         adam(router, router_first, router_second, grad_router_all * scale, LEARN_RATE),
-        adam(expert_in, expert_in_first, expert_in_second, grad_expert_in * scale, EXPERT_RATE),
-        adam(expert_out, expert_out_first, expert_out_second, grad_expert_out * scale, LEARN_RATE),
+        experts_updated(expert_in, expert_in_first, expert_in_second, in_factors, EXPERT_RATE),
+        experts_updated(expert_out, expert_out_first, expert_out_second, out_factors, LEARN_RATE),
         adam(classifier, classifier_first, classifier_second, shared_head * scale, LEARN_RATE),
         adam(norm_table, norm_table_first, norm_table_second, shared_table * scale, TABLE_RATE),
     )

time: 1290 us -> 783 us (0.61); the launches traced: 1280 us -> 799 us
  waiting for transfers between devices: 641 us -> 40.8 us
  Pallas kernels: 170 us -> 619 us
  blocking collectives: 141 us -> 0 us
  other arithmetic: 164 us -> 30.8 us
  matrix products: 54.6 us -> 4.34 us
  starting transfers between devices: 40.5 us -> 0.08 us
  local copies, waits for them, and re-layouts: 47.2 us -> 85.9 us
    pallas_call x0 -> x8, Pallas kernels: none -> 449 us  [the longest x4 185 us: exchange(): pl.pallas_call(kernel, in_specs=in_specs, out_specs=[inside] * len(out_sh...]
    unnamed x13 -> x2, waiting for transfers between devices: 277 us -> 0.03 us
    reduce_scatter x5 -> x0, waiting for transfers between devices: 134 us -> none  [the longest x1 102 us: on_device(): lax.psum_scatter(grad_attention, ('dp', 'fsdp'), scatter_dimension=0, til...]
    all_gather x2 -> x0, waiting for transfers between devices: 113 us -> none  [the longest x1 61.2 us: on_device(): lax.all_gather(dense_weights.T.astype(BF16), ('dp', 'fsdp'), axis=0, tile...]
    all_to_all x4 -> x0, blocking collectives: 90.4 us -> none  [the longest x3 70.8 us: to_experts(): lax.all_to_all(values, 'fsdp', split_axis=1, concat_axis=0, tiled=True)]
    sub x7 -> x5, other arithmetic: 93.9 us -> 11 us  [adam(): return (weight - rate * (ratio + WEIGHT_DECAY * weight), first, second)]
    all_gather x2, waiting for transfers between devices: 101 us -> 40.7 us  [fetch_layer(): both = lax.all_gather(pack, ('dp', 'fsdp'), axis=0)]
    dot_general x12 -> x0, matrix products: 52.2 us -> none  [matmul(): return jnp.einsum(form, left, right, preferred_element_type=jnp.float32)]
  transfers between devices with their start and end apart: 15 -> 2, of which waited for: 13 -> 1; matrix products, arithmetic and copies ran while one was open for 8% -> 2% of each run, Pallas kernels for 0% -> 8%
where the time goes in v2:
time: 783 us; the launch traced here: 799 us
  Pallas kernels  619 us (79%)
  local copies, waits for them, and re-layouts  85.9 us (11%)
  waiting for transfers between devices  40.8 us (5%)
  other arithmetic  30.8 us (4%)
  between operations  18 us (2%)
    pallas_call x4, Pallas kernels, exchange(): pl.pallas_call(kernel, in_specs=in_specs, out_specs=[inside] * len(out_sh...  185 us
    pallas_call x7, Pallas kernels, by_image(): pl.pallas_call(kernel, grid_spec=pltpu.PrefetchScalarGridSpec(num_scalar_...  170 us
    pallas_call x1, Pallas kernels, reduce_all(): pl.pallas_call(kernel, in_specs=[pl.BlockSpec(memory_space=pl.ANY), pl.Bl...  135 us
    pallas_call x2, Pallas kernels, expert_adam(): pl.pallas_call(kernel, grid=(layers, local), in_specs=[pl.BlockSpec(memor...  91.6 us
    concatenate x2, local copies, waits for them, and re-layouts, on_device(): jnp.concatenate(blocks, 1)  41.2 us
    all_gather x2, waiting for transfers between devices, fetch_layer(): both = lax.all_gather(pack, ('dp', 'fsdp'), axis=0)  40.7 us
    pallas_call x1, Pallas kernels, gather_all(): pl.pallas_call(kernel, in_specs=[pl.BlockSpec(memory_space=pltpu.VMEM)] *...  37 us
  transfers between devices with their start and end apart: 2, of which 1 were waited for; matrix products, arithmetic and copies ran while one was open for 2% of the time, Pallas kernels for 8%

profile of v2, /device:TPU:0, one launch (start us, length us, event | category | flops | bytes accessed | tf_op | source)
XLA Modules:
  0.0 799.0 jit_solution(17183357715109971838)
XLA Ops:
  11.1 2.4 slice.198
  17.9 37.0 %gather_all.1 = (bf16[2,2,2,2,2,120,384]{6,5,4,3,2,1,0:T(8,128)(2,1)}, bf16[2,2,2,2,2,48,384]{6,5,4,3,2,1,0:T(8,128)(2,1)}) custom-call(bf16[120,384]{1,0:T(8,128)(2,1)} %convert_bitcast_fusion.1.refs_0_, bf16[48,384]{1,0:T(8,128)(2,1)} %get-tuple-element.239.refs_1_), custom_call_target="tpu_custom_call" | custom-call | tf_op jit(solution)/shard_map/gather_all/pallas_call | solution.py:701
  60.3 26.0 %first_forward.1 = (f32[4,576,384]{2,1,0:T(8,128)}, bf16[4,576,1152]{2,1,0:T(8,128)(2,1)}, bf16[4,576,384]{2,1,0:T(8,128)(2,1)}, f32[4,576,384]{2,1,0:T(8,128)}, f32[4,576,384]{2,1,0:T(8,128)}) custom-call(s32[4]{0:T(128)} %refs_0_.13, bf16[4,576,768]{2,1,0:T(8,128)(2,1)} %refs_1_.9, bf16[3840,384]{1,0:T(8,128)(2,1)} %bitcast.92, ...), custom_call_target="tpu_custom_call" | custom-call | tf_op jit(solution)/shard_map/first_forward/pallas_call | solution.py:287
  88.5 40.7 %all-gather.9.cloned.1.call-done = bf16[32,52,384]{2,1,0:T(8,128)(2,1)} async-done(((bf16[1,52,384]{2,1,0:T(8,128)(2,1)}), bf16[32,52,384]{2,1,0:T(8,128)(2,1)}) %all-gather.9.cloned.1.call-update) | async-done | bytes 1277968 | tf_op jit(solution)/shard_map/all_gather | solution.py:560
  132.3 19.2 %sparse_forward.2 = (bf16[4,576,1152]{2,1,0:T(8,128)(2,1)}, bf16[4,576,384]{2,1,0:T(8,128)(2,1)}, f32[4,576,384]{2,1,0:T(8,128)}, bf16[4,576,128]{2,1,0:T(8,128)(2,1)}, bf16[4,128,384]{2,1,0:T(8,128)(2,1)}) custom-call(s32[4]{0:T(128)} %refs_0_.13, f32[4,576,384]{2,1,0:T(8,128)} %get-tuple-element.90.refs_1_, bf16[1536,384]{1,0:T(8,128)(2,1)} %bitcast.95, ...), custom_call_target="tpu_custom_call" | custom-call | tf_op jit(solution)/shard_map/sparse_forward/pallas_call | solution.py:287
  151.5 41.3 %exchange.2 = (bf16[4,128,384]{2,1,0:T(8,128)(2,1)}, bf16[8,128,384]{2,1,0:T(8,128)(2,1)}) custom-call(bf16[4,128,384]{2,1,0:T(8,128)(2,1)} %get-tuple-element.95.refs_0_, f32[2,8,384,768]{3,2,1,0:T(8,128)} %w_ref.2, f32[2,8,768,384]{3,2,1,0:T(8,128)} %w_ref.3), custom_call_target="tpu_custom_call" | custom-call | tf_op jit(solution)/shard_map/exchange/pallas_call | solution.py:1064
  194.0 19.7 %sparse_forward.3 = (f32[4,576,384]{2,1,0:T(8,128)}, bf16[4,576,1152]{2,1,0:T(8,128)(2,1)}, bf16[4,576,384]{2,1,0:T(8,128)(2,1)}, f32[4,576,384]{2,1,0:T(8,128)}...) custom-call(s32[4]{0:T(128)} %refs_0_.13, f32[4,576,384]{2,1,0:T(8,128)} %get-tuple-element.93.refs_1_.refs_4_, ...), custom_call_target="tpu_custom_call" | custom-call | tf_op jit(solution)/shard_map/sparse_forward/pallas_call | solution.py:287
  213.7 44.3 %exchange.3 = (bf16[4,128,384]{2,1,0:T(8,128)(2,1)}, bf16[8,128,384]{2,1,0:T(8,128)(2,1)}) custom-call(bf16[4,128,384]{2,1,0:T(8,128)(2,1)} %get-tuple-element.102.refs_0_, f32[2,8,384,768]{3,2,1,0:T(8,128)} %w_ref.2, f32[2,8,768,384]{3,2,1,0:T(8,128)} %w_ref.3), custom_call_target="tpu_custom_call" | custom-call | tf_op jit(solution)/shard_map/exchange/pallas_call | solution.py:1064
  258.0 10.8 %top.1 = (f32[4,576,384]{2,1,0:T(8,128)}, bf16[4,128,384]{2,1,0:T(8,128)(2,1)}, f32[1024,384]{1,0:T(8,128)}, f32[8,1024]{1,0:T(8,128)}, f32[8,384]{1,0:T(8,128)}, /*index=5*/f32[8,128]{1,0:T(8,128)}) custom-call(s32[4]{0:T(128)} %refs_0_.13, s32[4]{0:T(128)} %refs_1_.8, f32[4,576,384]{2,1,0:T(8,128)} %get-tuple-element.100.refs_2_.refs_4_, ...), custom_call_target="tpu_custom_call" | custom-call | tf_op jit(solution)/shard_map/top/pallas_call | solution.py:287
  268.8 35.8 %exchange_back.2 = (bf16[4,128,384]{2,1,0:T(8,128)(2,1)}, bf16[8,128,768]{2,1,0:T(8,128)(2,1)}, bf16[8,128,768]{2,1,0:T(8,128)(2,1)}, bf16[8,128,384]{2,1,0:T(8,128)(2,1)}, f32[8,128]{1,0:T(8,128)}) custom-call(bf16[4,128,384]{2,1,0:T(8,128)(2,1)} %get-tuple-element.105.refs_0_, bf16[8,128,384]{2,1,0:T(8,128)(2,1)} %get-tuple-element.106.refs_1_, ...), custom_call_target="tpu_custom_call" | custom-call | tf_op jit(solution)/shard_map/exchange_back/pallas_call | solution.py:1064
  304.7 26.1 %sparse_backward.2 = (f32[4,576,384]{2,1,0:T(8,128)}, bf16[4,128,384]{2,1,0:T(8,128)(2,1)}, f32[1536,384]{1,0:T(8,128)}, f32[128,384]{1,0:T(8,128)}, f32[8,384]{1,0:T(8,128)}) custom-call(s32[4]{0:T(128)} %refs_0_.13, f32[4,576,384]{2,1,0:T(8,128)} %get-tuple-element.97.refs_1_, bf16[4,576,1152]{2,1,0:T(8,128)(2,1)} %get-tuple-element.98.refs_2_, ...), custom_call_target="tpu_custom_call" | custom-call | tf_op jit(solution)/shard_map/sparse_backward/pallas_call | solution.py:287
  330.8 63.7 %exchange_back.3 = (bf16[4,128,384]{2,1,0:T(8,128)(2,1)}, bf16[8,128,768]{2,1,0:T(8,128)(2,1)}, bf16[8,128,768]{2,1,0:T(8,128)(2,1)}, bf16[8,128,384]{2,1,0:T(8,128)(2,1)}, f32[8,128]{1,0:T(8,128)}) custom-call(bf16[4,128,384]{2,1,0:T(8,128)(2,1)} %get-tuple-element.109.refs_0_, bf16[8,128,384]{2,1,0:T(8,128)(2,1)} %get-tuple-element.110.refs_1_.refs_0_, ...), custom_call_target="tpu_custom_call" | custom-call | tf_op jit(solution)/shard_map/exchange_back/pallas_call | solution.py:1064
  394.4 25.7 %sparse_backward.3 = (f32[4,576,384]{2,1,0:T(8,128)}, f32[1536,384]{1,0:T(8,128)}, f32[128,384]{1,0:T(8,128)}, f32[8,384]{1,0:T(8,128)}) custom-call(s32[4]{0:T(128)} %refs_0_.13, f32[4,576,384]{2,1,0:T(8,128)} %get-tuple-element.90.refs_1_, bf16[4,576,1152]{2,1,0:T(8,128)(2,1)} %get-tuple-element.91.refs_2_, ...), custom_call_target="tpu_custom_call" | custom-call | tf_op jit(solution)/shard_map/sparse_backward/pallas_call | solution.py:287
  420.2 42.8 %first_backward.1 = (f32[3840,384]{1,0:T(8,128)}, f32[1536,384]{1,0:T(8,128)}, f32[8,384]{1,0:T(8,128)}, f32[208,384]{1,0:T(8,128)}, f32[576,384]{1,0:T(8,128)}) custom-call(s32[4]{0:T(128)} %refs_0_.13, bf16[4,576,768]{2,1,0:T(8,128)(2,1)} %refs_1_.9, f32[4,576,384]{2,1,0:T(8,128)} %get-tuple-element.86.refs_2_, ...), custom_call_target="tpu_custom_call" | custom-call | tf_op jit(solution)/shard_map/first_backward/pallas_call | solution.py:287
  463.0 3.1 convert_element_type.88
  483.9 2.4 convert_element_type.100
  489.9 3.0 fusion.1
  498.5 41.2 %concatenate.41.grads_ref = bf16[2,2,2,2,2,320,384]{6,5,4,3,2,1,0:T(8,128)(2,1)} concatenate(bf16[2,2,2,2,2,120,384]{6,5,4,3,2,1,0:T(8,128)(2,1)S(1)} %bitcast.94, bf16[2,2,2,2,2,48,384]{6,5,4,3,2,1,0:T(8,128)(2,1)} %bitcast.103, bf16[2,2,2,2,2,48,384]{6,5,4,3,2,1,0:T(8,128)(2,1)} %bitcast.104, bf16[2,2,2,2,2,48,384]{6,5,4,3,2,1,0:T(8,128)(2,1)} %bitcast.105, ...), dimensions={5} | concatenate | bytes 15728640 | tf_op jit(solution)/shard_map/concatenate | solution.py:1318
  540.4 135.0 %reduce_all.1 = (f32[320,384]{1,0:T(8,128)}, bf16[2,2,2,2,2,48,384]{6,5,4,3,2,1,0:T(8,128)(2,1)}, f32[8,128]{1,0:T(8,128)}) custom-call(bf16[2,2,2,2,2,320,384]{6,5,4,3,2,1,0:T(8,128)(2,1)} %concatenate.41.grads_ref, f32[8,128]{1,0:T(8,128)} %broadcast.157.stats_ref), custom_call_target="tpu_custom_call" | custom-call | tf_op jit(solution)/shard_map/reduce_all/pallas_call | solution.py:805
  682.1 2.6 slice.171
  684.7 3.0 copy.92
  693.0 5.1 multiply_subtract_fusion
  699.1 45.7 %expert_adam.2 = (f32[2,8,384,768]{3,2,1,0:T(8,128)}, f32[2,8,384,768]{3,2,1,0:T(8,128)}, f32[2,8,384,768]{3,2,1,0:T(8,128)}) custom-call(f32[1]{0:T(128)} %bitcast.35.scale_ref, f32[2,8,384,768]{3,2,1,0:T(8,128)} %w_ref.2, f32[2,8,384,768]{3,2,1,0:T(8,128)} %m_ref.2, f32[2,8,384,768]{3,2,1,0:T(8,128)} %s_ref.2, ...), custom_call_target="tpu_custom_call" | custom-call | tf_op jit(solution)/shard_map/expert_adam/pallas_call | solution.py:1124
  744.7 45.9 %expert_adam.3 = (f32[2,8,768,384]{3,2,1,0:T(8,128)}, f32[2,8,768,384]{3,2,1,0:T(8,128)}, f32[2,8,768,384]{3,2,1,0:T(8,128)}) custom-call(f32[1]{0:T(128)} %bitcast.35.scale_ref, f32[2,8,768,384]{3,2,1,0:T(8,128)} %w_ref.3, f32[2,8,768,384]{3,2,1,0:T(8,128)} %m_ref.3, f32[2,8,768,384]{3,2,1,0:T(8,128)} %s_ref.3, ...), custom_call_target="tpu_custom_call" | custom-call | tf_op jit(solution)/shard_map/expert_adam/pallas_call | solution.py:1124
  (132 shorter events, 58.2 us)
Async XLA Ops:
  7.2 79.2 %all-gather.7.cloned.1.call-start = ((), (), s32[]{:S(2)}) async-start(), calls=%async_computation | async-start | bytes 1419264 | tf_op jit(solution)/shard_map/all_gather | solution.py:560
  10.3 118.9 %all-gather.9.cloned.1.call-start = ((), (), s32[]{:S(2)}) async-start(), calls=%async_computation.1 | async-start | bytes 1419264 | tf_op jit(solution)/shard_map/all_gather | solution.py:560
  13.8 2.8 slice-start.2
  13.8 3.4 copy-start.10
  14.8 42.3 %slice-start = ((f32[385,1000]{1,0:T(8,128)}), f32[1,1000]{1,0:T(1,128)S(1)}, s32[]{:S(2)}) async-start(f32[385,1000]{1,0:T(8,128)} %param.32), calls=%async_computation.2 | async-start | bytes 8192 | tf_op jit(solution)/shard_map/slice | solution.py:1232
  14.8 42.9 %slice-start.1 = ((f32[210,384]{1,0:T(8,128)}), f32[196,384]{1,0:T(8,128)S(1)}, s32[]{:S(2)}) async-start(f32[210,384]{1,0:T(8,128)} %param.33), calls=%async_computation.3 | async-start | bytes 614400 | tf_op jit(solution)/shard_map/slice | solution.py:1177
  86.3 44.8 %copy-start.7 = (bf16[32,52,384]{2,1,0:T(8,128)(2,1)S(1)}, bf16[32,52,384]{2,1,0:T(8,128)(2,1)}, u32[]{:S(2)}) copy-start(bf16[32,52,384]{2,1,0:T(8,128)(2,1)} %all-gather.7.cloned.1.call-done) | copy-start | bytes 3833860
  151.5 41.3 %copy-start.8 = (bf16[32,52,384]{2,1,0:T(8,128)(2,1)S(1)}, bf16[32,52,384]{2,1,0:T(8,128)(2,1)}, u32[]{:S(2)}) copy-start(bf16[32,52,384]{2,1,0:T(8,128)(2,1)} %all-gather.9.cloned.1.call-done) | copy-start | bytes 3833860
  463.0 3.4 copy-start.6
  466.4 2.1 copy-start.5
  486.2 9.0 %copy-start.19 = (f32[8,128]{1,0:T(8,128)S(1)}, f32[8,128]{1,0:T(8,128)}, u32[]{:S(2)}) copy-start(f32[8,128]{1,0:T(8,128)} %get-tuple-element.127) | copy-start | bytes 12292
  486.2 9.6 %copy-start.20 = (f32[8,128]{1,0:T(8,128)S(1)}, f32[8,128]{1,0:T(8,128)}, u32[]{:S(2)}) copy-start(f32[8,128]{1,0:T(8,128)} %get-tuple-element.128) | copy-start | bytes 12292
  682.1 5.7 copy-start.16
  684.7 3.2 copy-start.11
  687.8 2.4 copy-start.3
  687.9 4.4 copy-start.15
  687.9 4.4 copy-start.17
  687.9 4.4 copy-start.18
  688.0 5.0 copy-start
  688.0 5.0 copy-start.1
  688.0 5.0 slice-start.3
  693.0 5.2 copy-start.9
  693.0 5.1 copy-start.12
  693.0 5.1 copy-start.13
  (3 other events, 4.2 us)
Sparse Core Ops, SparseCore 0:
  11.4 60.6 all-gather.6
  75.5 53.6 all-gather.8

commit v3 on v2

--- a/solution.py
+++ b/solution.py
@@ -114,12 +114,12 @@
     width = context.shape[1]
     first = lax.broadcasted_iota(jnp.int32, (rows, 128), 1) < 64
     masks = side_masks()
-
-    def pair(index, carry):
-        offset = index * 128
-        query = qkv[:rows, lanes(offset)] * BF16(0.125)
-        keys = qkv[:rows, lanes(width + offset)]
-        values = qkv[:rows, lanes(2 * width + offset)]
+    ones = jnp.ones((rows, 128), BF16)
+    for offset in range(0, width, 128):
+        query = qkv[:rows, offset : offset + 128] * BF16(0.125)
+        keys = qkv[:rows, width + offset : width + offset + 128]
+        values = qkv[:rows, 2 * width + offset : 2 * width + offset + 128]
+        summing = jnp.concatenate([values, ones], 1)
         found = []
         for side in (0, 1):
             scores = nt(query * masks[side], keys)
@@ -127,51 +127,50 @@
                 lane = lax.broadcasted_iota(jnp.int32, (rows, rows), 1)
                 scores = jnp.where(lane < limit, scores, NEG_FILL)
             raised = jnp.exp(scores - jnp.max(scores, 1, keepdims=True))
-            total = jnp.sum(raised, 1, keepdims=True)
-            found.append(nn(raised.astype(BF16), values) * (1.0 / total))
-        context[:rows, lanes(offset)] = jnp.where(first, found[0], found[1]).astype(BF16)
-        return carry
-
-    lax.fori_loop(0, width // 128, pair, 0)
+            both = nn(raised.astype(BF16), summing)
+            found.append(both[:, :128] * (1.0 / both[:, 128:]))
+        context[:rows, offset : offset + 128] = jnp.where(first, found[0], found[1]).astype(BF16)
+
+
+def scores_back(limit, keys, values, query, grad):
+    scores = nt(keys, query)
+    if limit is not None:
+        scores = jnp.where(row_number(scores.shape) < limit, scores, NEG_FILL)
+    raised = jnp.exp(scores - jnp.max(scores, 0, keepdims=True))
+    probs = raised * (1.0 / jnp.sum(raised, 0, keepdims=True))
+    grad_values = nn(probs.astype(BF16), grad)
+    grad_probs = nt(values, grad)
+    mixed = jnp.sum(probs * grad_probs, 0, keepdims=True)
+    grad_scores = (probs * (grad_probs - mixed)).astype(BF16)
+    return grad_scores, nn(grad_scores, query), grad_values
 
 
 def attention_rows_back(rows, limit, qkv, grad_context, grad_qkv):
     width = grad_context.shape[1]
     masks = side_masks()
-
-    def pair(index, carry):
-        offset = index * 128
-        query = qkv[:rows, lanes(offset)] * BF16(0.125)
-        keys = qkv[:rows, lanes(width + offset)]
-        values = qkv[:rows, lanes(2 * width + offset)]
-        grad = grad_context[:rows, lanes(offset)]
-        grad_query = grad_keys = grad_values = None
-        for side in (0, 1):
-            query_side = query * masks[side]
-            grad_side = grad * masks[side]
-            scores = nt(keys, query_side)
-            if limit is not None:
-                scores = jnp.where(row_number((rows, rows)) < limit, scores, NEG_FILL)
-            raised = jnp.exp(scores - jnp.max(scores, 0, keepdims=True))
-            probs = raised * (1.0 / jnp.sum(raised, 0, keepdims=True))
-            part_values = nn(probs.astype(BF16), grad_side)
-            grad_probs = nt(values, grad_side)
-            mixed = jnp.sum(probs * grad_probs, 0, keepdims=True)
-            grad_scores = (probs * (grad_probs - mixed)).astype(BF16)
-            part_keys = nn(grad_scores, query_side)
-            part_query = tn(grad_scores, keys * masks[side])
-            if side == 0:
-                grad_query, grad_keys, grad_values = part_query, part_keys, part_values
-            else:
-                grad_query = grad_query + part_query
-                grad_keys = grad_keys + part_keys
-                grad_values = grad_values + part_values
-        grad_qkv[:rows, lanes(offset)] = (grad_query * 0.125).astype(BF16)
-        grad_qkv[:rows, lanes(width + offset)] = grad_keys.astype(BF16)
-        grad_qkv[:rows, lanes(2 * width + offset)] = grad_values.astype(BF16)
-        return carry
-
-    lax.fori_loop(0, width // 128, pair, 0)
+    first = lax.broadcasted_iota(jnp.int32, (rows, 128), 1) < 64
+    for offset in range(0, width, 128):
+        query = qkv[:rows, offset : offset + 128] * BF16(0.125)
+        keys = qkv[:rows, width + offset : width + offset + 128]
+        values = qkv[:rows, 2 * width + offset : 2 * width + offset + 128]
+        grad = grad_context[:rows, offset : offset + 128]
+        queries = [query * mask for mask in masks]
+        grads = [grad * mask for mask in masks]
+        if limit is None:
+            grad_scores, grad_keys, grad_values = scores_back(
+                limit, keys, values, jnp.concatenate(queries, 0), jnp.concatenate(grads, 0)
+            )
+            both = tn(grad_scores, keys)
+            grad_query = jnp.where(first, both[:rows], both[rows:])
+        else:
+            one, two = [
+                scores_back(limit, keys, values, queries[side], grads[side]) for side in (0, 1)
+            ]
+            grad_query = tn(one[0], keys * masks[0]) + tn(two[0], keys * masks[1])
+            grad_keys, grad_values = one[1] + two[1], one[2] + two[2]
+        grad_qkv[:rows, offset : offset + 128] = (grad_query * 0.125).astype(BF16)
+        grad_qkv[:rows, width + offset : width + offset + 128] = grad_keys.astype(BF16)
+        grad_qkv[:rows, 2 * width + offset : 2 * width + offset + 128] = grad_values.astype(BF16)
 
 
 def attention_forward(rows, limit, hidden, gains, weights, qkv, context):
@@ -255,9 +254,18 @@
     return jnp.where(row_number(values.shape) < limit, values, 0.0)
 
 
-def by_image(name, body, scalars, per_image, whole, out_image, out_sum, scratch=()):
+def work_of(giga):
+    return pl.CostEstimate(flops=giga * 10**9, bytes_accessed=1 << 20, transcendentals=0)
+
+
+def by_image(name, body, scalars, per_image, whole, out_image, out_sum, scratch=(), pack=None):
     images = scalars[0].shape[0]
-    counts = (len(scalars), len(per_image), len(whole), len(out_image), len(out_sum), len(scratch))
+    inner = pack[0] if pack else 0
+    packed = 1 if pack else 0
+    counts = (
+        len(scalars), len(per_image), len(whole), len(out_image), packed, len(out_sum) - inner,
+        inner, len(scratch),
+    )
 
     def kernel(*refs):
         groups, at = [], 0
@@ -265,21 +273,36 @@
             groups.append(refs[at : at + count])
             at += count
         index = pl.program_id(0)
+        sums = tuple(groups[6]) + tuple(groups[5])
 
         @pl.when(index == 0)
         def _():
-            for ref in groups[4]:
+            for ref in sums:
                 ref[...] = jnp.zeros_like(ref)
 
         numbers = [ref[index] for ref in groups[0]]
+        given = (*groups[1:4], sums, groups[7])
 
         @pl.when(numbers[0] == 1)
         def _():
-            body(LEN, None, numbers, *groups[1:])
+            body(LEN, None, numbers, *given)
 
         @pl.when(numbers[0] != 1)
         def _():
-            body(ROWS_LO, LEN_LO + numbers[0], numbers, *groups[1:])
+            body(ROWS_LO, LEN_LO + numbers[0], numbers, *given)
+
+        if pack:
+
+            @pl.when(index == images - 1)
+            def _():
+                def write(device, carry):
+                    groups[4][0][device] = pack[3](sums, device).astype(BF16)
+                    return carry
+
+                lax.fori_loop(0, pack[1], write, 0)
+
+    width = out_sum[0][1] if pack else 0
+    pack_shapes = [(pack[1], pack[2], width)] if pack else []
 
     def image_spec(shape):
         return pl.BlockSpec((None,) + tuple(shape[1:]), lambda i, *_: (i, 0, 0))
@@ -292,14 +315,32 @@
             in_specs=[image_spec(a.shape) for a in per_image]
             + [pl.BlockSpec(memory_space=pltpu.VMEM) for _ in whole],
             out_specs=[image_spec((images,) + shape) for shape, _ in out_image]
-            + [pl.BlockSpec(shape, lambda i, *_: (0, 0)) for shape in out_sum],
-            scratch_shapes=list(scratch),
+            + [pl.BlockSpec(shape, lambda i, *_: (0, 0, 0)) for shape in pack_shapes]
+            + [pl.BlockSpec(shape, lambda i, *_: (0, 0)) for shape in out_sum[inner:]],
+            scratch_shapes=[pltpu.VMEM(shape, F32) for shape in out_sum[:inner]] + list(scratch),
         ),
         out_shape=[jax.ShapeDtypeStruct((images,) + shape, dtype) for shape, dtype in out_image]
-        + [jax.ShapeDtypeStruct(shape, F32) for shape in out_sum],
+        + [jax.ShapeDtypeStruct(shape, BF16) for shape in pack_shapes]
+        + [jax.ShapeDtypeStruct(shape, F32) for shape in out_sum[inner:]],
         compiler_params=pltpu.CompilerParams(vmem_limit_bytes=VMEM_BYTES),
+        cost_estimate=work_of(images * 8),
         name=name,
     )(*scalars, *per_image, *whole)
+
+
+def rows_of(ref, device, count):
+    return ref[pl.ds(pl.multiple_of(device * count, 8), count)]
+
+
+def padded_rows(blocks):
+    rows = sum(block.shape[0] for block in blocks)
+    if rows % 16:
+        blocks = blocks + [jnp.zeros((-rows % 16, blocks[0].shape[1]), F32)]
+    return jnp.concatenate(blocks, 0) if len(blocks) > 1 else blocks[0]
+
+
+def up_16(count):
+    return count + -count % 16
 
 
 def first_forward(resolution, patches, dense, attention, positions, gains, width):
@@ -373,7 +414,7 @@
     )
 
 
-def top(resolution, labels, middle, combine, returned, head, head_bias, last_gains, classes, images):
+def top(resolution, labels, middle, combine, returned, head, head_bias, last_gains, classes, images, devices):
     width = middle.shape[2]
     experts = returned.shape[1]
     padded = head.shape[1]
@@ -425,15 +466,22 @@
         [head, head_bias, last_gains],
         [((LEN, width), F32), ((experts, width), BF16)],
         [(padded, width), (8, padded), (8, width), (8, 128)],
+        pack=devices
+        and (
+            1, devices, padded // devices,
+            lambda sums, device: rows_of(sums[0], device, padded // devices),
+        ),
     )
 
 
 def sparse_backward(
     resolution, hidden, qkv, context, middle, grad_hidden, returned, grad_home, below, attention,
-    router, gains,
+    router, gains, devices,
 ):
     width = middle.shape[2]
     experts = router.shape[0]
+    chips = lax.axis_size("fsdp")
+    local = experts // chips
 
     def body(rows, limit, numbers, images, whole, outs, sums, scratch):
         hidden_ref, qkv_ref, context_ref, middle_ref, grad_ref, returned_ref, home_ref = images[:7]
@@ -477,12 +525,25 @@
         outs,
         [(4 * width, width), (experts, width), (8, width)],
         [pltpu.VMEM((LEN, width), BF16), pltpu.VMEM((LEN, 3 * width), BF16)],
-    )
-
-
-def first_backward(resolution, patches, start, qkv, context, middle, grad_hidden, dense, attention, gains):
+        pack=devices
+        and (
+            2, devices, up_16(4 * width // devices + local),
+            lambda sums, device: padded_rows(
+                [
+                    rows_of(sums[0], device, 4 * width // devices),
+                    rows_of(sums[1], device % chips, local),
+                ]
+            ),
+        ),
+    )
+
+
+def first_backward(
+    resolution, patches, start, qkv, context, middle, grad_hidden, dense, attention, gains, devices
+):
     width = middle.shape[2]
     pixels = patches.shape[2]
+    columns = dense.shape[0]
 
     def body(rows, limit, numbers, images, whole, outs, sums, scratch):
         patches_ref, start_ref, qkv_ref, context_ref, middle_ref, grad_ref = images
@@ -510,8 +571,18 @@
         [patches, start, qkv, context, middle, grad_hidden],
         [dense, attention, gains],
         [],
-        [(dense.shape[0], width), (4 * width, width), (8, width), (ROWS_LO, width), (LEN, width)],
+        [(columns, width), (4 * width, width), (8, width), (ROWS_LO, width), (LEN, width)],
         [pltpu.VMEM((LEN, width), BF16), pltpu.VMEM((LEN, 3 * width), BF16)],
+        pack=devices
+        and (
+            2, devices, up_16((columns + 4 * width) // devices),
+            lambda sums, device: padded_rows(
+                [
+                    rows_of(sums[0], device, columns // devices),
+                    rows_of(sums[1], device, 4 * width // devices),
+                ]
+            ),
+        ),
     )
 
 
@@ -551,18 +622,21 @@
 
 
 def fetch_layer(attention_t, router_t):
-    part, width = attention_t.shape
-    part_cols, part_rows = router_t.shape
+    width = attention_t.shape[1]
     flat = router_t.reshape(-1)
     pack = jnp.concatenate(
         [attention_t, jnp.pad(flat, (0, -flat.size % width)).reshape(-1, width)], 0
     )
-    both = lax.all_gather(pack, ("dp", "fsdp"), axis=0)
+    return lax.all_gather(pack, ("dp", "fsdp"), axis=0)
+
+
+def open_layer(both, part, part_cols, part_rows):
+    width = both.shape[2]
     rows_dp = lax.axis_size("dp")
     cols_fsdp = lax.axis_size("fsdp")
     router = (
         both[:, part:]
-        .reshape(rows_dp * cols_fsdp, -1)[:, : flat.size]
+        .reshape(rows_dp * cols_fsdp, -1)[:, : part_cols * part_rows]
         .reshape(rows_dp, cols_fsdp, part_cols, part_rows)
         .transpose(1, 2, 0, 3)
         .reshape(cols_fsdp * part_cols, rows_dp * part_rows)
@@ -707,18 +781,25 @@
         compiler_params=pltpu.CompilerParams(
             collective_id=collective_id, has_side_effects=True, vmem_limit_bytes=VMEM_BYTES
         ),
+        cost_estimate=work_of(40),
         name="gather_all",
     )(*shards)
     return [out.reshape(-1, width) for out in outs]
 
 
-def reduce_all(grads, stats, shared, collective_id):
-    _, rows, width = grads.shape
+def reduce_all(grads, stats, shared, halved, collective_id):
+    width = grads[0].shape[2]
+    count = len(grads)
+    starts = [sum(grad.shape[1] for grad in grads[:at]) for at in range(count + 1)]
+    rows = starts[-1]
     cuts = lane_parts(width)
     parts = len(cuts)
     orders = [tuple(reversed(GATHER_ORDERS[number % 3])) for number in range(parts)]
 
-    def kernel(grads_ref, stats_ref, mine_ref, shared_ref, total_ref, *scratch):
+    def kernel(*refs):
+        grads_refs = refs[:count]
+        stats_ref, mine_ref, shared_ref, total_ref = refs[count : count + 4]
+        scratch = refs[count + 4 :]
         sums, first_get = scratch[:2]
         gets = scratch[2 : 2 + BITS]
         stats_all = scratch[2 + BITS]
@@ -726,27 +807,32 @@
         sems = scratch[8 + BITS :]
         core = lax.axis_index("dp")
         bits = my_bits()
-        local = [
-            pltpu.make_async_copy(
-                grads_ref.at[core, :, :, :, :, :, cut],
-                sums.at[:, :, :, :, :, cut],
-                local_sem.at[number],
+        places = [
+            (number, at, cut, slice(starts[at], starts[at + 1]))
+            for number, cut in enumerate(cuts)
+            for at in range(count)
+        ]
+        local = {
+            (number, at): pltpu.make_async_copy(
+                grads_refs[at].at[core, :, :, :, :, :, cut],
+                sums.at[:, :, :, :, span, cut],
+                local_sem.at[number, at],
             )
-            for number, cut in enumerate(cuts)
-        ]
-        for copy in local:
+            for number, at, cut, span in places
+        }
+        for copy in local.values():
             copy.start()
         greet_partners()
-        pairs = [
-            send(
-                grads_ref.at[1 - core, :, :, :, :, :, cut],
-                first_get.at[:, :, :, :, :, cut],
-                pair_send.at[number],
-                pair_get.at[number],
+        pairs = {
+            (number, at): send(
+                grads_refs[at].at[1 - core, :, :, :, :, :, cut],
+                first_get.at[:, :, :, :, span, cut],
+                pair_send.at[number, at],
+                pair_get.at[number, at],
                 sibling(),
             )
-            for number, cut in enumerate(cuts)
-        ]
+            for number, at, cut, span in places
+        }
 
         def index(number, stage, own):
             order = orders[number]
@@ -771,8 +857,9 @@
 
         going = []
         for number in range(parts):
-            local[number].wait()
-            pairs[number].wait()
+            for at in range(count):
+                local[number, at].wait()
+                pairs[number, at].wait()
             whole = (slice(None),) * (BITS + 1) + (cuts[number],)
             sums[whole] = sums[whole] + first_get[whole]
             going.append(go(number, 0))
@@ -788,7 +875,11 @@
                     at = index(number, stage, True)
                     mine_ref[:, cuts[number]] = sums[at].astype(F32) + gets[stage][number].astype(F32)
         mine = mine_ref[...]
-        squares = jnp.sum(jnp.sum(mine * mine, 0, keepdims=True), 1, keepdims=True)
+        row = row_number((rows, width))
+        counted = mine * mine
+        for low, high in halved:
+            counted = jnp.where((row >= low) & (row < high), 0.5 * counted, counted)
+        squares = jnp.sum(jnp.sum(counted, 0, keepdims=True), 1, keepdims=True)
         top_row = (row_number((8, 128)) == 0).astype(F32)
         stats_all[(core, *place)] = stats_ref[...] + top_row * squares
         shared_ref[(core, *place)] = mine_ref[rows - shared :, :].astype(BF16)
@@ -804,7 +895,8 @@
     grid = (2,) * BITS
     return pl.pallas_call(
         kernel,
-        in_specs=[pl.BlockSpec(memory_space=pl.ANY), pl.BlockSpec(memory_space=pltpu.VMEM)],
+        in_specs=[pl.BlockSpec(memory_space=pl.ANY)] * count
+        + [pl.BlockSpec(memory_space=pltpu.VMEM)],
         out_specs=[pl.BlockSpec(memory_space=pltpu.VMEM)] * 3,
         out_shape=[
             jax.ShapeDtypeStruct((rows, width), F32),
@@ -814,14 +906,15 @@
         scratch_shapes=[pltpu.VMEM(grid + (rows, width), BF16)] * 2
         + [pltpu.VMEM((parts,) + (2,) * (BITS - 1 - stage) + (rows, 128), BF16) for stage in range(BITS)]
         + [pltpu.VMEM((2,) + grid + (8, 128), F32)]
-        + [pltpu.SemaphoreType.DMA((parts,))] * 3
+        + [pltpu.SemaphoreType.DMA((parts, count))] * 3
         + [pltpu.SemaphoreType.DMA((parts, BITS))] * 2
         + spread_sems(parts + 1),
         compiler_params=pltpu.CompilerParams(
             collective_id=collective_id, has_side_effects=True, vmem_limit_bytes=VMEM_BYTES
         ),
+        cost_estimate=work_of(60),
         name="reduce_all",
-    )(grads.reshape((2,) + grid + (rows, width)), stats)
+    )(*[grad.reshape((2,) + grid + grad.shape[1:]) for grad in grads], stats)
 
 
 def chip(at):
@@ -1086,6 +1179,7 @@
         compiler_params=pltpu.CompilerParams(
             collective_id=collective_id, has_side_effects=True, vmem_limit_bytes=VMEM_BYTES
         ),
+        cost_estimate=work_of(40),
         name="exchange_back" if backward else "exchange",
     )(*operands)
 
@@ -1202,10 +1296,12 @@
         ]
     attention_all = [attention_one]
     router_all = [None]
+    fetched = [None]
     for layer in range(1, layers):
-        one, two = fetch_layer(attention_t[layer], router_t[layer - 1])
-        attention_all.append(one)
-        router_all.append(two)
+        share = attention_t[layer]
+        if layer > 1:
+            share, attention_all[0] = lax.optimization_barrier((share, attention_all[0]))
+        fetched.append(fetch_layer(share, router_t[layer - 1]))
 
     start, qkv, context, middle, hidden = first_forward(
         resolution, patches, dense, attention_all[0], positions, gains[0], width
@@ -1213,6 +1309,13 @@
     kept = [(start, qkv, context, middle)]
     mixing = None
     for layer in range(1, layers):
+        both = fetched[layer]
+        if mixing is not None:
+            both, last = lax.optimization_barrier((both, mixing[1]))
+            mixing = (mixing[0], last)
+        one, two = open_layer(both, attention_t.shape[1], router.shape[2], router.shape[1])
+        attention_all.append(one)
+        router_all.append(two)
         outs = sparse_forward(
             resolution, hidden, mixing, attention_all[layer], router_all[layer], gains[layer]
         )
@@ -1227,15 +1330,18 @@
         hidden = middle
         mixing = (combine, returned)
 
-    padding = -classes % 128
+    packs = devices if own else None
+    padding = -classes % 128 if not own else -classes % (16 * devices)
     head = jnp.pad(classifier[:width].astype(BF16), ((0, 0), (0, padding)))
     head_bias = jnp.pad(classifier[width:], ((0, 0), (0, padding)), constant_values=NEG_FILL)
     grad_hidden, grad_returned, grad_head, grad_bias, grad_last, loss_part = top(
-        resolution, labels, middle, combine, returned, head, head_bias, last_gains, classes, images
+        resolution, labels, middle, combine, returned, head, head_bias, last_gains, classes, images,
+        packs,
     )
     attention_grads = [None] * layers
     router_grads = [None] * (layers - 1)
     gain_grads = [None] * layers
+    layer_packs = [None] * layers
     in_factors = [None] * (layers - 1)
     out_factors = [None] * (layers - 1)
     local_squares = 0.0
@@ -1254,58 +1360,40 @@
         below = kept[layer - 1][4] if layer > 1 else None
         outs = sparse_backward(
             resolution, before, qkv, context, middle, grad_hidden, returned, grad_home, below,
-            attention_all[layer], router_all[layer], gains[layer],
+            attention_all[layer], router_all[layer], gains[layer], packs,
         )
         grad_hidden = outs[0]
         if below is not None:
             grad_returned = outs[1]
-        grad_attention, grad_router, grad_gain = outs[-3:]
-        attention_grads[layer] = grad_attention
-        router_grads[layer - 1] = grad_router
+        grad_gain = outs[-1]
+        if own:
+            layer_packs[layer] = outs[-2]
+        else:
+            attention_grads[layer], router_grads[layer - 1] = outs[-3:-1]
         gain_grads[layer] = grad_gain[:4]
     start, qkv, context, middle = kept[0]
-    grad_dense, grad_attention, grad_gain, grad_low, grad_high = first_backward(
+    outs = first_backward(
         resolution, patches, start, qkv, context, middle, grad_hidden, dense, attention_all[0],
-        gains[0],
-    )
+        gains[0], packs,
+    )
+    grad_gain, grad_low, grad_high = outs[-3:]
+    if own:
+        layer_packs[0] = outs[0]
+    else:
+        grad_dense, attention_grads[0] = outs[:2]
     gain_grads[0] = grad_gain[:4]
-    attention_grads[0] = grad_attention
     grad_pos = grad_low[:LEN_LO] + jnp.dot(interp.T, grad_high, precision=PRECISE)
     grad_table = jnp.concatenate([grad_pos] + gain_grads + [grad_last[:2]], 0)
     loss_local = loss_part[0, 0]
     part_rows, part_cols = router.shape[1:]
     table_rows = grad_table.shape[0]
     if own:
-        row_at = [0]
-        blocks = []
-
-        def block(values):
-            shaped = values.astype(BF16).reshape(devices, -1, width)
-            blocks.append(shaped)
-            row_at.append(row_at[-1] + shaped.shape[1])
-
-        block(grad_dense)
-        for grad in attention_grads:
-            block(grad)
-        for grad in router_grads:
-            block(
-                grad.reshape(lax.axis_size("fsdp"), part_cols, lax.axis_size("dp"), part_rows)
-                .transpose(2, 0, 1, 3)
-                .reshape(devices, -1)
-            )
-        alone = row_at[-1]
-        blocks.append(jnp.zeros((devices, -alone % 16, width), BF16))
-        head_rows = grad_head.shape[0]
-        head_pad = -head_rows % devices
-        blocks.append(jnp.pad(grad_head.astype(BF16), ((0, head_pad), (0, 0))).reshape(devices, -1, width))
         bias_flat = grad_bias[0]
         bias_flat = jnp.pad(bias_flat, (0, -bias_flat.shape[0] % width)).reshape(-1, width)
         tail = jnp.concatenate([grad_table, bias_flat], 0).astype(BF16)
-        tail = jnp.pad(tail, ((0, -tail.shape[0] % devices), (0, 0)))
-        blocks.append(tail.reshape(devices, -1, width))
-        shared_rows = blocks[-2].shape[1] + blocks[-1].shape[1]
-        last_pad = -shared_rows % 16
-        blocks.append(jnp.zeros((devices, last_pad, width), BF16))
+        tail = jnp.pad(tail, ((0, -tail.shape[0] % devices), (0, 0))).reshape(devices, -1, width)
+        tail_each = tail.shape[1]
+        tail = jnp.pad(tail, ((0, 0), (0, -tail_each % 16), (0, 0)))
         stats = jnp.concatenate(
             [
                 jnp.broadcast_to(local_squares, (1, 128)),
@@ -1314,23 +1402,33 @@
             ],
             0,
         )
+        blocks = layer_packs + [grad_head, tail]
+        starts = [sum(block.shape[1] for block in blocks[:at]) for at in range(layers)]
+        columns = dense.shape[0] // devices
+        part = attention_t.shape[1]
+        router_at = [starts[layer] + part for layer in range(1, layers)]
         mine, shared, totals = reduce_all(
-            jnp.concatenate(blocks, 1), stats, shared_rows + last_pad, 2 * layers
-        )
-        shared = shared.reshape(devices, -1, width).astype(F32)
-        head_each = blocks[-3].shape[1]
-        head_all = shared[:, :head_each].reshape(-1, width)[:classes].T
-        tail_all = shared[:, head_each:shared_rows].reshape(-1, width)
+            blocks, stats, grad_head.shape[1] + tail.shape[1],
+            [(at, at + part_cols) for at in router_at], 2 * layers,
+        )
+        shared = shared.reshape(devices, -1, width)
+        head_each = grad_head.shape[1]
+        head_all = shared[:, :head_each].reshape(-1, width)[:classes].T.astype(F32)
+        tail_all = shared[:, head_each : head_each + tail_each].reshape(-1, width).astype(F32)
         shared_table = tail_all[:table_rows]
         bias_all = tail_all[table_rows:].reshape(-1)[None, :classes]
         shared_head = jnp.concatenate([head_all, bias_all], 0)
         norm = jnp.sqrt(totals[0, 0])
         loss_total = totals[1, 0]
-        pieces = [mine[row_at[i] : row_at[i + 1]] for i in range(len(row_at) - 1)]
-        grad_first = pieces[0].T
-        grad_attention = jnp.stack(pieces[1 : 1 + layers]).transpose(0, 2, 1)
+        grad_first = mine[:columns].T
+        attention_at = [columns] + starts[1:]
+        grad_attention = jnp.stack([mine[at : at + part].T for at in attention_at])
+        lane_at = lax.axis_index("dp") * part_rows
         grad_router_all = jnp.stack(
-            [piece.reshape(part_cols, part_rows).T for piece in pieces[1 + layers :]]
+            [
+                lax.dynamic_slice_in_dim(mine[at : at + part_cols], lane_at, part_rows, 1).T
+                for at in router_at
+            ]
         )
     else:
         grad_first = lax.psum_scatter(

time: 783 us -> 651 us (0.83); the launches traced: 799 us -> 646 us
  local copies, waits for them, and re-layouts: 85.9 us -> 29.5 us
  Pallas kernels: 619 us -> 574 us
  waiting for transfers between devices: 40.8 us -> 0.06 us
  other arithmetic: 30.8 us -> 21 us
    concatenate x2 -> x0, local copies, waits for them, and re-layouts: 41.2 us -> none  [on_device(): jnp.concatenate(blocks, 1)]
    all_gather x2, waiting for transfers between devices: 40.7 us -> 0.02 us  [fetch_layer(): return lax.all_gather(pack, ('dp', 'fsdp'), axis=0)]
    pallas_call x1, Pallas kernels: 135 us -> 94.5 us  [reduce_all(): pl.pallas_call(kernel, in_specs=[pl.BlockSpec(memory_space=pl.ANY)] * cou...]
    pallas_call x4, Pallas kernels: 185 us -> 159 us  [exchange(): pl.pallas_call(kernel, in_specs=in_specs, out_specs=[inside] * len(out_sh...]
    pallas_call x7, Pallas kernels: 170 us -> 194 us  [by_image(): pl.pallas_call(kernel, grid_spec=pltpu.PrefetchScalarGridSpec(num_scalar_...]
    convert_element_type x8 -> x2, other arithmetic: 12.6 us -> 1.12 us  [the longest x1 0.95 us: on_device(): shared[:, head_each:head_each + tail_each].reshape(-1, width).astype(F32)]
    convert_element_type x6 -> x0, local copies, waits for them, and re-layouts: 9.89 us -> none  [block(): shaped = values.astype(BF16).reshape(devices, -1, width)]
  transfers between devices with their start and end apart: 2 -> 2, of which waited for: 1 -> 0; matrix products, arithmetic and copies ran while one was open for 2% -> 2% of each run, Pallas kernels for 8% -> 18%
where the time goes in v3:
time: 651 us; the launch traced here: 646 us
  Pallas kernels  574 us (88%)
  local copies, waits for them, and re-layouts  29.5 us (5%)
  other arithmetic  21 us (3%)
  between operations  18.1 us (3%)
    pallas_call x7, Pallas kernels, by_image(): pl.pallas_call(kernel, grid_spec=pltpu.PrefetchScalarGridSpec(num_scalar_...  194 us
    pallas_call x4, Pallas kernels, exchange(): pl.pallas_call(kernel, in_specs=in_specs, out_specs=[inside] * len(out_sh...  159 us
    pallas_call x1, Pallas kernels, reduce_all(): pl.pallas_call(kernel, in_specs=[pl.BlockSpec(memory_space=pl.ANY)] * cou...  94.5 us
    pallas_call x2, Pallas kernels, expert_adam(): pl.pallas_call(kernel, grid=(layers, local), in_specs=[pl.BlockSpec(memor...  91.6 us
    pallas_call x1, Pallas kernels, gather_all(): pl.pallas_call(kernel, in_specs=[pl.BlockSpec(memory_space=pltpu.VMEM)] *...  34.5 us
  transfers between devices with their start and end apart: 2, of which 0 were waited for; matrix products, arithmetic and copies ran while one was open for 2% of the time, Pallas kernels for 18%

profile of v3, /device:TPU:0, one launch (start us, length us, event | category | flops | bytes accessed | tf_op | source)
XLA Modules:
  0.0 645.9 jit_solution(9308095962151746567)
XLA Ops:
  11.9 34.5 %gather_all.1 = (bf16[2,2,2,2,2,120,384]{6,5,4,3,2,1,0:T(8,128)(2,1)}, bf16[2,2,2,2,2,48,384]{6,5,4,3,2,1,0:T(8,128)(2,1)}) custom-call(bf16[120,384]{1,0:T(8,128)(2,1)} %convert_bitcast_fusion.2.refs_0_, bf16[48,384]{1,0:T(8,128)(2,1)} %get-tuple-element.241.refs_1_), custom_call_target="tpu_custom_call" | custom-call | flops 40000000000 | bytes 1048576 | tf_op jit(solution)/shard_map/gather_all/pallas_call | solution.py:775
  56.0 24.7 %first_forward.1 = (f32[4,576,384]{2,1,0:T(8,128)}, bf16[4,576,1152]{2,1,0:T(8,128)(2,1)}, bf16[4,576,384]{2,1,0:T(8,128)(2,1)}, f32[4,576,384]{2,1,0:T(8,128)}, f32[4,576,384]{2,1,0:T(8,128)}) custom-call(s32[4]{0:T(128)} %refs_0_.13, bf16[4,576,768]{2,1,0:T(8,128)(2,1)} %refs_1_.9, bf16[3840,384]{1,0:T(8,128)(2,1)} %bitcast.93, ...), custom_call_target="tpu_custom_call" | custom-call | flops 32000000000 | bytes 1048576 | tf_op jit(solution)/shard_map/first_forward/pallas_call | solution.py:310
  82.7 2.4 slice.160
  85.1 16.4 %sparse_forward.2 = (bf16[4,576,1152]{2,1,0:T(8,128)(2,1)}, bf16[4,576,384]{2,1,0:T(8,128)(2,1)}, f32[4,576,384]{2,1,0:T(8,128)}, bf16[4,576,128]{2,1,0:T(8,128)(2,1)}, bf16[4,128,384]{2,1,0:T(8,128)(2,1)}) custom-call(s32[4]{0:T(128)} %refs_0_.13, f32[4,576,384]{2,1,0:T(8,128)} %get-tuple-element.92.refs_1_, bf16[1536,384]{1,0:T(8,128)(2,1)} %bitcast.82, ...), custom_call_target="tpu_custom_call" | custom-call | flops 32000000000 | bytes 1048576 | tf_op jit(solution)/shard_map/sparse_forward/pallas_call | solution.py:310
  101.5 42.5 %exchange.2 = (bf16[4,128,384]{2,1,0:T(8,128)(2,1)}, bf16[8,128,384]{2,1,0:T(8,128)(2,1)}) custom-call(bf16[4,128,384]{2,1,0:T(8,128)(2,1)} %get-tuple-element.98.refs_0_, f32[2,8,384,768]{3,2,1,0:T(8,128)} %w_ref.2, f32[2,8,768,384]{3,2,1,0:T(8,128)} %w_ref.3), custom_call_target="tpu_custom_call" | custom-call | flops 40000000000 | bytes 1048576 | tf_op jit(solution)/shard_map/exchange/pallas_call | solution.py:1157
  144.0 2.4 slice.129
  148.4 17.1 %sparse_forward.3 = (f32[4,576,384]{2,1,0:T(8,128)}, bf16[4,576,1152]{2,1,0:T(8,128)(2,1)}, bf16[4,576,384]{2,1,0:T(8,128)(2,1)}, f32[4,576,384]{2,1,0:T(8,128)}...) custom-call(s32[4]{0:T(128)} %refs_0_.13, f32[4,576,384]{2,1,0:T(8,128)} %get-tuple-element.95.refs_1_.refs_4_, ...), custom_call_target="tpu_custom_call" | custom-call | flops 32000000000 | bytes 1048576 | tf_op jit(solution)/shard_map/sparse_forward/pallas_call | solution.py:310
  165.6 36.7 %exchange.3 = (bf16[4,128,384]{2,1,0:T(8,128)(2,1)}, bf16[8,128,384]{2,1,0:T(8,128)(2,1)}) custom-call(bf16[4,128,384]{2,1,0:T(8,128)(2,1)} %get-tuple-element.107.refs_0_, f32[2,8,384,768]{3,2,1,0:T(8,128)} %w_ref.2, f32[2,8,768,384]{3,2,1,0:T(8,128)} %w_ref.3), custom_call_target="tpu_custom_call" | custom-call | flops 40000000000 | bytes 1048576 | tf_op jit(solution)/shard_map/exchange/pallas_call | solution.py:1157
  202.3 11.1 %top.1 = (f32[4,576,384]{2,1,0:T(8,128)}, bf16[4,128,384]{2,1,0:T(8,128)(2,1)}, bf16[32,32,384]{2,1,0:T(8,128)(2,1)}, f32[8,1024]{1,0:T(8,128)}, f32[8,384]{1,0:T(8,128)}, /*index=5*/f32[8,128]{1,0:T(8,128)}) custom-call(s32[4]{0:T(128)} %refs_0_.13, s32[4]{0:T(128)} %refs_1_.8, f32[4,576,384]{2,1,0:T(8,128)} %get-tuple-element.105.refs_2_.refs_4_, ...), custom_call_target="tpu_custom_call" | custom-call | flops 32000000000 | bytes 1048576 | tf_op jit(solution)/shard_map/top/pallas_call | solution.py:310
  213.4 37.2 %exchange_back.2 = (bf16[4,128,384]{2,1,0:T(8,128)(2,1)}, bf16[8,128,768]{2,1,0:T(8,128)(2,1)}, bf16[8,128,768]{2,1,0:T(8,128)(2,1)}, bf16[8,128,384]{2,1,0:T(8,128)(2,1)}, f32[8,128]{1,0:T(8,128)}) custom-call(bf16[4,128,384]{2,1,0:T(8,128)(2,1)} %get-tuple-element.110.refs_0_, bf16[8,128,384]{2,1,0:T(8,128)(2,1)} %get-tuple-element.111.refs_1_, ...), custom_call_target="tpu_custom_call" | custom-call | flops 40000000000 | bytes 1048576 | tf_op jit(solution)/shard_map/exchange_back/pallas_call | solution.py:1157
  250.6 30.8 %sparse_backward.2 = (f32[4,576,384]{2,1,0:T(8,128)}, bf16[4,128,384]{2,1,0:T(8,128)(2,1)}, bf16[32,64,384]{2,1,0:T(8,128)(2,1)}, f32[8,384]{1,0:T(8,128)}) custom-call(s32[4]{0:T(128)} %refs_0_.13, f32[4,576,384]{2,1,0:T(8,128)} %get-tuple-element.102.refs_1_, bf16[4,576,1152]{2,1,0:T(8,128)(2,1)} %get-tuple-element.103.refs_2_, ...), custom_call_target="tpu_custom_call" | custom-call | flops 32000000000 | bytes 1048576 | tf_op jit(solution)/shard_map/sparse_backward/pallas_call | solution.py:310
  281.4 42.3 %exchange_back.3 = (bf16[4,128,384]{2,1,0:T(8,128)(2,1)}, bf16[8,128,768]{2,1,0:T(8,128)(2,1)}, bf16[8,128,768]{2,1,0:T(8,128)(2,1)}, bf16[8,128,384]{2,1,0:T(8,128)(2,1)}, f32[8,128]{1,0:T(8,128)}) custom-call(bf16[4,128,384]{2,1,0:T(8,128)(2,1)} %get-tuple-element.114.refs_0_, bf16[8,128,384]{2,1,0:T(8,128)(2,1)} %get-tuple-element.115.refs_1_.refs_0_, ...), custom_call_target="tpu_custom_call" | custom-call | flops 40000000000 | bytes 1048576 | tf_op jit(solution)/shard_map/exchange_back/pallas_call | solution.py:1157
  323.7 29.2 %sparse_backward.3 = (f32[4,576,384]{2,1,0:T(8,128)}, bf16[32,64,384]{2,1,0:T(8,128)(2,1)}, f32[8,384]{1,0:T(8,128)}) custom-call(s32[4]{0:T(128)} %refs_0_.13, f32[4,576,384]{2,1,0:T(8,128)} %get-tuple-element.92.refs_1_, bf16[4,576,1152]{2,1,0:T(8,128)(2,1)} %get-tuple-element.93.refs_2_, bf16[4,576,384]{2,1,0:T(8,128)(2,1)} %get-tuple-element.94.refs_3_, ...), custom_call_target="tpu_custom_call" | custom-call | flops 32000000000 | bytes 1048576 | tf_op jit(solution)/shard_map/sparse_backward/pallas_call | solution.py:310
  352.9 65.0 %first_backward.1 = (bf16[32,176,384]{2,1,0:T(8,128)(2,1)}, f32[8,384]{1,0:T(8,128)}, f32[208,384]{1,0:T(8,128)}, f32[576,384]{1,0:T(8,128)}) custom-call(s32[4]{0:T(128)} %refs_0_.13, bf16[4,576,768]{2,1,0:T(8,128)(2,1)} %refs_1_.9, f32[4,576,384]{2,1,0:T(8,128)} %get-tuple-element.88.refs_2_, bf16[4,576,1152]{2,1,0:T(8,128)(2,1)} %get-tuple-element.89.refs_3_, ...), custom_call_target="tpu_custom_call" | custom-call | flops 32000000000 | bytes 1048576 | tf_op jit(solution)/shard_map/first_backward/pallas_call | solution.py:310
  421.5 2.4 fusion.1
  430.3 94.5 %reduce_all.1 = (f32[352,384]{1,0:T(8,128)}, bf16[2,2,2,2,2,48,384]{6,5,4,3,2,1,0:T(8,128)(2,1)}, f32[8,128]{1,0:T(8,128)}) custom-call(bf16[2,2,2,2,2,176,384]{6,5,4,3,2,1,0:T(8,128)(2,1)} %bitcast.92, bf16[2,2,2,2,2,64,384]{6,5,4,3,2,1,0:T(8,128)(2,1)} %bitcast.96, bf16[2,2,2,2,2,64,384]{6,5,4,3,2,1,0:T(8,128)(2,1)} %bitcast.95, ...), custom_call_target="tpu_custom_call" | custom-call | flops 60000002048 | bytes 1048576 | tf_op jit(solution)/shard_map/reduce_all/pallas_call | solution.py:896
  524.8 1.6 slice_bitcast_fusion.2
  532.2 1.9 slice_multiply_fusion
  534.1 1.8 mul.289
  535.8 2.2 multiply_subtract_fusion.3
  538.1 2.3 multiply_subtract_fusion.1
  541.9 3.1 multiply_subtract_fusion
  546.0 45.7 %expert_adam.2 = (f32[2,8,384,768]{3,2,1,0:T(8,128)}, f32[2,8,384,768]{3,2,1,0:T(8,128)}, f32[2,8,384,768]{3,2,1,0:T(8,128)}) custom-call(f32[1]{0:T(128)} %bitcast.35.scale_ref, f32[2,8,384,768]{3,2,1,0:T(8,128)} %w_ref.2, f32[2,8,384,768]{3,2,1,0:T(8,128)} %m_ref.2, f32[2,8,384,768]{3,2,1,0:T(8,128)} %s_ref.2, ...), custom_call_target="tpu_custom_call" | custom-call | tf_op jit(solution)/shard_map/expert_adam/pallas_call | solution.py:1218
  591.7 45.9 %expert_adam.3 = (f32[2,8,768,384]{3,2,1,0:T(8,128)}, f32[2,8,768,384]{3,2,1,0:T(8,128)}, f32[2,8,768,384]{3,2,1,0:T(8,128)}) custom-call(f32[1]{0:T(128)} %bitcast.35.scale_ref, f32[2,8,768,384]{3,2,1,0:T(8,128)} %w_ref.3, f32[2,8,768,384]{3,2,1,0:T(8,128)} %m_ref.3, f32[2,8,768,384]{3,2,1,0:T(8,128)} %s_ref.3, ...), custom_call_target="tpu_custom_call" | custom-call | tf_op jit(solution)/shard_map/expert_adam/pallas_call | solution.py:1218
  (113 shorter events, 34.2 us)
Async XLA Ops:
  7.2 73.5 %all-gather.7.cloned.1.call-start = ((), (), s32[]{:S(2)}) async-start(), calls=%async_computation | async-start | bytes 1419264 | tf_op jit(solution)/shard_map/all_gather | solution.py:630
  10.3 133.7 %all-gather.9.cloned.1.call-start = ((), (), s32[]{:S(2)}) async-start(), calls=%async_computation.1 | async-start | bytes 1419264 | tf_op jit(solution)/shard_map/all_gather | solution.py:630
  11.9 35.3 %copy-start.5 = (f32[210,384]{1,0:T(8,128)S(1)}, f32[210,384]{1,0:T(8,128)}, u32[]{:S(2)}) copy-start(f32[210,384]{1,0:T(8,128)} %param.33) | copy-start | bytes 967684
  11.9 35.3 %copy-start.2 = (f32[385,1000]{1,0:T(8,128)S(1)}, f32[385,1000]{1,0:T(8,128)}, u32[]{:S(2)}) copy-start(f32[385,1000]{1,0:T(8,128)} %param.32) | copy-start | bytes 4620004
  49.2 5.2 copy-start
  49.3 1.3 slice-start.1
  49.3 3.2 slice-start.2
  53.1 1.4 copy-start.4
  53.1 2.4 slice-start
  352.8 68.7 %copy-start.1 = (f32[576,196]{0,1:T(8,128)S(1)}, f32[576,196]{0,1:T(8,128)}, u32[]{:S(2)}) copy-start(f32[576,196]{0,1:T(8,128)} %copy-done) | copy-start | bytes 1354756
  421.5 4.9 copy-start.17
  421.5 5.5 copy-start.18
  528.2 3.3 copy-start.9
  532.1 6.0 copy-start.6
  532.2 9.6 %copy-start.8 = (f32[385,1000]{1,0:T(8,128)S(1)}, f32[385,1000]{1,0:T(8,128)}, u32[]{:S(2)}) copy-start(f32[385,1000]{1,0:T(8,128)} %param.45) | copy-start | bytes 4620004
  534.1 6.3 copy-start.16
  535.8 5.9 copy-start.3
  535.8 5.9 copy-start.7
  541.8 3.2 copy-start.10
  541.8 3.2 copy-start.11
  541.8 3.2 copy-start.12
  541.8 3.2 copy-start.13
  541.8 3.2 copy-start.14
  541.9 3.2 copy-start.15
Sparse Core Ops, SparseCore 0:
  11.4 59.3 all-gather.6
  74.2 56.5 all-gather.8
